TPU v7x, 512 devices: a whole 4x4x16 slice. The times are simulated.
512 devices in a mesh: dp: 64 (over z, x), tensor: 8 (over y, core).
Axes of the slice: x: 4, y: 4, z: 16, core: 2. Of those that a mesh axis runs over, the one named last changes fastest.
Arguments:
- inputs_x: bfloat16 [16384, 8192], P('dp', 'tensor'), may hold values from -7 to 7
- gate_z: bfloat16 [16384, 8192], P('dp', 'tensor'), may hold values from -6 to 6
- input_b: bfloat16 [16384, 1024], P('dp', 'tensor'), may hold values from -1 to 1
- input_c: bfloat16 [16384, 1024], P('dp', 'tensor'), may hold values from -1 to 1
- dt_raw: float32 [16384, 128], P('dp', 'tensor'), may hold values from -3 to 3
- a_log: float32 [128], P('tensor'), may hold values from -8.5 to -2
- dt_bias: float32 [128], P('tensor'), may hold values from -3 to -1
- skip_d: float32 [128], P('tensor'), may hold values from 0.5 to 1.5
- norm_gain: float32 [8192], P('tensor'), may hold values from 0.1 to 1.9
- lengths: int32 [16], replicated, may hold values from 1 to 8192, 16256 in all
- cotangent: bfloat16 [16384, 8192], P('dp', 'tensor'), may hold values from -6 to 6
Outputs:
- grad_x: bfloat16 [16384, 8192], P('dp', 'tensor')
- grad_b: bfloat16 [16384, 1024], P('dp', 'tensor')
- grad_c: bfloat16 [16384, 1024], P('dp', 'tensor')
- grad_dt: float32 [16384, 128], P('dp', 'tensor')
- grad_gain: float32 [8192], P(('tensor', 'dp'))
Inputs may be any that keep to these rules, and one draw needn't show every extreme that they name: `lengths`: each document holds 1 to 8192 tokens and one holds exactly 8192; together they fill exactly the first 16256 positions, and the last 128 positions are padding.
All inputs are finite; a program needn't handle non-finite values.
Results may differ from a plain program's by a relative error of at most 0.0011.
Values sent between devices are 32-bit elements; how exact they have to be, the bound alone decides.
No kernel may reach another device: no remote copies, remote signals or barrier semaphores. Data moves between devices by JAX's collectives and lax.ppermute only.
A program may use at most 128 MiB of HBM per device.

v0:
```python
import jax
import jax.numpy as jnp
from jax import lax
from jax.sharding import PartitionSpec as P

HEADS = 128
HEAD_DIM = 64
STATE = 128
STRETCH = 128


EPSILON = 1e-05
PRECISE = lax.Precision.HIGHEST


def carried_in(part, axis, combine, identity, reverse):
    count = lax.axis_size(axis)
    place = lax.axis_index(axis)
    ahead = count - 1 - place if reverse else place
    gathered = jax.tree.map(lambda a: lax.all_gather(a, axis), part)
    state = jax.tree.map(lambda a, e: jnp.zeros_like(a) + jnp.asarray(e, a.dtype), part, identity)

    def one(hop, state):
        source = count - 1 - hop if reverse else hop
        return combine(
            state, jax.tree.map(lambda a: lax.dynamic_index_in_dim(a, source, 0, False), gathered)
        )

    return lax.fori_loop(0, ahead, one, state)


def decay_terms(raw_steps, log_rates, step_bias):
    deltas = jax.nn.softplus(raw_steps + step_bias[None, :])
    return (deltas, -jnp.exp(log_rates)[None, :] * deltas)


def token_flags(lengths, first_place, count, live_end):
    doc_ends = jnp.cumsum(lengths)
    doc_starts = doc_ends - lengths
    places = first_place + jnp.arange(count, dtype=jnp.int32)
    opened = jnp.any(places[:, None] == doc_starts[None, :], axis=1)
    living = places < live_end
    keeping = jnp.where(living & jnp.logical_not(opened), 1.0, 0.0).astype(jnp.float32)
    return (keeping, jnp.where(living, 1.0, 0.0).astype(jnp.float32))


def block_state(signal, input_map, deltas, log_decay, keeping):
    length, head_count, head_width = signal.shape
    group_count = input_map.shape[1]
    resets = jnp.cumsum(1.0 - keeping)
    summed = jnp.cumsum(log_decay, axis=0)
    ending = summed[-1]
    weights = (
        jnp.where((resets == resets[-1])[:, None], jnp.exp(ending[None, :] - summed), 0.0) * deltas
    )
    through = jnp.where(resets[-1] == 0.0, jnp.exp(ending), 0.0)
    scaled = (signal * weights[:, :, None]).reshape(length, group_count, -1, head_width)
    states = jnp.einsum("lgkp,lgn->gkpn", scaled, input_map, precision=PRECISE)
    return (through, states.reshape(head_count, head_width, input_map.shape[2]))


def block_output(signal, input_map, output_map, deltas, log_decay, keeping, entering):
    length, head_count, head_width = signal.shape
    group_count, state_width = (input_map.shape[1], input_map.shape[2])
    resets = jnp.cumsum(1.0 - keeping)
    summed = jnp.cumsum(log_decay, axis=0).T
    places = jnp.arange(length)
    allowed = (places[:, None] >= places[None, :]) & (resets[:, None] == resets[None, :])
    spread = jnp.where(allowed[None], summed[:, :, None] - summed[:, None, :], 0.0)
    decays = jnp.where(allowed[None], jnp.exp(spread), 0.0)
    intersection = jnp.einsum("tgn,sgn->gts", output_map, input_map, precision=PRECISE)
    mixing = (
        decays.reshape(group_count, -1, length, length)
        * intersection[:, None]
        * deltas.T.reshape(group_count, -1, 1, length)
    )
    within = jnp.einsum(
        "gkts,sgkp->tgkp",
        mixing,
        signal.reshape(length, group_count, -1, head_width),
        precision=PRECISE,
    )
    carried = jnp.einsum(
        "tgn,gkpn->tgkp",
        output_map,
        entering.reshape(group_count, -1, head_width, state_width),
        precision=PRECISE,
    )
    fresh = jnp.where(resets[:, None] == 0.0, jnp.exp(summed.T), 0.0)
    joined = within + carried * fresh.reshape(length, group_count, -1)[..., None]
    return joined.reshape(length, head_count, head_width)


def chain_states(throughs, states, entering):

    def advance(holding, member):
        return (member[0][:, None, None] * holding + member[1], holding)

    leaving, starting = lax.scan(advance, entering, (throughs, states))
    return (starting, leaving)


def join_pairs(earlier, later):
    return (later[0] * earlier[0], later[0][:, None, None] * earlier[1] + later[1])


def per_device(
    inputs_x,
    gate_z,
    input_b,
    input_c,
    dt_raw,
    a_log,
    dt_bias,
    skip_d,
    norm_gain,
    lengths,
    cotangent,
):
    tok_rows = inputs_x.shape[0]
    head_count = dt_raw.shape[1]
    head_width = inputs_x.shape[1] // head_count
    group_count = input_b.shape[1] // STATE
    block_count = tok_rows // STRETCH
    dp_count = lax.axis_size("dp")
    first_place = lax.axis_index("dp") * tok_rows
    keeping, living = token_flags(lengths, first_place, tok_rows, dp_count * tok_rows - STRETCH)
    keep_blocks = keeping.reshape(block_count, STRETCH)
    x_float = inputs_x.astype(jnp.float32).reshape(tok_rows, head_count, head_width)
    b_float = input_b.astype(jnp.float32).reshape(tok_rows, group_count, STATE)
    c_float = input_c.astype(jnp.float32).reshape(tok_rows, group_count, STATE)

    def split_blocks(value):
        return value.reshape((block_count, STRETCH) + value.shape[1:])

    def device_states(signal, in_map, raw_steps):
        deltas, log_decay = decay_terms(raw_steps, a_log, dt_bias)
        return jax.vmap(block_state)(
            split_blocks(signal),
            split_blocks(in_map),
            split_blocks(deltas),
            split_blocks(log_decay),
            keep_blocks,
        )

    def device_output(signal, in_map, out_map, raw_steps, entries):
        deltas, log_decay = decay_terms(raw_steps, a_log, dt_bias)
        produced = jax.vmap(block_output)(
            split_blocks(signal),
            split_blocks(in_map),
            split_blocks(out_map),
            split_blocks(deltas),
            split_blocks(log_decay),
            keep_blocks,
            entries,
        )
        produced = (
            produced.reshape(tok_rows, head_count, head_width) + skip_d[None, :, None] * signal
        )
        return produced.reshape(tok_rows, head_count * head_width)

    (throughs, states), back_states = jax.vjp(device_states, x_float, b_float, dt_raw)
    empty_state = jnp.zeros((head_count, head_width, STATE), jnp.float32)
    _, leaving = chain_states(throughs, states, empty_state)
    through_all = jnp.prod(throughs, axis=0)
    identity = (jnp.ones((head_count,), jnp.float32), empty_state)
    _, entering = carried_in((through_all, leaving), "dp", join_pairs, identity, False)
    (starting, outgoing), back_chain = jax.vjp(chain_states, throughs, states, entering)
    core_value, back_core = jax.vjp(device_output, x_float, b_float, c_float, dt_raw, starting)
    gate_value = jax.nn.silu(gate_z.astype(jnp.float32))
    live_mask = living[:, None]
    shaped = core_value * gate_value * live_mask
    pulling = cotangent.astype(jnp.float32)
    gain_row = norm_gain[None, :]
    squares, products = lax.psum(
        (jnp.sum(shaped * shaped, axis=1), jnp.sum(gain_row * pulling * shaped, axis=1)), "tensor"
    )
    channels = HEADS * HEAD_DIM
    scaling = lax.rsqrt(squares / channels + EPSILON)
    grad_gain = lax.psum_scatter(
        jnp.sum(pulling * shaped * scaling[:, None], axis=0), "dp", scatter_dimension=0, tiled=True
    )
    back_shaped = (
        scaling[:, None] * gain_row * pulling
        - (scaling * scaling * scaling * products / channels)[:, None] * shaped
    )
    core_pull = back_shaped * gate_value * live_mask
    grad_xa, grad_ba, grad_ca, grad_ta, grad_starts = back_core(core_pull)
    _, _, local_pull = back_chain((grad_starts, jnp.zeros_like(outgoing)))
    _, later_pull = carried_in((through_all, local_pull), "dp", join_pairs, identity, True)
    grad_through, grad_state, _ = back_chain((grad_starts, later_pull))
    grad_xb, grad_bb, grad_tb = back_states((grad_through, grad_state))
    grad_x = (grad_xa + grad_xb).reshape(tok_rows, head_count * head_width).astype(jnp.bfloat16)
    grad_b = (grad_ba + grad_bb).reshape(tok_rows, group_count * STATE).astype(jnp.bfloat16)
    grad_c = grad_ca.reshape(tok_rows, group_count * STATE).astype(jnp.bfloat16)
    grad_dt = grad_ta + grad_tb
    return (grad_x, grad_b, grad_c, grad_dt, grad_gain)


def solution(mesh):
    return jax.shard_map(
        per_device,
        mesh=mesh,
        in_specs=(
            P("dp", "tensor"),
            P("dp", "tensor"),
            P("dp", "tensor"),
            P("dp", "tensor"),
            P("dp", "tensor"),
            P("tensor"),
            P("tensor"),
            P("tensor"),
            P("tensor"),
            P(),
            P("dp", "tensor"),
        ),
        out_specs=(
            P("dp", "tensor"),
            P("dp", "tensor"),
            P("dp", "tensor"),
            P("dp", "tensor"),
            P(("tensor", "dp")),
        ),
        check_vma=False,
    )
```

profile of v0, /device:TPU:1, one launch (start us, length us, event | category | flops | bytes accessed | tf_op | source)
XLA Modules:
  0.0 879.1 jit_solution(3857844933250377765)
XLA Ops:
  12.1 1.2 copy.213
  15.4 1.7 while.88
  21.2 123.4 %all-reduce.1 = f32[1024]{0:T(1024)S(1)} all-reduce(f32[1024]{0:T(1024)S(1)} %dynamic-update-slice), channel_id=2, replica_groups=mesh['dp'=64,'tensor'=8] {'dp'}, use_global_device_ids=true, to_apply=%add.1 | all-reduce | flops 1024 | bytes 8192
  145.7 2.1 copy.223
  148.1 169.9 %all-gather.6.cloned.1.call-done = f32[1024,64,128]{2,1,0:T(8,128)} async-done(((f32[16,64,128]{2,1,0:T(8,128)}), f32[1024,64,128]{2,1,0:T(8,128)}) %all-gather.6.cloned.1.call-update) | async-done | bytes 33554448 | tf_op jit(solution)/shard_map/all_gather | solution.py:20
  318.7 4.3 while.85
  319.4 1.2 constant_dynamic-update-slice_fusion.2
  321.5 1.3 constant_dynamic-update-slice_fusion.2
  324.6 2.7 fusion.16
  329.0 12.8 %psum.14 = f32[256]{0:T(256)S(1)} all-reduce(f32[256]{0:T(256)S(1)} %get-tuple-element.556), channel_id=1, replica_groups=mesh['dp'=64,'tensor'=8] {'tensor'}, use_global_device_ids=true, to_apply=%region_12.14 | all-reduce | flops 256 | bytes 2048 | tf_op jit(solution)/shard_map/psum | solution.py:175
  342.4 14.5 %psum.15 = f32[256]{0:T(256)S(1)} all-reduce(f32[256]{0:T(256)S(1)} %get-tuple-element.491), channel_id=1, replica_groups=mesh['dp'=64,'tensor'=8] {'tensor'}, use_global_device_ids=true, to_apply=%region_14.16 | all-reduce | flops 256 | bytes 2048 | tf_op jit(solution)/shard_map/psum | solution.py:175
  356.9 2.5 fusion.27
  359.4 2.7 reshape.342
  362.1 1.8 fusion.38
  365.7 3.7 fusion.13
  369.4 1.8 copy.225
  371.2 190.3 %all-reduce.2 = f32[1024]{0:T(1024)S(1)} all-reduce(f32[1024]{0:T(1024)S(1)} %get-tuple-element.490), channel_id=5, replica_groups=mesh['dp'=64,'tensor'=8] {'dp'}, use_global_device_ids=true, to_apply=%region_32.34.clone | all-reduce | flops 1024 | bytes 8192
  562.1 2.5 multiply_reduce_fusion.2
  564.6 3.1 convolution_bitcast_fusion.1
  567.7 4.1 fusion.21
  572.9 151.9 %all-gather.8.cloned.1.call-done = f32[1024,64,128]{2,1,0:T(8,128)} async-done(((f32[16,64,128]{2,1,0:T(8,128)}), f32[1024,64,128]{2,1,0:T(8,128)}) %all-gather.8.cloned.1.call-update) | async-done | bytes 33554448 | tf_op jit(solution)/shard_map/all_gather | solution.py:20
  724.9 120.2 %while.86 = (s32[]{:T(128)}, f32[16,64,128]{2,1,0:T(8,128)S(1)}, s32[]{:T(128)}, f32[64,16]{1,0:T(8,128)}, f32[64,16,64,128]{3,2,1,0:T(8,128)}, /*index=5*/s32[]{:T(128)}, s32[]{:T(128)}, s32[]{:T(128)}, s32[]{:T(128)}) while((s32[]{:T(128)}, f32[16,64,128]{2,1,0:T(8,128)S(1)}, s32[]{:T(128)}, f32[64,16]{1,0:T(8,128)}, ...), condition=%wide.region_18.20_spmd, body=%wide.region_17.19_spmd.sunk | while | flops 262150 | bytes 1573211 | solution.py:29
  727.5 1.2 bitcast_add_fusion.19
  731.3 1.2 bitcast_add_fusion.19
  735.1 1.2 bitcast_add_fusion.19
  738.9 1.2 bitcast_add_fusion.19
  740.8 1.2 bitcast_add_fusion.19
  742.7 1.2 bitcast_add_fusion.19
  744.7 1.2 bitcast_add_fusion.19
  746.6 1.2 bitcast_add_fusion.19
  748.5 1.2 bitcast_add_fusion.19
  750.4 1.2 bitcast_add_fusion.19
  752.3 1.2 bitcast_add_fusion.19
  756.1 1.2 bitcast_add_fusion.19
  759.9 1.2 bitcast_add_fusion.19
  763.7 1.2 bitcast_add_fusion.19
  767.5 1.2 bitcast_add_fusion.19
  771.3 1.2 bitcast_add_fusion.19
  775.1 1.2 bitcast_add_fusion.19
  777.0 1.2 bitcast_add_fusion.19
  778.9 1.2 bitcast_add_fusion.19
  780.8 1.2 bitcast_add_fusion.19
  782.7 1.2 bitcast_add_fusion.19
  784.6 1.2 bitcast_add_fusion.19
  786.5 1.2 bitcast_add_fusion.19
  788.4 1.2 bitcast_add_fusion.19
  792.3 1.2 bitcast_add_fusion.19
  796.1 1.2 bitcast_add_fusion.19
  799.9 1.2 bitcast_add_fusion.19
  803.7 1.2 bitcast_add_fusion.19
  807.5 1.2 bitcast_add_fusion.19
  811.3 1.2 bitcast_add_fusion.19
  813.2 1.2 bitcast_add_fusion.19
  815.1 1.2 bitcast_add_fusion.19
  817.0 1.2 bitcast_add_fusion.19
  818.9 1.2 bitcast_add_fusion.19
  820.8 1.2 bitcast_add_fusion.19
  846.2 2.3 while.87
  848.6 3.5 fusion.55
  856.2 3.7 reduce_window_sum.51
  861.7 3.7 reduce_window_sum.50
  866.4 1.5 fusion.66
  867.9 1.7 fusion.33
  869.6 2.0 copy.243
  (273 shorter events, 110.2 us)
Async XLA Ops:
  7.2 7.2 copy-start
  7.2 310.9 %all-gather.6.cloned.1.call-start = ((), (), s32[]{:S(2)}) async-start(), calls=%async_computation | async-start | bytes 34078720 | tf_op jit(solution)/shard_map/all_gather | solution.py:20
  9.4 4.9 copy-start.36
  9.5 4.9 copy-start.30
  9.5 4.9 copy-start.32
  10.2 4.2 copy-start.35
  11.0 3.4 copy-start.19
  11.3 0.8 copy-start.24
  13.4 4.6 copy-start.9
  13.9 1.1 copy-start.4
  14.4 1.0 copy-start.7
  15.4 3.5 copy-start.41
  15.4 4.3 copy-start.40
  17.1 0.8 copy-start.2
  17.1 127.6 %copy-start.16 = (bf16[256,1024]{1,0:T(8,128)(2,1)S(1)}, bf16[256,1024]{1,0:T(8,128)(2,1)}, u32[]{:S(2)}) copy-start(bf16[256,1024]{1,0:T(8,128)(2,1)} %param.25) | copy-start | bytes 1572868
  17.1 130.8 %copy-start.15 = (bf16[256,128]{1,0:T(8,128)(2,1)S(1)}, bf16[256,128]{1,0:T(8,128)(2,1)}, u32[]{:S(2)}) copy-start(bf16[256,128]{1,0:T(8,128)(2,1)} %param.27) | copy-start | bytes 196612
  17.9 706.9 %all-gather.8.cloned.1.call-start = ((), (), s32[]{:S(2)}) async-start(), calls=%async_computation.1 | async-start | bytes 34078720 | tf_op jit(solution)/shard_map/all_gather | solution.py:20
  19.1 309.1 %copy-start.22 = (f32[1024]{0:T(1024)}, f32[1024]{0:T(1024)S(1)}, u32[]{:S(2)}) copy-start(f32[1024]{0:T(1024)S(1)} %mul.385) | copy-start | bytes 12292
  147.8 180.4 %copy-start.34 = (f32[256]{0:T(256)}, f32[256]{0:T(256)S(1)}, u32[]{:S(2)}) copy-start(f32[256]{0:T(256)S(1)} %compare_select_fusion.3) | copy-start | bytes 3076
  318.1 0.6 copy-start.23
  323.0 1.6 copy-start.17
  323.0 1.6 copy-start.29
  323.6 1.0 copy-start.13
  327.3 1.0 copy-start.10
  327.3 1.2 copy-start.12
  328.2 13.7 %copy-start.11 = (bf16[256,1024]{0,1:T(8,128)(2,1)S(1)}, bf16[256,1024]{0,1:T(8,128)(2,1)}, u32[]{:S(2)}) copy-start(bf16[256,1024]{0,1:T(8,128)(2,1)} %copy.223) | copy-start | bytes 1572868
  328.2 13.7 %copy-start.26 = (f32[1024]{0:T(1024)S(1)}, f32[1024]{0:T(1024)}, u32[]{:S(2)}) copy-start(f32[1024]{0:T(1024)} %param.32) | copy-start | bytes 12292
  359.4 4.6 copy-start.42
  364.2 0.8 copy-start.1
  562.1 5.6 copy-start.3
  562.1 5.6 copy-start.18
  724.9 121.3 %copy-start.43 = (f32[2,16,1,1]{1,3,2,0:T(1,128)S(1)}, f32[2,16,1,1]{1,3,2,0:T(1,128)}, u32[]{:S(2)}) copy-start(f32[2,16,1,1]{1,3,2,0:T(1,128)} %get-tuple-element.888) | copy-start | bytes 388
  848.5 4.3 copy-start.38
  848.6 3.5 copy-start.5
  848.6 3.5 copy-start.6
  852.1 1.6 copy-start.20
  852.1 1.6 copy-start.21
  852.1 1.6 copy-start.25
  852.1 1.6 copy-start.27
  852.1 1.6 copy-start.28
  852.2 1.6 copy-start.31
  852.2 1.6 copy-start.33
  852.2 2.3 copy-start.37
  852.9 15.0 %copy-start.8 = (f32[256,1024]{0,1:T(8,128)S(1)}, f32[256,1024]{0,1:T(8,128)}, u32[]{:S(2)}) copy-start(f32[256,1024]{0,1:T(8,128)} %fusion.27) | copy-start | bytes 3145732
  852.9 15.0 %copy-start.14 = (f32[2,128,1,16,64]{1,0,4,3,2:T(2,128)S(1)}, f32[2,128,1,16,64]{1,0,4,3,2:T(2,128)}, u32[]{:S(2)}) copy-start(f32[2,128,1,16,64]{1,0,4,3,2:T(2,128)} %copy.225) | copy-start | bytes 3145732
  852.9 1.6 copy-start.39
Sparse Core Ops, SparseCore 0:
  18.0 299.9 all-gather.5
  365.2 359.5 all-gather.7
where the time goes:
time: 885 us; the launch traced here: 879 us
  blocking collectives  341 us (39%)
  waiting for transfers between devices  322 us (36%)
  other arithmetic  98.8 us (11%)
  local copies, waits for them, and re-layouts  77.1 us (9%)
  matrix products  22.1 us (2%)
  between operations  16 us (2%)
    all_gather x2, waiting for transfers between devices, carried_in(): gathered = jax.tree.map(lambda a: lax.all_gather(a, axis), part)  322 us
    unnamed x2, blocking collectives  314 us
    add x63, other arithmetic, join_pairs(): later[0][:, None, None] * earlier[1] + later[1]  74.3 us
    mul x63, local copies, waits for them, and re-layouts, join_pairs(): later[0][:, None, None] * earlier[1] + later[1]  43.9 us
    psum x2, blocking collectives, per_device(): lax.psum((jnp.sum(shaped * shaped, axis=1), jnp.sum(gain_row * pulling *...  27.3 us
  transfers between devices with their start and end apart: 2, of which 2 were waited for; matrix products, arithmetic and copies ran while one was open for 3% of the time, Pallas kernels for 0%

commit v1 on v0

v1 whole, which is shorter than its diff:
```python
import functools

import jax
import jax.numpy as jnp
from jax import lax
from jax.experimental import pallas as pl
from jax.experimental.pallas import tpu as pltpu
from jax.sharding import Mesh
from jax.sharding import PartitionSpec as P

HEAD_DIM = 64
STATE = 128
STRETCH = 128
LANES = 128
QUAD = 4
EPSILON = 1e-05
F32 = jnp.float32
BF16 = jnp.bfloat16
NN = (((1,), (0,)), ((), ()))
NT = (((1,), (1,)), ((), ()))


def mul(a, b, dims=NN):
    return lax.dot_general(a, b, dims, preferred_element_type=F32)


def exact(a, b, dims=NN):
    return lax.dot_general(
        a, b, dims, precision=lax.Precision.HIGHEST, preferred_element_type=F32
    )


def split(a):
    high = a.astype(BF16)
    return (high, (a - high.astype(F32)).astype(BF16))


def mul_sx(a, b, dims=NN):
    return mul(a[0], b, dims) + mul(a[1], b, dims)


def mul_xs(a, b, dims=NN):
    return mul(a, b[0], dims) + mul(a, b[1], dims)


def mul_ss(a, b, dims=NN):
    return mul(a[0], b[0], dims) + (mul(a[0], b[1], dims) + mul(a[1], b[0], dims))


def spread(a, tile):
    rows = a.shape[0]
    lane = lax.broadcasted_iota(jnp.int32, (rows, LANES), 1)
    left = jnp.broadcast_to(a[:, 2 * tile : 2 * tile + 1], (rows, LANES))
    right = jnp.broadcast_to(a[:, 2 * tile + 1 : 2 * tile + 2], (rows, LANES))
    return jnp.where(lane < HEAD_DIM, left, right)


def cols(tile):
    return pl.ds(tile * LANES, LANES)


def head_sums(values, heads):
    total = None
    for tile, value in enumerate(values):
        lane = lax.broadcasted_iota(jnp.int32, (LANES, heads), 0)
        head = lax.broadcasted_iota(jnp.int32, (LANES, heads), 1)
        ones = jnp.where(head == 2 * tile + (lane >= HEAD_DIM).astype(jnp.int32), 1.0, 0.0)
        part = exact(value, ones.astype(F32))
        total = part if total is None else total + part
    return total


def place_marks(info_ref, docs, rows, axis):
    shape = (rows, 1) if axis == 0 else (1, rows)
    first, live_end = info_ref[docs], info_ref[docs + 1]
    places = first + lax.broadcasted_iota(jnp.int32, shape, axis)
    resets = jnp.maximum(places - live_end + 1, 0)
    start = jnp.int32(0)
    for doc in range(docs):
        inside = jnp.where(start >= first, 1, 0)
        resets = resets + jnp.where(places >= start, inside, 0)
        start = start + info_ref[doc]
    return (places < live_end, resets)


def steps(dt_ref, alog_ref, bias_ref, rows):
    raw = dt_ref[...] + bias_ref[...]
    deltas = jnp.maximum(raw, 0.0) + jnp.log1p(jnp.exp(-jnp.abs(raw)))
    log_decay = -jnp.exp(alog_ref[...]) * deltas
    at = lax.broadcasted_iota(jnp.int32, (rows, rows), 0)
    of = lax.broadcasted_iota(jnp.int32, (rows, rows), 1)
    lower = jnp.where(at >= of, 1.0, 0.0).astype(F32)
    return (raw, deltas, exact(lower, log_decay))


def states_kernel(docs, info_ref, x_ref, b_ref, dt_ref, alog_ref, bias_ref, out_ref):
    rows = x_ref.shape[0]
    tiles = x_ref.shape[1] // LANES
    _, resets = place_marks(info_ref, docs, rows, 0)
    _, deltas, summed = steps(dt_ref, alog_ref, bias_ref, rows)
    ending = summed[rows - 1 : rows, :]
    last = resets[rows - 1 : rows, :]
    weights = jnp.where(resets == last, jnp.exp(ending - summed), 0.0) * deltas
    through = jnp.where(last == 0, jnp.exp(ending), 0.0)
    b_turned = b_ref[...].astype(F32).T.astype(BF16)
    per = tiles // QUAD
    for tile in range(tiles):
        weighted = x_ref[:, cols(tile)].astype(F32) * spread(weights, tile)
        part, half = divmod(tile, per)
        out_ref[part, pl.ds(half * STATE, STATE), :] = mul_xs(b_turned, split(weighted))
    for part in range(QUAD):
        out_ref[part, pl.ds(per * STATE, 8), :] = jnp.concatenate(
            [spread(through, part * per + half) for half in range(per)]
            + [jnp.zeros((8 - per, LANES), F32)]
        )


def within_kernel(
    docs, info_ref, x_ref, b_ref, c_ref, dt_ref, alog_ref, bias_ref, skip_ref, out_ref
):
    rows = x_ref.shape[0]
    tiles = x_ref.shape[1] // LANES
    _, resets = place_marks(info_ref, docs, rows, 0)
    _, resets_row = place_marks(info_ref, docs, rows, 1)
    _, deltas, summed = steps(dt_ref, alog_ref, bias_ref, rows)
    middle = summed[rows // 2 - 1 : rows // 2, :]
    rising = jnp.exp(summed - middle)
    falling = jnp.exp(middle - summed) * deltas
    at = lax.broadcasted_iota(jnp.int32, (rows, rows), 0)
    of = lax.broadcasted_iota(jnp.int32, (rows, rows), 1)
    allowed = (at >= of) & (resets == resets_row)
    crossing = split(jnp.where(allowed, mul(c_ref[...], b_ref[...], NT), 0.0))
    skip = skip_ref[...]
    for tile in range(tiles):
        x = x_ref[:, cols(tile)].astype(F32)
        inner = mul_ss(crossing, split(x * spread(falling, tile)))
        out_ref[:, cols(tile)] = inner * spread(rising, tile) + x * spread(skip, tile)


def sigmoid(value):
    return 1.0 / (1.0 + jnp.exp(-value))


def output_kernel(
    docs,
    info_ref,
    within_ref,
    z_ref,
    cot_ref,
    c_ref,
    dt_ref,
    alog_ref,
    bias_ref,
    gain_ref,
    entering_ref,
    core_ref,
    sums_ref,
):
    rows = z_ref.shape[0]
    tiles = z_ref.shape[1] // LANES
    per = tiles // QUAD
    living, resets = place_marks(info_ref, docs, rows, 0)
    _, _, summed = steps(dt_ref, alog_ref, bias_ref, rows)
    fresh = jnp.where(resets == 0, jnp.exp(summed), 0.0)
    c = c_ref[...]
    squares = jnp.zeros((rows, LANES), F32)
    products = jnp.zeros((rows, LANES), F32)
    for tile in range(tiles):
        part, half = divmod(tile, per)
        entering = split(entering_ref[part, pl.ds(half * STATE, STATE), :])
        core = within_ref[:, cols(tile)] + mul_xs(c, entering) * spread(fresh, tile)
        core_ref[:, cols(tile)] = core
        z = z_ref[:, cols(tile)].astype(F32)
        shaped = jnp.where(living, core * (z * sigmoid(z)), 0.0)
        squares += shaped * shaped
        products += gain_ref[:, cols(tile)] * cot_ref[:, cols(tile)].astype(F32) * shaped
    ones = jnp.ones((8, LANES), F32)
    sums_ref[0:1, :] = exact(ones, squares, NT)[0:1]
    sums_ref[1:2, :] = exact(ones, products, NT)[0:1]


def pull_kernel(
    docs,
    channels,
    info_ref,
    core_ref,
    z_ref,
    cot_ref,
    c_ref,
    dt_ref,
    alog_ref,
    bias_ref,
    gain_ref,
    sums_ref,
    pull_ref,
    out_ref,
    gain_out_ref,
):
    rows = z_ref.shape[0]
    tiles = z_ref.shape[1] // LANES
    per = tiles // QUAD
    living, resets = place_marks(info_ref, docs, rows, 0)
    _, _, summed = steps(dt_ref, alog_ref, bias_ref, rows)
    fresh = jnp.where(resets == 0, jnp.exp(summed), 0.0)
    sums = sums_ref[0]
    for other in range(1, sums_ref.shape[0]):
        sums = sums + sums_ref[other]
    scaling_row = lax.rsqrt(sums[0:1] / channels + EPSILON)
    second_row = scaling_row * scaling_row * scaling_row * sums[1:2] / channels
    at = lax.broadcasted_iota(jnp.int32, (rows, rows), 0)
    of = lax.broadcasted_iota(jnp.int32, (rows, rows), 1)
    scaling = jnp.sum(jnp.where(at == of, scaling_row, 0.0), axis=1, keepdims=True)
    second = jnp.sum(jnp.where(at == of, second_row, 0.0), axis=1, keepdims=True)
    c_turned = c_ref[...].astype(F32).T.astype(BF16)
    for tile in range(tiles):
        part, half = divmod(tile, per)
        z = z_ref[:, cols(tile)].astype(F32)
        gate = jnp.where(living, z * sigmoid(z), 0.0)
        shaped = core_ref[:, cols(tile)] * gate
        scaled = cot_ref[:, cols(tile)].astype(F32) * scaling
        gain_out_ref[:, cols(tile)] = jnp.sum(scaled * shaped, axis=0, keepdims=True)
        pulled = (scaled * gain_ref[:, cols(tile)] - second * shaped) * gate
        pull_ref[:, cols(tile)] = pulled
        out_ref[part, pl.ds(half * STATE, STATE), :] = mul_xs(
            c_turned, split(pulled * spread(fresh, tile))
        )
        out_ref[part, pl.ds(per * STATE, 8), :] = jnp.zeros((8, LANES), F32)


def inner_kernel(
    docs,
    info_ref,
    x_ref,
    b_ref,
    c_ref,
    dt_ref,
    alog_ref,
    bias_ref,
    skip_ref,
    core_ref,
    pull_ref,
    entering_ref,
    inner_ref,
    b_out_ref,
    c_out_ref,
    rows_out_ref,
):
    rows = x_ref.shape[0]
    tiles = x_ref.shape[1] // LANES
    per = tiles // QUAD
    _, resets = place_marks(info_ref, docs, rows, 0)
    _, resets_row = place_marks(info_ref, docs, rows, 1)
    _, deltas, summed = steps(dt_ref, alog_ref, bias_ref, rows)
    middle = summed[rows // 2 - 1 : rows // 2, :]
    rising = jnp.exp(summed - middle)
    falling = jnp.exp(middle - summed)
    fresh = jnp.where(resets == 0, jnp.exp(summed), 0.0)
    falling_steps = falling * deltas
    at = lax.broadcasted_iota(jnp.int32, (rows, rows), 0)
    of = lax.broadcasted_iota(jnp.int32, (rows, rows), 1)
    same = resets == resets_row
    b, c = b_ref[...], c_ref[...]
    turned = split(jnp.where((at <= of) & same, mul(b, c, NT), 0.0))
    skip = skip_ref[...]
    paired = jnp.zeros((rows, rows), F32)
    c_sum = jnp.zeros((rows, STATE), F32)
    along = []
    for tile in range(tiles):
        part, half = divmod(tile, per)
        pulled = pull_ref[:, cols(tile)]
        x = x_ref[:, cols(tile)].astype(F32)
        raised = split(pulled * spread(rising, tile))
        inner_ref[:, cols(tile)] = mul_ss(turned, raised) * spread(falling, tile)
        paired += mul_ss(raised, split(x * spread(falling_steps, tile)), NT)
        entering = split(entering_ref[part, pl.ds(half * STATE, STATE), :])
        c_sum += mul_ss(split(pulled * spread(fresh, tile)), entering, NT)
        along.append(pulled * (core_ref[:, cols(tile)] - x * spread(skip, tile)))
    paired = jnp.where((at >= of) & same, paired, 0.0)
    c_out_ref[...] = (c_sum + mul_sx(split(paired), b)).astype(BF16)
    b_out_ref[...] = mul_sx(split(paired.T), c)
    rows_out_ref[...] = head_sums(along, deltas.shape[1])


def final_kernel(
    docs,
    info_ref,
    x_ref,
    b_ref,
    dt_ref,
    alog_ref,
    bias_ref,
    skip_ref,
    pull_ref,
    inner_ref,
    b_in_ref,
    rows_in_ref,
    entering_ref,
    own_ref,
    later_ref,
    x_out_ref,
    b_out_ref,
    dt_out_ref,
):
    rows = x_ref.shape[0]
    tiles = x_ref.shape[1] // LANES
    per = tiles // QUAD
    _, resets = place_marks(info_ref, docs, rows, 0)
    raw, deltas, summed = steps(dt_ref, alog_ref, bias_ref, rows)
    ending = summed[rows - 1 : rows, :]
    last = resets[rows - 1 : rows, :]
    to_end = jnp.where(resets == last, jnp.exp(ending - summed), 0.0)
    weights = to_end * deltas
    b = b_ref[...]
    skip = skip_ref[...]
    b_sum = b_in_ref[...]
    along = []
    ends = []
    for tile in range(tiles):
        part, half = divmod(tile, per)
        place = pl.ds(half * STATE, STATE)
        later_full = later_ref[part, place, :]
        later = split(later_full)
        x = x_ref[:, cols(tile)].astype(F32)
        back = inner_ref[:, cols(tile)] + mul_xs(b, later) * spread(to_end, tile)
        x_out_ref[:, cols(tile)] = (
            back * spread(deltas, tile) + pull_ref[:, cols(tile)] * spread(skip, tile)
        ).astype(BF16)
        b_sum += mul_ss(split(x * spread(weights, tile)), later, NT)
        along.append(x * back)
        through = own_ref[part, pl.ds(per * STATE + half, 1), :]
        leaving = through * entering_ref[part, place, :] + own_ref[part, place, :]
        ends.append(
            jnp.broadcast_to(jnp.sum(later_full * leaving, axis=0, keepdims=True), (8, LANES))
        )
    b_out_ref[...] = b_sum.astype(BF16)
    heads = deltas.shape[1]
    direct = head_sums(along, heads)
    end_pull = head_sums(ends, heads)[0:1]
    at = lax.broadcasted_iota(jnp.int32, (rows, rows), 0)
    of = lax.broadcasted_iota(jnp.int32, (rows, rows), 1)
    upper = jnp.where(at <= of, 1.0, 0.0).astype(F32)
    log_pull = exact(upper, rows_in_ref[...] - direct * deltas) + end_pull
    dt_out_ref[...] = (direct - jnp.exp(alog_ref[...]) * log_pull) * sigmoid(raw)


def gather_kernel(reverse, got_ref, marks_ref, out_ref):
    count = out_ref.shape[0]
    per = out_ref.shape[1] - 8
    halves = (got_ref.shape[1] - 8) // STATE
    piece = per // halves
    order = list(range(QUAD))
    if reverse:
        order.reverse()
    for half in range(halves):
        place = pl.ds(half * STATE, STATE)
        joined = got_ref[order[0], place, :]
        for one in order[1:]:
            through = marks_ref[one, pl.ds(halves * STATE + half, 1), :]
            joined = through * joined + got_ref[one, place, :]
        for to in range(count):
            out_ref[to, pl.ds(half * piece, piece), :] = joined[to * piece : (to + 1) * piece]
    marks = marks_ref[0, pl.ds(halves * STATE, 8), :]
    for one in range(1, QUAD):
        marks = marks * marks_ref[one, pl.ds(halves * STATE, 8), :]
    for to in range(count):
        out_ref[to, pl.ds(per, 8), :] = marks


def along_kernel(reverse, got_ref, marks_ref, out_ref):
    count = got_ref.shape[0]
    per = out_ref.shape[1]
    halves = 2
    piece = per // halves
    order = list(range(count))
    if reverse:
        order.reverse()
    for half in range(halves):
        place = pl.ds(half * piece, piece)
        holding = jnp.zeros((piece, LANES), F32)
        for one in order:
            out_ref[one, place, :] = holding
            through = marks_ref[one, pl.ds(per + half, 1), :]
            holding = through * holding + got_ref[one, place, :]


def hand_kernel(reverse, back_ref, got_ref, marks_ref, out_ref):
    count = back_ref.shape[0]
    halves = out_ref.shape[1] // STATE
    piece = back_ref.shape[1] // halves
    order = list(range(QUAD))
    if reverse:
        order.reverse()
    for half in range(halves):
        place = pl.ds(half * STATE, STATE)
        holding = jnp.concatenate(
            [back_ref[one, pl.ds(half * piece, piece), :] for one in range(count)]
        )
        for one in order:
            out_ref[one, place, :] = holding
            through = marks_ref[one, pl.ds(halves * STATE + half, 1), :]
            holding = through * holding + got_ref[one, place, :]


def call(kernel, outs, *operands, smem=False):
    in_specs = [pl.BlockSpec(memory_space=pltpu.VMEM) for _ in operands]
    if smem:
        in_specs[0] = pl.BlockSpec(memory_space=pltpu.SMEM)
    many = isinstance(outs, (list, tuple))
    spec = pl.BlockSpec(memory_space=pltpu.VMEM)
    return pl.pallas_call(
        kernel,
        out_shape=outs,
        in_specs=in_specs,
        out_specs=[spec] * len(outs) if many else spec,
        compiler_params=pltpu.CompilerParams(vmem_limit_bytes=32 * 1024 * 1024),
    )(*operands)


def like(shape, kind=F32):
    return jax.ShapeDtypeStruct(shape, kind)


def exchange(value, axis):
    return lax.all_to_all(value, axis, 0, 0, tiled=True)


def carry(own, marks, reverse):
    along = lax.axis_size("z")
    halves = (own.shape[1] - 8) // STATE
    per = halves * STATE // along
    got = exchange(own, "x")
    quad_marks = got if marks is None else marks[0]
    joined = call(
        functools.partial(gather_kernel, reverse),
        like((along, per + 8, LANES)),
        got,
        quad_marks,
    )
    pieces = exchange(joined, "z")
    piece_marks = pieces if marks is None else marks[1]
    scanned = call(
        functools.partial(along_kernel, reverse),
        like((along, per, LANES)),
        pieces,
        piece_marks,
    )
    back = exchange(scanned, "z")
    handed = call(
        functools.partial(hand_kernel, reverse),
        like((QUAD, halves * STATE, LANES)),
        back,
        got,
        quad_marks,
    )
    return (exchange(handed, "x"), (quad_marks, piece_marks))


def per_device(
    inputs_x,
    gate_z,
    input_b,
    input_c,
    dt_raw,
    a_log,
    dt_bias,
    skip_d,
    norm_gain,
    lengths,
    cotangent,
):
    rows, width = inputs_x.shape
    docs = lengths.shape[0]
    along = lax.axis_size("z")
    place = lax.axis_index("z") * lax.axis_size("x") + lax.axis_index("x")
    total = rows * lax.axis_size("z") * lax.axis_size("x")
    channels = float(width * lax.axis_size("tensor"))
    info = jnp.concatenate(
        [lengths, jnp.stack([place * rows, jnp.int32(total - STRETCH)]).astype(jnp.int32)]
    )
    a_log, dt_bias, skip_d = a_log[None, :], dt_bias[None, :], skip_d[None, :]
    gain = norm_gain[None, :]
    message = like((QUAD, width // QUAD // LANES * STATE + 8, LANES))
    wide = like((rows, width))

    own = call(
        functools.partial(states_kernel, docs),
        message,
        info,
        inputs_x,
        input_b,
        dt_raw,
        a_log,
        dt_bias,
        smem=True,
    )
    entering, marks = carry(own, None, False)
    within = call(
        functools.partial(within_kernel, docs),
        wide,
        info,
        inputs_x,
        input_b,
        input_c,
        dt_raw,
        a_log,
        dt_bias,
        skip_d,
        smem=True,
    )
    core, sums = call(
        functools.partial(output_kernel, docs),
        [wide, like((2, rows))],
        info,
        within,
        gate_z,
        cotangent,
        input_c,
        dt_raw,
        a_log,
        dt_bias,
        gain,
        entering,
        smem=True,
    )
    sums = lax.all_gather(sums, "tensor")
    pulled, own_back, gain_part = call(
        functools.partial(pull_kernel, docs, channels),
        [wide, message, like((1, width))],
        info,
        core,
        gate_z,
        cotangent,
        input_c,
        dt_raw,
        a_log,
        dt_bias,
        gain,
        sums,
        smem=True,
    )
    grad_gain = exchange(gain_part.reshape(along, QUAD, -1).transpose(1, 0, 2), "x").sum(0)
    grad_gain = exchange(grad_gain, "z").sum(0)
    later, _ = carry(own_back, marks, True)
    inner, b_part, grad_c, rows_part = call(
        functools.partial(inner_kernel, docs),
        [wide, like((rows, STATE)), like((rows, STATE), BF16), like(dt_raw.shape)],
        info,
        inputs_x,
        input_b,
        input_c,
        dt_raw,
        a_log,
        dt_bias,
        skip_d,
        core,
        pulled,
        entering,
        smem=True,
    )
    grad_x, grad_b, grad_dt = call(
        functools.partial(final_kernel, docs),
        [like((rows, width), BF16), like((rows, STATE), BF16), like(dt_raw.shape)],
        info,
        inputs_x,
        input_b,
        dt_raw,
        a_log,
        dt_bias,
        skip_d,
        pulled,
        inner,
        b_part,
        rows_part,
        entering,
        own,
        later,
        smem=True,
    )
    return (grad_x, grad_b, grad_c, grad_dt, grad_gain)


def solution(mesh):
    count = mesh.devices.shape[0]
    split_mesh = Mesh(
        mesh.devices.reshape(count // QUAD, QUAD, mesh.devices.shape[1]), ("z", "x", "tensor")
    )
    tokens = ("z", "x")
    both = P(tokens, "tensor")
    return jax.shard_map(
        per_device,
        mesh=split_mesh,
        in_specs=(
            both,
            both,
            both,
            both,
            both,
            P("tensor"),
            P("tensor"),
            P("tensor"),
            P("tensor"),
            P(),
            both,
        ),
        out_specs=(both, both, both, both, P(("tensor", "z", "x"))),
        check_vma=False,
    )
```

time: 885 us -> 200 us (0.23)
  the two profiles are of different devices: /device:TPU:1 before, /device:TPU:2 now
where the time goes in v1:
time: 200 us; the launch traced here: 199 us
  blocking collectives  86 us (43%)
  waiting for transfers between devices  40.5 us (20%)
  starting transfers between devices  27 us (14%)
  Pallas kernels  23.7 us (12%)
  local copies, waits for them, and re-layouts  18 us (9%)
  other arithmetic  2.56 us (1%)
    all_to_all x4, blocking collectives, exchange(): return lax.all_to_all(value, axis, 0, 0, tiled=True)  73.9 us
    all_to_all x6, waiting for transfers between devices, exchange(): return lax.all_to_all(value, axis, 0, 0, tiled=True)  40.5 us
    all_to_all x6, starting transfers between devices, exchange(): return lax.all_to_all(value, axis, 0, 0, tiled=True)  27 us
    pallas_call x12, Pallas kernels, call(): pl.pallas_call(kernel, out_shape=outs, in_specs=in_specs, out_specs=[spec...  23.7 us
    unnamed x52, local copies, waits for them, and re-layouts  16.9 us
    all_gather x1, blocking collectives, per_device(): sums = lax.all_gather(sums, 'tensor')  12.1 us
  transfers between devices with their start and end apart: 6, of which 5 were waited for; matrix products, arithmetic and copies ran while one was open for 2% of the time, Pallas kernels for 5%

profile of v1, /device:TPU:2, one launch (start us, length us, event | category | flops | bytes accessed | tf_op | source)
XLA Modules:
  0.0 198.6 jit_solution(10259998090255334542)
XLA Ops:
  0.6 0.0 copy-start.11
  0.6 0.8 copy.28.dt_ref
  1.5 0.0 copy-start.23
  1.5 0.6 copy-done.23
  2.2 0.1 pad_add_fusion.info_ref
  2.2 0.0 copy-done.11
  2.2 0.7 copy-done.19
  2.9 0.0 copy-done.20
  2.9 1.0 copy-done
  4.0 2.2 %shard_map.147.own_ref = f32[4,264,128]{2,1,0:T(8,128)S(1)} custom-call(s32[18]{0:T(128)S(1)} %pad_add_fusion.info_ref, bf16[256,1024]{1,0:T(8,128)(2,1)S(1)} %copy-done, bf16[256,128]{1,0:T(8,128)(2,1)S(1)} %copy-done.11, f32[256,16]{1,0:T(8,128)S(1)} %copy.28.dt_ref, f32[1,16]{1,0:T(1,128)S(1)} %bitcast.10, f32[1,16]{1,0:T(1,128)S(1)} %bitcast.16), custom_call_target="tpu_custom_call" | custom-call | tf_op jit(solution)/shard_map/pallas_call | solution.py:410
  6.1 15.0 %all_to_all.54.got_ref.marks_ref = f32[4,264,128]{2,1,0:T(8,128)S(1)} all-to-all(f32[4,264,128]{2,1,0:T(8,128)S(1)} %shard_map.147.own_ref), channel_id=1, replica_groups=mesh['z'=16,'x'=4,'tensor'=8] {'x'}, dimensions={0} | all-to-all | bytes 1081344 | tf_op jit(solution)/shard_map/all_to_all | solution.py:424
  21.1 28.6 %all_to_all.55.got_ref.marks_ref = f32[16,24,128]{2,1,0:T(8,128)S(1)} all-to-all(f32[16,24,128]{2,1,0:T(8,128)S(1)} %shard_map.148), channel_id=1, replica_groups=mesh['z'=16,'x'=4,'tensor'=8] {'z'}, dimensions={0} | all-to-all | bytes 393216 | tf_op jit(solution)/shard_map/all_to_all | solution.py:424
  49.8 17.6 %all_to_all.56.back_ref = f32[16,16,128]{2,1,0:T(8,128)S(1)} all-to-all(f32[16,16,128]{2,1,0:T(8,128)S(1)} %shard_map.149), channel_id=1, replica_groups=mesh['z'=16,'x'=4,'tensor'=8] {'z'}, dimensions={0} | all-to-all | bytes 262144 | tf_op jit(solution)/shard_map/all_to_all | solution.py:424
  67.3 0.8 shard_map.150
  68.1 5.0 %all-to-all-start.3 = ((f32[4,256,128]{2,1,0:T(8,128)}), f32[4,256,128]{2,1,0:T(8,128)S(1)}, u32[]{:S(2)}, u32[]{:S(2)}) async-start(f32[4,256,128]{2,1,0:T(8,128)} %shard_map.150), calls=%async_computation.3 | async-start | bytes 1048576 | tf_op jit(solution)/shard_map/all_to_all | solution.py:424
  73.2 0.0 copy-done.1
  73.2 0.7 copy-done.22
  73.8 0.8 copy-done.12
  74.7 0.8 copy-done.14
  75.5 2.8 %shard_map.146.within_ref = f32[256,1024]{1,0:T(8,128)S(1)} custom-call(s32[18]{0:T(128)S(1)} %pad_add_fusion.info_ref, bf16[256,1024]{1,0:T(8,128)(2,1)S(1)} %copy-done.1, bf16[256,128]{1,0:T(8,128)(2,1)S(1)} %copy-done.12, bf16[256,128]{1,0:T(8,128)(2,1)S(1)} %copy-done.14, f32[256,16]{1,0:T(8,128)S(1)} %copy.28.dt_ref, f32[1,16]{1,0:T(1,128)S(1)} %bitcast.11, ...), custom_call_target="tpu_custom_call" | custom-call | tf_op jit(solution)/shard_map/pallas_call | solution.py:410
  78.3 0.0 copy-start.7
  78.3 1.0 copy-done.7
  79.3 0.5 all-to-all-done.3.entering_ref
  79.8 0.0 copy-done.9
  79.8 0.0 copy-done.10
  79.8 0.0 copy-done.21
  79.8 0.0 copy-start.8
  79.8 1.2 copy-done.8
  81.0 0.8 copy-done.15
  81.9 2.3 %shard_map.151 = (f32[256,1024]{1,0:T(8,128)S(1)}, f32[2,256]{1,0:T(2,128)S(1)}) custom-call(s32[18]{0:T(128)S(1)} %pad_add_fusion.info_ref, f32[256,1024]{1,0:T(8,128)S(1)} %copy-done.8, bf16[256,1024]{1,0:T(8,128)(2,1)S(1)} %copy-done.9, bf16[256,1024]{1,0:T(8,128)(2,1)S(1)} %copy-done.10, bf16[256,128]{1,0:T(8,128)(2,1)S(1)} %copy-done.15, ...), custom_call_target="tpu_custom_call" | custom-call | tf_op jit(solution)/shard_map/pallas_call | solution.py:410
  84.2 12.1 %all-gather.1.sums_ref = f32[8,2,256]{2,1,0:T(2,128)S(1)} all-gather(f32[1,2,256]{2,1,0:T(2,128)S(1)} %bitcast.27), channel_id=2, replica_groups=mesh['z'=16,'x'=4,'tensor'=8] {'tensor'}, dimensions={0}, use_global_device_ids=true | all-gather | bytes 18432 | tf_op jit(solution)/shard_map/all_gather | solution.py:525
  96.3 2.4 %shard_map.152 = (f32[256,1024]{1,0:T(8,128)S(1)}, f32[4,264,128]{2,1,0:T(8,128)S(1)}, f32[1,1024]{1,0:T(1,128)S(1)}) custom-call(s32[18]{0:T(128)S(1)} %pad_add_fusion.info_ref, f32[256,1024]{1,0:T(8,128)S(1)} %get-tuple-element.17.core_ref, bf16[256,1024]{1,0:T(8,128)(2,1)S(1)} %copy-done.9, bf16[256,1024]{1,0:T(8,128)(2,1)S(1)} %copy-done.10, ...), custom_call_target="tpu_custom_call" | custom-call | tf_op jit(solution)/shard_map/pallas_call | solution.py:410
  98.7 1.0 copy-done.4
  99.7 12.8 %all_to_all.57.got_ref = f32[4,264,128]{2,1,0:T(8,128)S(1)} all-to-all(f32[4,264,128]{2,1,0:T(8,128)S(1)} %get-tuple-element.23), channel_id=1, replica_groups=mesh['z'=16,'x'=4,'tensor'=8] {'x'}, dimensions={0} | all-to-all | bytes 1081344 | tf_op jit(solution)/shard_map/all_to_all | solution.py:424
  112.5 0.7 shard_map.154
  113.2 3.7 %all-to-all-start.5 = ((f32[16,24,128]{2,1,0:T(8,128)}), f32[16,24,128]{2,1,0:T(8,128)S(1)}, u32[]{:S(2)}, u32[]{:S(2)}) async-start(f32[16,24,128]{2,1,0:T(8,128)} %shard_map.154), calls=%async_computation.5 | async-start | bytes 393216 | tf_op jit(solution)/shard_map/all_to_all | solution.py:424
  117.0 0.5 broadcast.3
  117.5 0.7 reduce.4
  118.1 0.1 reshape.15
  118.2 0.7 reshape.29
  118.9 13.9 %all-to-all-done.5.got_ref = f32[16,24,128]{2,1,0:T(8,128)S(1)} async-done(((f32[16,24,128]{2,1,0:T(8,128)}), f32[16,24,128]{2,1,0:T(8,128)S(1)}, u32[]{:S(2)}, u32[]{:S(2)}) %all-to-all-start.5) | async-done | bytes 196640 | tf_op jit(solution)/shard_map/all_to_all | solution.py:424
  132.9 4.7 %all-to-all-start.8 = ((f32[4,1,256]{2,1,0:T(1,128)}), f32[4,1,256]{2,1,0:T(1,128)S(1)}, u32[]{:S(2)}, u32[]{:S(2)}) async-start(f32[4,1,256]{2,1,0:T(1,128)} %reshape.29), calls=%async_computation.8 | async-start | bytes 8192 | tf_op jit(solution)/shard_map/all_to_all | solution.py:424
  137.5 0.7 shard_map.155
  138.2 3.1 %all-to-all-done.8 = f32[4,1,256]{2,1,0:T(1,128)S(1)} async-done(((f32[4,1,256]{2,1,0:T(1,128)}), f32[4,1,256]{2,1,0:T(1,128)S(1)}, u32[]{:S(2)}, u32[]{:S(2)}) %all-to-all-start.8) | async-done | bytes 4128 | tf_op jit(solution)/shard_map/all_to_all | solution.py:424
  141.4 4.8 %all-to-all-start.6 = ((f32[16,16,128]{2,1,0:T(8,128)}), f32[16,16,128]{2,1,0:T(8,128)S(1)}, u32[]{:S(2)}, u32[]{:S(2)}) async-start(f32[16,16,128]{2,1,0:T(8,128)} %shard_map.155), calls=%async_computation.6 | async-start | bytes 262144 | tf_op jit(solution)/shard_map/all_to_all | solution.py:424
  146.2 0.5 broadcast.4
  146.7 0.7 reduce.5
  147.3 0.1 reshape.30
  147.4 0.6 reduce_sum.18
  148.0 11.3 %all-to-all-done.6.back_ref = f32[16,16,128]{2,1,0:T(8,128)S(1)} async-done(((f32[16,16,128]{2,1,0:T(8,128)}), f32[16,16,128]{2,1,0:T(8,128)S(1)}, u32[]{:S(2)}, u32[]{:S(2)}) %all-to-all-start.6) | async-done | bytes 131104 | tf_op jit(solution)/shard_map/all_to_all | solution.py:424
  159.4 3.9 %all-to-all-start.9 = ((f32[16,1,16]{2,1,0:T(1,128)}), f32[16,1,16]{2,1,0:T(1,128)S(1)}, u32[]{:S(2)}, u32[]{:S(2)}) async-start(f32[16,1,16]{2,1,0:T(1,128)} %bitcast.7), calls=%async_computation.9 | async-start | bytes 16384 | tf_op jit(solution)/shard_map/all_to_all | solution.py:424
  163.3 0.8 shard_map.156
  164.2 11.5 %all-to-all-done.9 = f32[16,1,16]{2,1,0:T(1,128)S(1)} async-done(((f32[16,1,16]{2,1,0:T(1,128)}), f32[16,1,16]{2,1,0:T(1,128)S(1)}, u32[]{:S(2)}, u32[]{:S(2)}) %all-to-all-start.9) | async-done | bytes 1056 | tf_op jit(solution)/shard_map/all_to_all | solution.py:424
  175.7 4.9 %all-to-all-start.7 = ((f32[4,256,128]{2,1,0:T(8,128)}), f32[4,256,128]{2,1,0:T(8,128)S(1)}, u32[]{:S(2)}, u32[]{:S(2)}) async-start(f32[4,256,128]{2,1,0:T(8,128)} %shard_map.156), calls=%async_computation.7 | async-start | bytes 1048576 | tf_op jit(solution)/shard_map/all_to_all | solution.py:424
  180.6 1.2 copy-done.3
  181.8 1.2 copy-done.5
  183.0 6.2 %shard_map.153 = (f32[256,1024]{1,0:T(8,128)S(1)}, f32[256,128]{1,0:T(8,128)S(1)}, bf16[256,128]{1,0:T(8,128)(2,1)}, f32[256,16]{1,0:T(8,128)S(1)}) custom-call(s32[18]{0:T(128)S(1)} %pad_add_fusion.info_ref, bf16[256,1024]{1,0:T(8,128)(2,1)S(1)} %copy-done.1, bf16[256,128]{1,0:T(8,128)(2,1)S(1)} %copy-done.13, bf16[256,128]{1,0:T(8,128)(2,1)S(1)} %copy-done.16, ...), custom_call_target="tpu_custom_call" | custom-call | tf_op jit(solution)/shard_map/pallas_call | solution.py:410
  189.2 1.0 copy-done.17
  190.2 0.5 reduce_sum.19
  190.7 0.0 all-to-all-done.7.later_ref
  190.7 1.2 copy-done.6
  192.0 1.2 copy-done.18
  193.2 4.7 %shard_map.157 = (bf16[256,1024]{1,0:T(8,128)(2,1)}, bf16[256,128]{1,0:T(8,128)(2,1)}, f32[256,16]{1,0:T(8,128)S(1)}) custom-call(s32[18]{0:T(128)S(1)} %pad_add_fusion.info_ref, bf16[256,1024]{1,0:T(8,128)(2,1)S(1)} %copy-done.1, bf16[256,128]{1,0:T(8,128)(2,1)S(1)} %copy-done.13, f32[256,16]{1,0:T(8,128)S(1)} %copy.28.dt_ref, f32[1,16]{1,0:T(1,128)S(1)} %bitcast.15, ...), custom_call_target="tpu_custom_call" | custom-call | tf_op jit(solution)/shard_map/pallas_call | solution.py:410
  197.9 0.7 copy.30
  (26 shorter events, 0.1 us)
Async XLA Ops:
  0.6 1.6 copy-start.11
  1.5 0.7 copy-start.23
  2.2 0.7 copy-start.19
  2.2 0.7 copy-start.20
  2.9 1.0 copy-start
  68.1 5.0 %copy-start.1 = (bf16[256,1024]{1,0:T(8,128)(2,1)S(1)}, bf16[256,1024]{1,0:T(8,128)(2,1)}, u32[]{:S(2)}) copy-start(bf16[256,1024]{1,0:T(8,128)(2,1)} %x_ref.7) | copy-start | bytes 1572868
  68.1 11.7 %all-to-all-start.3 = ((f32[4,256,128]{2,1,0:T(8,128)}), f32[4,256,128]{2,1,0:T(8,128)S(1)}, u32[]{:S(2)}, u32[]{:S(2)}) async-start(f32[4,256,128]{2,1,0:T(8,128)} %shard_map.150), calls=%async_computation.3 | async-start | bytes 1048576 | tf_op jit(solution)/shard_map/all_to_all | solution.py:424
  73.2 0.7 copy-start.22
  73.8 0.8 copy-start.12
  74.7 0.8 copy-start.14
  75.5 4.3 %copy-start.9 = (bf16[256,1024]{1,0:T(8,128)(2,1)S(1)}, bf16[256,1024]{1,0:T(8,128)(2,1)}, u32[]{:S(2)}) copy-start(bf16[256,1024]{1,0:T(8,128)(2,1)} %z_ref.3) | copy-start | bytes 1572868
  75.5 4.3 %copy-start.10 = (bf16[256,1024]{1,0:T(8,128)(2,1)S(1)}, bf16[256,1024]{1,0:T(8,128)(2,1)}, u32[]{:S(2)}) copy-start(bf16[256,1024]{1,0:T(8,128)(2,1)} %cot_ref.3) | copy-start | bytes 1572868
  75.5 4.3 %copy-start.21 = (f32[1024]{0:T(1024)S(1)}, f32[1024]{0:T(1024)}, u32[]{:S(2)}) copy-start(f32[1024]{0:T(1024)} %param.19) | copy-start | bytes 12292
  78.3 1.0 copy-start.7
  79.8 1.2 copy-start.8
  81.0 0.8 copy-start.15
  84.2 14.5 %copy-start.2 = (f32[256,1024]{1,0:T(8,128)}, f32[256,1024]{1,0:T(8,128)S(1)}, u32[]{:S(2)}) copy-start(f32[256,1024]{1,0:T(8,128)S(1)} %get-tuple-element.17.core_ref) | copy-start | bytes 3145732
  98.7 1.0 copy-start.4
  113.2 19.6 %all-to-all-start.5 = ((f32[16,24,128]{2,1,0:T(8,128)}), f32[16,24,128]{2,1,0:T(8,128)S(1)}, u32[]{:S(2)}, u32[]{:S(2)}) async-start(f32[16,24,128]{2,1,0:T(8,128)} %shard_map.154), calls=%async_computation.5 | async-start | bytes 393216 | tf_op jit(solution)/shard_map/all_to_all | solution.py:424
  132.9 8.5 %all-to-all-start.8 = ((f32[4,1,256]{2,1,0:T(1,128)}), f32[4,1,256]{2,1,0:T(1,128)S(1)}, u32[]{:S(2)}, u32[]{:S(2)}) async-start(f32[4,1,256]{2,1,0:T(1,128)} %reshape.29), calls=%async_computation.8 | async-start | bytes 8192 | tf_op jit(solution)/shard_map/all_to_all | solution.py:424
  141.4 18.0 %all-to-all-start.6 = ((f32[16,16,128]{2,1,0:T(8,128)}), f32[16,16,128]{2,1,0:T(8,128)S(1)}, u32[]{:S(2)}, u32[]{:S(2)}) async-start(f32[16,16,128]{2,1,0:T(8,128)} %shard_map.155), calls=%async_computation.6 | async-start | bytes 262144 | tf_op jit(solution)/shard_map/all_to_all | solution.py:424
  159.4 16.3 %all-to-all-start.9 = ((f32[16,1,16]{2,1,0:T(1,128)}), f32[16,1,16]{2,1,0:T(1,128)S(1)}, u32[]{:S(2)}, u32[]{:S(2)}) async-start(f32[16,1,16]{2,1,0:T(1,128)} %bitcast.7), calls=%async_computation.9 | async-start | bytes 16384 | tf_op jit(solution)/shard_map/all_to_all | solution.py:424
  164.2 16.4 %copy-start.13 = (bf16[256,128]{1,0:T(8,128)(2,1)S(1)}, bf16[256,128]{1,0:T(8,128)(2,1)}, u32[]{:S(2)}) copy-start(bf16[256,128]{1,0:T(8,128)(2,1)} %b_ref.7) | copy-start | bytes 196612
  164.2 16.4 %copy-start.16 = (bf16[256,128]{1,0:T(8,128)(2,1)S(1)}, bf16[256,128]{1,0:T(8,128)(2,1)}, u32[]{:S(2)}) copy-start(bf16[256,128]{1,0:T(8,128)(2,1)} %c_ref.7) | copy-start | bytes 196612
  175.7 15.0 %all-to-all-start.7 = ((f32[4,256,128]{2,1,0:T(8,128)}), f32[4,256,128]{2,1,0:T(8,128)S(1)}, u32[]{:S(2)}, u32[]{:S(2)}) async-start(f32[4,256,128]{2,1,0:T(8,128)} %shard_map.156), calls=%async_computation.7 | async-start | bytes 1048576 | tf_op jit(solution)/shard_map/all_to_all | solution.py:424
  180.6 1.2 copy-start.3
  181.8 1.2 copy-start.5
  189.2 1.0 copy-start.17
  190.7 1.2 copy-start.6
  192.0 1.2 copy-start.18

commit v2 on v0

v2 whole, which is shorter than its diff:
```python
import functools

import jax
import jax.numpy as jnp
from jax import lax
from jax.experimental import pallas as pl
from jax.experimental.pallas import tpu as pltpu
from jax.sharding import Mesh
from jax.sharding import PartitionSpec as P

HEAD_DIM = 64
STATE = 128
STRETCH = 128
LANES = 128
WIDE = 2 * LANES
GROUP = 8
EPSILON = 1e-05
F32 = jnp.float32
BF16 = jnp.bfloat16
NN = (((1,), (0,)), ((), ()))
NT = (((1,), (1,)), ((), ()))


def mul(a, b, dims=NN):
    return lax.dot_general(a, b, dims, preferred_element_type=F32)


def split(a):
    high = a.astype(BF16)
    return (high, (a - high.astype(F32)).astype(BF16))


def mul_sx(a, b, dims=NN):
    return mul(a[0], b, dims) + mul(a[1], b, dims)


def mul_xs(a, b, dims=NN):
    return mul(a, b[0], dims) + mul(a, b[1], dims)


def mul_ss(a, b, dims=NN):
    return mul(a[0], b[0], dims) + (mul(a[0], b[1], dims) + mul(a[1], b[0], dims))


def mul_3x(a, b, dims=NN):
    high = a.astype(BF16)
    rest = a - high.astype(F32)
    middle = rest.astype(BF16)
    low = (rest - middle.astype(F32)).astype(BF16)
    return mul(high, b, dims) + (mul(middle, b, dims) + mul(low, b, dims))


def spread(a, pair):
    rows = a.shape[0]
    lane = lax.broadcasted_iota(jnp.int32, (rows, LANES), 1)
    tiles = []
    for one in (4 * pair, 4 * pair + 2):
        left = jnp.broadcast_to(a[:, one : one + 1], (rows, LANES))
        right = jnp.broadcast_to(a[:, one + 1 : one + 2], (rows, LANES))
        tiles.append(jnp.where(lane < HEAD_DIM, left, right))
    return jnp.concatenate(tiles, axis=1)


def cols(pair):
    return pl.ds(pair * WIDE, WIDE)


def two_tiles(ref, pair, place):
    return jnp.concatenate([ref[2 * pair, place, :], ref[2 * pair + 1, place, :]], axis=1)


def head_marks(heads, pair):
    head = lax.broadcasted_iota(jnp.int32, (heads, WIDE), 0)
    lane = lax.broadcasted_iota(jnp.int32, (heads, WIDE), 1)
    start = (head - 4 * pair) * HEAD_DIM
    return jnp.where((lane >= start) & (lane < start + HEAD_DIM), 1.0, 0.0).astype(BF16)


def ordered(rows):
    at = lax.broadcasted_iota(jnp.int32, (rows, rows), 0)
    of = lax.broadcasted_iota(jnp.int32, (rows, rows), 1)
    return (at, of)


def place_marks(info_ref, docs, rows, axis):
    shape = (rows, 1) if axis == 0 else (1, rows)
    first, live_end = info_ref[docs], info_ref[docs + 1]
    places = first + lax.broadcasted_iota(jnp.int32, shape, axis)
    resets = jnp.maximum(places - live_end + 1, 0)
    start = jnp.int32(0)
    for doc in range(docs):
        inside = jnp.where(start >= first, 1, 0)
        resets = resets + jnp.where(places >= start, inside, 0)
        start = start + info_ref[doc]
    return (places < live_end, resets)


def softplus(value):
    return jnp.maximum(value, 0.0) + jnp.log1p(jnp.exp(-jnp.abs(value)))


def sigmoid(value):
    return 1.0 / (1.0 + jnp.exp(-value))


def states_kernel(
    docs, info_ref, x_ref, b_ref, dt_ref, alog_ref, bias_ref, out_ref, summed_ref, deltas_ref
):
    rows = x_ref.shape[0]
    pairs = x_ref.shape[1] // WIDE
    _, resets = place_marks(info_ref, docs, rows, 0)
    at, of = ordered(rows)
    deltas_row = softplus(dt_ref[...] + bias_ref[...])
    before = jnp.where(at <= of, 1.0, 0.0).astype(BF16)
    summed = mul_3x(-jnp.exp(alog_ref[...]) * deltas_row, before).T
    deltas = deltas_row.T
    summed_ref[...] = summed
    deltas_ref[...] = deltas
    ending = summed[rows - 1 : rows, :]
    last = resets[rows - 1 : rows, :]
    weights = jnp.where(resets == last, jnp.exp(ending - summed), 0.0) * deltas
    through = jnp.broadcast_to(jnp.where(last == 0, jnp.exp(ending), 0.0), (8, deltas.shape[1]))
    b_turned = b_ref[...].astype(F32).T.astype(BF16)
    for pair in range(pairs):
        weighted = x_ref[:, cols(pair)].astype(F32) * spread(weights, pair)
        state = mul_xs(b_turned, split(weighted))
        marks = spread(through, pair)
        for half in range(2):
            lanes = slice(half * LANES, (half + 1) * LANES)
            out_ref[2 * pair + half, 0:STATE, :] = state[:, lanes]
            out_ref[2 * pair + half, STATE : STATE + 8, :] = marks[:, lanes]


def within_kernel(
    docs,
    info_ref,
    x_ref,
    z_ref,
    cot_ref,
    b_ref,
    c_ref,
    summed_ref,
    deltas_ref,
    skip_ref,
    out_ref,
    fresh_ref,
    gate_ref,
    gated_ref,
):
    rows = x_ref.shape[0]
    pairs = x_ref.shape[1] // WIDE
    living, resets = place_marks(info_ref, docs, rows, 0)
    _, resets_row = place_marks(info_ref, docs, rows, 1)
    deltas, summed = deltas_ref[...], summed_ref[...]
    middle = summed[rows // 2 - 1 : rows // 2, :]
    rising = jnp.exp(summed - middle)
    falling = jnp.exp(middle - summed) * deltas
    fresh = jnp.where(resets == 0, jnp.exp(summed), 0.0)
    at, of = ordered(rows)
    allowed = (at >= of) & (resets == resets_row)
    crossing = split(jnp.where(allowed, mul(c_ref[...], b_ref[...], NT), 0.0))
    skip = skip_ref[...]
    for pair in range(pairs):
        x = x_ref[:, cols(pair)].astype(F32)
        inner = mul_ss(crossing, split(x * spread(falling, pair)))
        out_ref[:, cols(pair)] = inner * spread(rising, pair) + x * spread(skip, pair)
        fresh_ref[:, cols(pair)] = spread(fresh, pair)
        z = z_ref[:, cols(pair)].astype(F32)
        gate = jnp.where(living, z * sigmoid(z), 0.0)
        gate_ref[:, cols(pair)] = gate
        gated_ref[:, cols(pair)] = gate * cot_ref[:, cols(pair)].astype(F32)


def output_kernel(
    within_ref,
    fresh_ref,
    gate_ref,
    gated_ref,
    c_ref,
    gain_ref,
    entering_ref,
    core_ref,
    bent_ref,
    sums_ref,
):
    rows, width = within_ref.shape
    c = c_ref[...]
    c_twice = jnp.concatenate([c, c], axis=1)
    squares = jnp.zeros((rows, WIDE), F32)
    products = jnp.zeros((rows, WIDE), F32)
    for pair in range(width // WIDE):
        entering = split(two_tiles(entering_ref, pair, slice(None)))
        carried = mul(c_twice, jnp.concatenate(entering, axis=0))
        core = within_ref[:, cols(pair)] + carried * fresh_ref[:, cols(pair)]
        core_ref[:, cols(pair)] = core
        gate = gate_ref[:, cols(pair)]
        shaped = core * gate
        bent_ref[:, cols(pair)] = shaped * gate
        squares += shaped * shaped
        products += gain_ref[:, cols(pair)] * (gated_ref[:, cols(pair)] * core)
    ones = jnp.ones((8, WIDE), BF16)
    for row, total in enumerate((squares, products)):
        high, low = split(total)
        rest = (total - high.astype(F32) - low.astype(F32)).astype(BF16)
        sum_row = mul(ones, high, NT) + (mul(ones, low, NT) + mul(ones, rest, NT))
        sums_ref[row : row + 1, :] = sum_row[0:1]


def pull_kernel(
    channels,
    core_ref,
    bent_ref,
    gated_ref,
    fresh_ref,
    c_ref,
    gain_ref,
    sums_ref,
    pull_ref,
    out_ref,
):
    rows, width = core_ref.shape
    sums = sums_ref[0]
    for other in range(1, sums_ref.shape[0]):
        sums = sums + sums_ref[other]
    scaling_row = lax.rsqrt(sums[0:1] / channels + EPSILON)
    second_row = scaling_row * scaling_row * scaling_row * sums[1:2] / channels
    at, of = ordered(rows)
    scaling = jnp.sum(jnp.where(at == of, scaling_row, 0.0), axis=1, keepdims=True)
    second = jnp.sum(jnp.where(at == of, second_row, 0.0), axis=1, keepdims=True)
    c_turned = c_ref[...].astype(F32).T.astype(BF16)
    gains = []
    for pair in range(width // WIDE):
        scaled = gated_ref[:, cols(pair)] * scaling
        gain_sum = jnp.sum(scaled * core_ref[:, cols(pair)], axis=0, keepdims=True)
        gains += [gain_sum[:, :LANES], gain_sum[:, LANES:]]
        pulled = scaled * gain_ref[:, cols(pair)] - second * bent_ref[:, cols(pair)]
        pull_ref[:, cols(pair)] = pulled
        state = mul_xs(c_turned, split(pulled * fresh_ref[:, cols(pair)]))
        out_ref[2 * pair, 0:STATE, :] = state[:, :LANES]
        out_ref[2 * pair + 1, 0:STATE, :] = state[:, LANES:]
    for member in range(GROUP):
        for one in range(GROUP):
            out_ref[member, STATE + one : STATE + one + 1, :] = gains[one]


def inner_kernel(
    docs,
    info_ref,
    x_ref,
    b_ref,
    c_ref,
    summed_ref,
    deltas_ref,
    skip_ref,
    core_ref,
    pull_ref,
    fresh_ref,
    entering_ref,
    own_ref,
    base_ref,
    weights_ref,
    leaving_ref,
    b_out_ref,
    c_out_ref,
    along_ref,
    back_ref,
):
    rows = x_ref.shape[0]
    pairs = x_ref.shape[1] // WIDE
    _, resets = place_marks(info_ref, docs, rows, 0)
    _, resets_row = place_marks(info_ref, docs, rows, 1)
    deltas, summed = deltas_ref[...], summed_ref[...]
    heads = deltas.shape[1]
    middle = summed[rows // 2 - 1 : rows // 2, :]
    rising = jnp.exp(summed - middle)
    falling = jnp.exp(middle - summed) * deltas
    ending = summed[rows - 1 : rows, :]
    last = resets[rows - 1 : rows, :]
    weights = jnp.where(resets == last, jnp.exp(ending - summed), 0.0) * deltas
    at, of = ordered(rows)
    same = resets == resets_row
    b, c = b_ref[...], c_ref[...]
    turned = split(jnp.where((at <= of) & same, mul(b, c, NT), 0.0))
    skip = skip_ref[...]
    paired = jnp.zeros((rows, rows), F32)
    c_sum = jnp.zeros((rows, STATE), F32)
    along = jnp.zeros((heads, rows), F32)
    back = jnp.zeros((heads, rows), F32)
    for pair in range(pairs):
        pulled = pull_ref[:, cols(pair)]
        x = x_ref[:, cols(pair)].astype(F32)
        raised = split(pulled * spread(rising, pair))
        lowered = spread(falling, pair)
        direct = mul_ss(turned, raised) * lowered
        skipped = spread(skip, pair)
        base_ref[:, cols(pair)] = direct + skipped * pulled
        weights_ref[:, cols(pair)] = spread(weights, pair)
        paired += mul_ss(raised, split(x * lowered), NT)
        entering = two_tiles(entering_ref, pair, slice(None))
        c_sum += mul_ss(split(pulled * fresh_ref[:, cols(pair)]), split(entering), NT)
        marks = head_marks(heads, pair)
        along += mul_xs(marks, split(pulled * (core_ref[:, cols(pair)] - x * skipped)), NT)
        back += mul_xs(marks, split(x * direct), NT)
        through = two_tiles(own_ref, pair, slice(STATE, STATE + 1))
        leaving = through * entering + two_tiles(own_ref, pair, slice(0, STATE))
        leaving_ref[:, cols(pair)] = leaving
    paired = jnp.where((at >= of) & same, paired, 0.0)
    c_out_ref[...] = (c_sum + mul_sx(split(paired), b)).astype(BF16)
    b_out_ref[...] = mul_sx(split(paired.T), c)
    along_ref[...] = along
    back_ref[...] = back


def final_kernel(
    x_ref,
    b_ref,
    dt_ref,
    alog_ref,
    bias_ref,
    base_ref,
    weights_ref,
    leaving_ref,
    b_in_ref,
    along_ref,
    back_ref,
    later_ref,
    x_out_ref,
    b_out_ref,
    dt_out_ref,
):
    rows = x_ref.shape[0]
    heads = dt_ref.shape[0]
    b = b_ref[...]
    b_twice = jnp.concatenate([b, b], axis=1)
    b_sum = b_in_ref[...]
    back = back_ref[...]
    ends = jnp.zeros((heads, 8), F32)
    for pair in range(x_ref.shape[1] // WIDE):
        later_full = two_tiles(later_ref, pair, slice(None))
        later = split(later_full)
        weights = weights_ref[:, cols(pair)]
        gained = mul(b_twice, jnp.concatenate(later, axis=0)) * weights
        x_out_ref[:, cols(pair)] = (base_ref[:, cols(pair)] + gained).astype(BF16)
        x = x_ref[:, cols(pair)].astype(F32)
        b_sum += mul_ss(split(x * weights), later, NT)
        marks = head_marks(heads, pair)
        back += mul_xs(marks, split(x * gained), NT)
        end = jnp.sum(later_full * leaving_ref[:, cols(pair)], axis=0, keepdims=True)
        ends += mul_xs(marks, split(jnp.broadcast_to(end, (8, WIDE))), NT)
    b_out_ref[...] = b_sum.astype(BF16)
    at, of = ordered(rows)
    after = jnp.where(at >= of, 1.0, 0.0).astype(BF16)
    log_pull = mul_3x(along_ref[...] - back, after) + ends[:, 0:1]
    raw = dt_ref[...] + bias_ref[...]
    direct = back / softplus(raw)
    dt_out_ref[...] = (direct - jnp.exp(alog_ref[...]) * log_pull) * sigmoid(raw)


def gather_kernel(reverse, got_ref, marks_ref, out_ref, rest_ref):
    order = list(range(GROUP))
    if reverse:
        order.reverse()
    joined = got_ref[order[0], 0:STATE, :]
    rest = got_ref[0, STATE : STATE + 8, :]
    marks = marks_ref[0, STATE : STATE + 8, :]
    for one in order[1:]:
        joined = marks_ref[one, STATE : STATE + 1, :] * joined + got_ref[one, 0:STATE, :]
    for one in range(1, GROUP):
        rest = rest + got_ref[one, STATE : STATE + 8, :]
        marks = marks * marks_ref[one, STATE : STATE + 8, :]
    out_ref[0:STATE, :] = joined
    out_ref[STATE : STATE + 8, :] = marks
    rest_ref[...] = rest


def join_kernel(own_ref, got_ref, out_ref):
    through = own_ref[STATE : STATE + 1, :]
    out_ref[0:STATE, :] = own_ref[0:STATE, :] + through * got_ref[0:STATE, :]
    out_ref[STATE : STATE + 8, :] = (
        own_ref[STATE : STATE + 8, :] * got_ref[STATE : STATE + 8, :]
    )


def hand_kernel(reverse, near_ref, far_ref, got_ref, marks_ref, out_ref):
    order = list(range(GROUP))
    if reverse:
        order.reverse()
    holding = near_ref[0:STATE, :] + near_ref[STATE : STATE + 1, :] * far_ref[0:STATE, :]
    for one in order:
        out_ref[one] = holding
        if one != order[-1]:
            through = marks_ref[one, STATE : STATE + 1, :]
            holding = through * holding + got_ref[one, 0:STATE, :]


def call(kernel, outs, *operands, smem=False):
    in_specs = [pl.BlockSpec(memory_space=pltpu.VMEM) for _ in operands]
    if smem:
        in_specs[0] = pl.BlockSpec(memory_space=pltpu.SMEM)
    many = isinstance(outs, (list, tuple))
    spec = pl.BlockSpec(memory_space=pltpu.VMEM)
    return pl.pallas_call(
        kernel,
        out_shape=outs,
        in_specs=in_specs,
        out_specs=[spec] * len(outs) if many else spec,
        compiler_params=pltpu.CompilerParams(vmem_limit_bytes=32 * 1024 * 1024),
    )(*operands)


def like(shape, kind=F32):
    return jax.ShapeDtypeStruct(shape, kind)


def exchange(value):
    return lax.all_to_all(value, ("zl", "x"), 0, 0, tiled=True)


def moved(value, by):
    count = lax.axis_size("zh")
    pairs = [(i, i + by) for i in range(count) if 0 <= i + by < count]
    return lax.ppermute(value, "zh", pairs) if pairs else jnp.zeros_like(value)


def swapped(value, bit):
    count = lax.axis_size("zh")
    if bit >= count:
        return jnp.zeros_like(value)
    return lax.ppermute(value, "zh", [(i, i ^ bit) for i in range(count)])


def carry(own, marks, beside):
    reverse = marks is not None
    way = -1 if reverse else 1
    got = exchange(own)
    if not reverse:
        marks = got
    joined, rest = call(
        functools.partial(gather_kernel, reverse),
        [like(own.shape[1:]), like((8, LANES))],
        got,
        marks,
    )
    from_next = moved(joined, way)
    beside = beside()
    if reverse:
        rest = rest + swapped(rest, 4)
    from_next, rest, beside = lax.optimization_barrier((from_next, rest, beside))
    twice = call(join_kernel, like(own.shape[1:]), joined, from_next)
    near, far = moved(twice, way), moved(twice, 3 * way)
    if reverse:
        rest = rest + swapped(rest, 2)
    handed = call(
        functools.partial(hand_kernel, reverse),
        like((GROUP, STATE, LANES)),
        near,
        far,
        got,
        marks,
    )
    return (exchange(handed), marks, rest, beside)


def per_device(
    inputs_x,
    gate_z,
    input_b,
    input_c,
    dt_raw,
    a_log,
    dt_bias,
    skip_d,
    norm_gain,
    lengths,
    cotangent,
):
    rows, width = inputs_x.shape
    heads = dt_raw.shape[1]
    docs = lengths.shape[0]
    member = lax.axis_index(("zl", "x"))
    group = lax.axis_index("zh")
    total = rows * lax.axis_size("zh") * GROUP
    channels = float(width * lax.axis_size("tensor"))
    first = (group * GROUP + member) * rows
    info = jnp.concatenate(
        [lengths, jnp.stack([first, jnp.int32(total - STRETCH)]).astype(jnp.int32)]
    )
    steps = dt_raw.T
    a_log, dt_bias = a_log[:, None], dt_bias[:, None]
    skip_d, gain = skip_d[None, :], norm_gain[None, :]
    message = like((GROUP, STATE + 8, LANES))
    wide = like((rows, width))
    small = like((rows, heads))
    turned = like((heads, rows))

    own, summed, deltas = call(
        functools.partial(states_kernel, docs),
        [message, small, small],
        info,
        inputs_x,
        input_b,
        steps,
        a_log,
        dt_bias,
        smem=True,
    )

    def before():
        return call(
            functools.partial(within_kernel, docs),
            [wide, wide, wide, wide],
            info,
            inputs_x,
            gate_z,
            cotangent,
            input_b,
            input_c,
            summed,
            deltas,
            skip_d,
            smem=True,
        )

    entering, marks, _, (within, fresh, gate, gated) = carry(own, None, before)
    core, bent, sums = call(
        output_kernel,
        [wide, wide, like((2, rows))],
        within,
        fresh,
        gate,
        gated,
        input_c,
        gain,
        entering,
    )
    sums = lax.all_gather(sums, "tensor")
    pulled, own_back = call(
        functools.partial(pull_kernel, channels),
        [wide, message],
        core,
        bent,
        gated,
        fresh,
        input_c,
        gain,
        sums,
    )

    def after():
        return call(
            functools.partial(inner_kernel, docs),
            [
                wide,
                wide,
                like((STATE, width)),
                like((rows, STATE)),
                like((rows, STATE), BF16),
                turned,
                turned,
            ],
            info,
            inputs_x,
            input_b,
            input_c,
            summed,
            deltas,
            skip_d,
            core,
            pulled,
            fresh,
            entering,
            own,
            smem=True,
        )

    later, _, gain_sum, beside = carry(own_back, marks, after)
    base, weights, leaving, b_part, grad_c, along, back = beside
    grad_x, grad_b, grad_dt = call(
        final_kernel,
        [like((rows, width), BF16), like((rows, STATE), BF16), turned],
        inputs_x,
        input_b,
        steps,
        a_log,
        dt_bias,
        base,
        weights,
        leaving,
        b_part,
        along,
        back,
        later,
    )
    gain_sum = gain_sum + swapped(gain_sum, 1)
    share = width // (GROUP * lax.axis_size("zh"))
    grad_gain = lax.dynamic_slice(gain_sum, (group, member * share), (1, share))[0]
    return (grad_x, grad_b, grad_c, grad_dt.T, grad_gain)


def solution(mesh):
    count, across = mesh.devices.shape
    split_mesh = Mesh(
        mesh.devices.reshape(count // GROUP, 2, GROUP // 2, across), ("zh", "zl", "x", "tensor")
    )
    tokens = ("zh", "zl", "x")
    both = P(tokens, "tensor")
    alone = P("tensor")
    return jax.shard_map(
        per_device,
        mesh=split_mesh,
        in_specs=(both, both, both, both, both, alone, alone, alone, alone, P(), both),
        out_specs=(both, both, both, both, P(("tensor", "zh", "zl", "x"))),
        check_vma=False,
    )
```

time: 885 us -> 155 us (0.18)
  the two profiles are of different devices: /device:TPU:1 before, /device:TPU:2 now
where the time goes in v2:
time: 155 us; the launch traced here: 154 us
  starting transfers between devices  57.2 us (37%)
  blocking collectives  52.9 us (34%)
  waiting for transfers between devices  23.1 us (15%)
  Pallas kernels  14.6 us (9%)
  local copies, waits for them, and re-layouts  5.62 us (4%)
    all_to_all x3, blocking collectives, exchange(): return lax.all_to_all(value, ('zl', 'x'), 0, 0, tiled=True)  40.8 us
    ppermute x3, starting transfers between devices, swapped(): return lax.ppermute(value, 'zh', [(i, i ^ bit) for i in range(count)])  27.6 us
    ppermute x6, starting transfers between devices, moved(): return lax.ppermute(value, 'zh', pairs) if pairs else jnp.zeros_like(value)  25.3 us
    ppermute x6, waiting for transfers between devices, moved(): return lax.ppermute(value, 'zh', pairs) if pairs else jnp.zeros_like(value)  18.4 us
    pallas_call x12, Pallas kernels, call(): pl.pallas_call(kernel, out_shape=outs, in_specs=in_specs, out_specs=[spec...  14.6 us
    all_gather x1, blocking collectives, per_device(): sums = lax.all_gather(sums, 'tensor')  12.1 us
    unnamed x30, local copies, waits for them, and re-layouts  4.87 us
    ppermute x3, waiting for transfers between devices, swapped(): return lax.ppermute(value, 'zh', [(i, i ^ bit) for i in range(count)])  4.7 us
  transfers between devices with their start and end apart: 10, of which 4 were waited for; matrix products, arithmetic and copies ran while one was open for 0% of the time, Pallas kernels for 5%

profile of v2, /device:TPU:2, one launch (start us, length us, event | category | flops | bytes accessed | tf_op | source)
XLA Modules:
  0.0 154.4 jit_solution(11689901982029236827)
XLA Ops:
  0.6 0.0 copy-start.12
  0.6 0.0 copy-start.13
  0.7 0.6 copy-done.12
  1.3 0.0 copy-start.9
  1.3 0.1 copy.22.alog_ref
  1.4 0.0 copy-done.13
  1.4 0.1 copy.23.bias_ref
  1.5 0.0 copy-start.14
  1.5 0.7 copy-done.14
  2.1 0.1 pad_add_fusion.info_ref
  2.2 0.0 copy-done.9
  2.2 0.0 copy-start
  2.2 1.0 copy-done
  3.2 0.0 copy-start.3
  3.2 0.8 copy-done.3
  4.1 2.0 %shard_map.146 = (f32[8,136,128]{2,1,0:T(8,128)S(1)}, f32[256,16]{1,0:T(8,128)S(1)}, f32[256,16]{1,0:T(8,128)S(1)}) custom-call(s32[18]{0:T(128)S(1)} %pad_add_fusion.info_ref, bf16[256,1024]{1,0:T(8,128)(2,1)S(1)} %copy-done, bf16[256,128]{1,0:T(8,128)(2,1)S(1)} %copy-done.3, f32[16,256]{1,0:T(8,128)S(1)} %bitcast.10, f32[16,1]{1,0:T(8,128)S(1)} %copy.22.alog_ref, ...), custom_call_target="tpu_custom_call" | custom-call | tf_op jit(solution)/shard_map/pallas_call | solution.py:402
  6.1 0.0 copy-start.6
  6.1 16.0 %all_to_all.20.got_ref.marks_ref = f32[8,136,128]{2,1,0:T(8,128)S(1)} all-to-all(f32[8,136,128]{2,1,0:T(8,128)S(1)} %get-tuple-element.44.own_ref), channel_id=1, replica_groups=mesh['zh'=8,'zl'=2,'x'=4,'tensor'=8] {'zl','x'}, dimensions={0} | all-to-all | bytes 1114112 | tf_op jit(solution)/shard_map/all_to_all | solution.py:416
  22.1 0.0 copy-start.2
  22.1 0.0 copy-start.5
  22.2 0.6 shard_map.147
  22.8 4.5 %collective-permute-start = (f32[136,128]{1,0:T(8,128)S(1)}, f32[136,128]{1,0:T(8,128)S(1)}, u32[]{:S(2)}, u32[]{:S(2)}) collective-permute-start(f32[136,128]{1,0:T(8,128)S(1)} %get-tuple-element.45.own_ref), channel_id=1, source_target_pairs={{0,64},{64,128},{128,192},{192,256},{256,320},{320,384},{384,448},... | collective-permute-start | bytes 208904 | tf_op jit(solution)/shard_map/ppermute | solution.py:422
  27.3 0.0 copy-start.11
  27.3 0.0 copy-done.6
  27.3 0.0 copy-done.2
  27.3 0.0 copy-done.4
  27.3 0.0 copy-done.5
  27.3 0.6 copy-done.11
  27.9 2.9 %shard_map.148 = (f32[256,1024]{1,0:T(8,128)S(1)}, f32[256,1024]{1,0:T(8,128)S(1)}, f32[256,1024]{1,0:T(8,128)S(1)}, f32[256,1024]{1,0:T(8,128)S(1)}) custom-call(s32[18]{0:T(128)S(1)} %pad_add_fusion.info_ref, bf16[256,1024]{1,0:T(8,128)(2,1)S(1)} %copy-done, bf16[256,1024]{1,0:T(8,128)(2,1)S(1)} %copy-done.5, bf16[256,1024]{1,0:T(8,128)(2,1)S(1)} %copy-done.6, ...), custom_call_target="tpu_custom_call" | custom-call | tf_op jit(solution)/shard_map/pallas_call | solution.py:402
  30.8 0.0 collective-permute-done.got_ref
  30.8 12.1 %collective-permute-start.2 = (f32[136,128]{1,0:T(8,128)S(1)}, f32[136,128]{1,0:T(8,128)S(1)}, u32[]{:S(2)}, u32[]{:S(2)}) collective-permute-start(f32[136,128]{1,0:T(8,128)S(1)} %shard_map.149), channel_id=1, source_target_pairs={{0,192},{64,256},{128,320},{192,384},{256,448},{1,193},{65,257},{1... | collective-permute-start | bytes 208904 | tf_op jit(solution)/shard_map/ppermute | solution.py:422
  43.0 4.7 %collective-permute-start.1 = (f32[136,128]{1,0:T(8,128)S(1)}, f32[136,128]{1,0:T(8,128)S(1)}, u32[]{:S(2)}, u32[]{:S(2)}) collective-permute-start(f32[136,128]{1,0:T(8,128)S(1)} %shard_map.149), channel_id=1, source_target_pairs={{0,64},{64,128},{128,192},{192,256},{256,320},{320,384},{384,448},... | collective-permute-start | bytes 208904 | tf_op jit(solution)/shard_map/ppermute | solution.py:422
  47.7 0.0 collective-permute-done.2.far_ref
  47.7 1.9 %collective-permute-done.1.near_ref = f32[136,128]{1,0:T(8,128)S(1)} collective-permute-done((f32[136,128]{1,0:T(8,128)S(1)}, f32[136,128]{1,0:T(8,128)S(1)}, u32[]{:S(2)}, u32[]{:S(2)}) %collective-permute-start.1) | collective-permute-done | bytes 69664 | tf_op jit(solution)/shard_map/ppermute | solution.py:422
  49.7 0.0 copy-start.10
  49.7 10.7 %all_to_all.21.entering_ref = f32[8,128,128]{2,1,0:T(8,128)S(1)} all-to-all(f32[8,128,128]{2,1,0:T(8,128)S(1)} %shard_map.150), channel_id=1, replica_groups=mesh['zh'=8,'zl'=2,'x'=4,'tensor'=8] {'zl','x'}, dimensions={0} | all-to-all | bytes 1048576 | tf_op jit(solution)/shard_map/all_to_all | solution.py:416
  60.4 0.0 copy-done.10
  60.4 0.9 shard_map.151
  61.3 12.1 %all-gather.1.sums_ref = f32[8,2,256]{2,1,0:T(2,128)S(1)} all-gather(f32[1,2,256]{2,1,0:T(2,128)S(1)} %bitcast.16), channel_id=2, replica_groups=mesh['zh'=8,'zl'=2,'x'=4,'tensor'=8] {'tensor'}, dimensions={0}, use_global_device_ids=true | all-gather | bytes 18432 | tf_op jit(solution)/shard_map/all_gather | solution.py:536
  73.4 0.7 shard_map.152
  74.1 14.1 %all_to_all.22.got_ref = f32[8,136,128]{2,1,0:T(8,128)S(1)} all-to-all(f32[8,136,128]{2,1,0:T(8,128)S(1)} %get-tuple-element.60), channel_id=1, replica_groups=mesh['zh'=8,'zl'=2,'x'=4,'tensor'=8] {'zl','x'}, dimensions={0} | all-to-all | bytes 1114112 | tf_op jit(solution)/shard_map/all_to_all | solution.py:416
  88.3 1.4 collective-permute-start.3
  89.7 16.6 %collective-permute-start.4 = (f32[8,128]{1,0:T(8,128)S(1)}, f32[8,128]{1,0:T(8,128)S(1)}, u32[]{:S(2)}, u32[]{:S(2)}) collective-permute-start(f32[8,128]{1,0:T(8,128)S(1)} %get-tuple-element.62), channel_id=1, source_target_pairs={{0,256},{64,320},{128,384},{192,448},{256,0},{320,64},{384,128},{4... | collective-permute-start | bytes 12296 | tf_op jit(solution)/shard_map/ppermute | solution.py:429
  106.3 0.0 copy-done.1
  106.3 4.3 %shard_map.154 = (f32[256,1024]{1,0:T(8,128)S(1)}, f32[256,1024]{1,0:T(8,128)S(1)}, f32[128,1024]{1,0:T(8,128)S(1)}, f32[256,128]{1,0:T(8,128)S(1)}, bf16[256,12...) custom-call(s32[18]{0:T(128)S(1)} %pad_add_fusion.info_ref, bf16[256,1024]{1,0:T(8,128)(2,1)S(1)} %copy-done.1, ...), custom_call_target="tpu_custom_call" | custom-call | tf_op jit(solution)/shard_map/pallas_call | solution.py:402
  110.6 0.0 copy-start.7
  110.6 0.0 collective-permute-done.4
  110.6 0.0 collective-permute-done.3.got_ref
  110.7 1.3 collective-permute-start.6
  112.0 1.3 collective-permute-start.5
  113.3 16.5 %collective-permute-done.6.far_ref = f32[136,128]{1,0:T(8,128)S(1)} collective-permute-done((f32[136,128]{1,0:T(8,128)S(1)}, f32[136,128]{1,0:T(8,128)S(1)}, u32[]{:S(2)}, u32[]{:S(2)}) %collective-permute-start.6) | collective-permute-done | bytes 69664 | tf_op jit(solution)/shard_map/ppermute | solution.py:422
  129.8 0.0 collective-permute-done.5.near_ref
  129.8 0.8 shard_map.156
  130.6 0.0 copy-done.7
  130.6 4.2 %all-to-all-start.3 = ((f32[8,128,128]{2,1,0:T(8,128)}), f32[8,128,128]{2,1,0:T(8,128)S(1)}, u32[]{:S(2)}, u32[]{:S(2)}) async-start(f32[8,128,128]{2,1,0:T(8,128)} %shard_map.156), calls=%async_computation.3 | async-start | bytes 1048576 | tf_op jit(solution)/shard_map/all_to_all | solution.py:416
  134.8 6.8 %collective-permute-start.7 = (f32[8,128]{1,0:T(8,128)S(1)}, f32[8,128]{1,0:T(8,128)S(1)}, u32[]{:S(2)}, u32[]{:S(2)}) collective-permute-start(f32[8,128]{1,0:T(8,128)S(1)} %add.23), channel_id=1, source_target_pairs={{0,128},{64,192},{128,0},{192,64},{256,384},{320,448},{384,256},{4... | collective-permute-start | bytes 12296 | tf_op jit(solution)/shard_map/ppermute | solution.py:429
  141.7 2.6 %collective-permute-done.7 = f32[8,128]{1,0:T(8,128)S(1)} collective-permute-done((f32[8,128]{1,0:T(8,128)S(1)}, f32[8,128]{1,0:T(8,128)S(1)}, u32[]{:S(2)}, u32[]{:S(2)}) %collective-permute-start.7) | collective-permute-done | bytes 4128 | tf_op jit(solution)/shard_map/ppermute | solution.py:429
  144.2 4.2 %collective-permute-start.8 = (f32[8,128]{1,0:T(8,128)S(1)}, f32[8,128]{1,0:T(8,128)S(1)}, u32[]{:S(2)}, u32[]{:S(2)}) collective-permute-start(f32[8,128]{1,0:T(8,128)S(1)} %add.24), channel_id=1, source_target_pairs={{0,64},{64,0},{128,192},{192,128},{256,320},{320,256},{384,448},{4... | collective-permute-start | bytes 12296 | tf_op jit(solution)/shard_map/ppermute | solution.py:429
  148.5 2.1 %collective-permute-done.8 = f32[8,128]{1,0:T(8,128)S(1)} collective-permute-done((f32[8,128]{1,0:T(8,128)S(1)}, f32[8,128]{1,0:T(8,128)S(1)}, u32[]{:S(2)}, u32[]{:S(2)}) %collective-permute-start.8) | collective-permute-done | bytes 4128 | tf_op jit(solution)/shard_map/ppermute | solution.py:429
  150.6 0.6 dynamic-slice_bitcast_fusion
  151.2 0.0 all-to-all-done.3.later_ref
  151.2 0.0 copy-start.8
  151.2 1.0 copy-done.8
  152.2 2.2 %shard_map.157 = (bf16[256,1024]{1,0:T(8,128)(2,1)}, bf16[256,128]{1,0:T(8,128)(2,1)}, f32[16,256]{1,0:T(8,128)}) custom-call(bf16[256,1024]{1,0:T(8,128)(2,1)S(1)} %copy-done.1, bf16[256,128]{1,0:T(8,128)(2,1)S(1)} %copy-done.4, f32[16,256]{1,0:T(8,128)S(1)} %bitcast.11, f32[16,1]{1,0:T(8,128)S(1)} %copy.22.alog_ref, f32[16,1]{1,0:T(8,128)S(1)} %copy.23.bias_ref, ...), custom_call_target="tpu_custom_call" | custom-call | tf_op jit(solution)/shard_map/pallas_call | solution.py:402
  (9 shorter events, 0.1 us)
Async XLA Ops:
  0.6 0.7 copy-start.12
  0.6 0.7 copy-start.13
  1.3 0.9 copy-start.9
  1.5 0.7 copy-start.14
  2.2 1.0 copy-start
  3.2 0.8 copy-start.3
  6.1 21.2 %copy-start.6 = (bf16[256,1024]{1,0:T(8,128)(2,1)S(1)}, bf16[256,1024]{1,0:T(8,128)(2,1)}, u32[]{:S(2)}) copy-start(bf16[256,1024]{1,0:T(8,128)(2,1)} %cot_ref.1) | copy-start | bytes 1572868
  22.1 5.1 %copy-start.2 = (bf16[256,128]{1,0:T(8,128)(2,1)S(1)}, bf16[256,128]{1,0:T(8,128)(2,1)}, u32[]{:S(2)}) copy-start(bf16[256,128]{1,0:T(8,128)(2,1)} %c_ref.7) | copy-start | bytes 196612
  22.1 5.1 %copy-start.4 = (bf16[256,128]{1,0:T(8,128)(2,1)S(1)}, bf16[256,128]{1,0:T(8,128)(2,1)}, u32[]{:S(2)}) copy-start(bf16[256,128]{1,0:T(8,128)(2,1)} %b_ref.7) | copy-start | bytes 196612
  22.1 5.1 %copy-start.5 = (bf16[256,1024]{1,0:T(8,128)(2,1)S(1)}, bf16[256,1024]{1,0:T(8,128)(2,1)}, u32[]{:S(2)}) copy-start(bf16[256,1024]{1,0:T(8,128)(2,1)} %z_ref.1) | copy-start | bytes 1572868
  22.8 8.0 %collective-permute-start = (f32[136,128]{1,0:T(8,128)S(1)}, f32[136,128]{1,0:T(8,128)S(1)}, u32[]{:S(2)}, u32[]{:S(2)}) collective-permute-start(f32[136,128]{1,0:T(8,128)S(1)} %get-tuple-element.45.own_ref), channel_id=1, source_target_pairs={{0,64},{64,128},{128,192},{192,256},{256,320},{320,384},{384,448},... | collective-permute-start | bytes 208904 | tf_op jit(solution)/shard_map/ppermute | solution.py:422
  27.3 0.7 copy-start.11
  30.8 16.9 %collective-permute-start.2 = (f32[136,128]{1,0:T(8,128)S(1)}, f32[136,128]{1,0:T(8,128)S(1)}, u32[]{:S(2)}, u32[]{:S(2)}) collective-permute-start(f32[136,128]{1,0:T(8,128)S(1)} %shard_map.149), channel_id=1, source_target_pairs={{0,192},{64,256},{128,320},{192,384},{256,448},{1,193},{65,257},{1... | collective-permute-start | bytes 208904 | tf_op jit(solution)/shard_map/ppermute | solution.py:422
  43.0 6.7 %collective-permute-start.1 = (f32[136,128]{1,0:T(8,128)S(1)}, f32[136,128]{1,0:T(8,128)S(1)}, u32[]{:S(2)}, u32[]{:S(2)}) collective-permute-start(f32[136,128]{1,0:T(8,128)S(1)} %shard_map.149), channel_id=1, source_target_pairs={{0,64},{64,128},{128,192},{192,256},{256,320},{320,384},{384,448},... | collective-permute-start | bytes 208904 | tf_op jit(solution)/shard_map/ppermute | solution.py:422
  49.7 10.7 %copy-start.10 = (f32[1024]{0:T(1024)S(1)}, f32[1024]{0:T(1024)}, u32[]{:S(2)}) copy-start(f32[1024]{0:T(1024)} %param.19) | copy-start | bytes 12292
  88.3 18.1 %copy-start.1 = (bf16[256,1024]{1,0:T(8,128)(2,1)S(1)}, bf16[256,1024]{1,0:T(8,128)(2,1)}, u32[]{:S(2)}) copy-start(bf16[256,1024]{1,0:T(8,128)(2,1)} %x_ref.7) | copy-start | bytes 1572868
  88.3 22.3 %collective-permute-start.3 = (f32[136,128]{1,0:T(8,128)S(1)}, f32[136,128]{1,0:T(8,128)S(1)}, u32[]{:S(2)}, u32[]{:S(2)}) collective-permute-start(f32[136,128]{1,0:T(8,128)S(1)} %get-tuple-element.61.own_ref), channel_id=1, source_target_pairs={{64,0},{128,64},{192,128},{256,192},{320,256},{384,320},{448,384},... | collective-permute-start | bytes 208904 | tf_op jit(solution)/shard_map/ppermute | solution.py:422
  89.7 20.9 %collective-permute-start.4 = (f32[8,128]{1,0:T(8,128)S(1)}, f32[8,128]{1,0:T(8,128)S(1)}, u32[]{:S(2)}, u32[]{:S(2)}) collective-permute-start(f32[8,128]{1,0:T(8,128)S(1)} %get-tuple-element.62), channel_id=1, source_target_pairs={{0,256},{64,320},{128,384},{192,448},{256,0},{320,64},{384,128},{4... | collective-permute-start | bytes 12296 | tf_op jit(solution)/shard_map/ppermute | solution.py:429
  110.6 20.0 %copy-start.7 = (f32[128,1024]{1,0:T(8,128)}, f32[128,1024]{1,0:T(8,128)S(1)}, u32[]{:S(2)}) copy-start(f32[128,1024]{1,0:T(8,128)S(1)} %get-tuple-element.73.leaving_ref) | copy-start | bytes 1572868
  110.7 19.1 %collective-permute-start.6 = (f32[136,128]{1,0:T(8,128)S(1)}, f32[136,128]{1,0:T(8,128)S(1)}, u32[]{:S(2)}, u32[]{:S(2)}) collective-permute-start(f32[136,128]{1,0:T(8,128)S(1)} %shard_map.155), channel_id=1, source_target_pairs={{192,0},{256,64},{320,128},{384,192},{448,256},{193,1},{257,65},{3... | collective-permute-start | bytes 208904 | tf_op jit(solution)/shard_map/ppermute | solution.py:422
  112.0 17.8 %collective-permute-start.5 = (f32[136,128]{1,0:T(8,128)S(1)}, f32[136,128]{1,0:T(8,128)S(1)}, u32[]{:S(2)}, u32[]{:S(2)}) collective-permute-start(f32[136,128]{1,0:T(8,128)S(1)} %shard_map.155), channel_id=1, source_target_pairs={{64,0},{128,64},{192,128},{256,192},{320,256},{384,320},{448,384},... | collective-permute-start | bytes 208904 | tf_op jit(solution)/shard_map/ppermute | solution.py:422
  130.6 20.6 %all-to-all-start.3 = ((f32[8,128,128]{2,1,0:T(8,128)}), f32[8,128,128]{2,1,0:T(8,128)S(1)}, u32[]{:S(2)}, u32[]{:S(2)}) async-start(f32[8,128,128]{2,1,0:T(8,128)} %shard_map.156), calls=%async_computation.3 | async-start | bytes 1048576 | tf_op jit(solution)/shard_map/all_to_all | solution.py:416
  134.8 9.4 %collective-permute-start.7 = (f32[8,128]{1,0:T(8,128)S(1)}, f32[8,128]{1,0:T(8,128)S(1)}, u32[]{:S(2)}, u32[]{:S(2)}) collective-permute-start(f32[8,128]{1,0:T(8,128)S(1)} %add.23), channel_id=1, source_target_pairs={{0,128},{64,192},{128,0},{192,64},{256,384},{320,448},{384,256},{4... | collective-permute-start | bytes 12296 | tf_op jit(solution)/shard_map/ppermute | solution.py:429
  144.2 6.4 %collective-permute-start.8 = (f32[8,128]{1,0:T(8,128)S(1)}, f32[8,128]{1,0:T(8,128)S(1)}, u32[]{:S(2)}, u32[]{:S(2)}) collective-permute-start(f32[8,128]{1,0:T(8,128)S(1)} %add.24), channel_id=1, source_target_pairs={{0,64},{64,0},{128,192},{192,128},{256,320},{320,256},{384,448},{4... | collective-permute-start | bytes 12296 | tf_op jit(solution)/shard_map/ppermute | solution.py:429
  151.2 1.0 copy-start.8

commit v3 on v2

--- a/solution.py
+++ b/solution.py
@@ -82,16 +82,22 @@
     return (at, of)
 
 
-def place_marks(info_ref, docs, rows, axis):
+def member_index():
+    return lax.axis_index("zl") * lax.axis_size("x") + lax.axis_index("x")
+
+
+def place_marks(lengths_ref, rows, axis):
     shape = (rows, 1) if axis == 0 else (1, rows)
-    first, live_end = info_ref[docs], info_ref[docs + 1]
+    docs = lengths_ref.shape[0]
+    first = (lax.axis_index("zh") * GROUP + member_index()) * rows
+    live_end = rows * GROUP * lax.axis_size("zh") - STRETCH
     places = first + lax.broadcasted_iota(jnp.int32, shape, axis)
     resets = jnp.maximum(places - live_end + 1, 0)
     start = jnp.int32(0)
     for doc in range(docs):
         inside = jnp.where(start >= first, 1, 0)
         resets = resets + jnp.where(places >= start, inside, 0)
-        start = start + info_ref[doc]
+        start = start + lengths_ref[doc]
     return (places < live_end, resets)
 
 
@@ -103,16 +109,45 @@
     return 1.0 / (1.0 + jnp.exp(-value))
 
 
+def column(row):
+    at, of = ordered(row.shape[1])
+    return jnp.sum(jnp.where(at == of, row, 0.0), axis=1, keepdims=True)
+
+
 def states_kernel(
-    docs, info_ref, x_ref, b_ref, dt_ref, alog_ref, bias_ref, out_ref, summed_ref, deltas_ref
+    lengths_ref,
+    x_hbm,
+    b_hbm,
+    dt_hbm,
+    alog_hbm,
+    bias_hbm,
+    out_ref,
+    summed_ref,
+    deltas_ref,
+    x_ref,
+    b_ref,
+    dt_ref,
+    alog_ref,
+    bias_ref,
+    sems,
 ):
+    sources = (alog_hbm, bias_hbm, dt_hbm, b_hbm, x_hbm)
+    targets = (alog_ref, bias_ref, dt_ref, b_ref, x_ref)
+    copies = [
+        pltpu.make_async_copy(source, target, sems.at[one])
+        for one, (source, target) in enumerate(zip(sources, targets))
+    ]
+    for copy in copies:
+        copy.start()
     rows = x_ref.shape[0]
     pairs = x_ref.shape[1] // WIDE
-    _, resets = place_marks(info_ref, docs, rows, 0)
+    _, resets = place_marks(lengths_ref, rows, 0)
     at, of = ordered(rows)
-    deltas_row = softplus(dt_ref[...] + bias_ref[...])
     before = jnp.where(at <= of, 1.0, 0.0).astype(BF16)
-    summed = mul_3x(-jnp.exp(alog_ref[...]) * deltas_row, before).T
+    for copy in copies[:3]:
+        copy.wait()
+    deltas_row = softplus(dt_ref[...] + column(bias_ref[...]))
+    summed = mul_3x(-jnp.exp(column(alog_ref[...])) * deltas_row, before).T
     deltas = deltas_row.T
     summed_ref[...] = summed
     deltas_ref[...] = deltas
@@ -120,7 +155,9 @@
     last = resets[rows - 1 : rows, :]
     weights = jnp.where(resets == last, jnp.exp(ending - summed), 0.0) * deltas
     through = jnp.broadcast_to(jnp.where(last == 0, jnp.exp(ending), 0.0), (8, deltas.shape[1]))
+    copies[3].wait()
     b_turned = b_ref[...].astype(F32).T.astype(BF16)
+    copies[4].wait()
     for pair in range(pairs):
         weighted = x_ref[:, cols(pair)].astype(F32) * spread(weights, pair)
         state = mul_xs(b_turned, split(weighted))
@@ -132,8 +169,7 @@
 
 
 def within_kernel(
-    docs,
-    info_ref,
+    lengths_ref,
     x_ref,
     z_ref,
     cot_ref,
@@ -149,8 +185,8 @@
 ):
     rows = x_ref.shape[0]
     pairs = x_ref.shape[1] // WIDE
-    living, resets = place_marks(info_ref, docs, rows, 0)
-    _, resets_row = place_marks(info_ref, docs, rows, 1)
+    living, resets = place_marks(lengths_ref, rows, 0)
+    _, resets_row = place_marks(lengths_ref, rows, 1)
     deltas, summed = deltas_ref[...], summed_ref[...]
     middle = summed[rows // 2 - 1 : rows // 2, :]
     rising = jnp.exp(summed - middle)
@@ -203,7 +239,10 @@
         high, low = split(total)
         rest = (total - high.astype(F32) - low.astype(F32)).astype(BF16)
         sum_row = mul(ones, high, NT) + (mul(ones, low, NT) + mul(ones, rest, NT))
-        sums_ref[row : row + 1, :] = sum_row[0:1]
+        for half in range(2):
+            line = 2 * row + half
+            for to in range(sums_ref.shape[0]):
+                sums_ref[to, line : line + 1, :] = sum_row[0:1, half * LANES : (half + 1) * LANES]
 
 
 def pull_kernel(
@@ -222,11 +261,12 @@
     sums = sums_ref[0]
     for other in range(1, sums_ref.shape[0]):
         sums = sums + sums_ref[other]
-    scaling_row = lax.rsqrt(sums[0:1] / channels + EPSILON)
-    second_row = scaling_row * scaling_row * scaling_row * sums[1:2] / channels
-    at, of = ordered(rows)
-    scaling = jnp.sum(jnp.where(at == of, scaling_row, 0.0), axis=1, keepdims=True)
-    second = jnp.sum(jnp.where(at == of, second_row, 0.0), axis=1, keepdims=True)
+    squares = jnp.concatenate([sums[0:1], sums[1:2]], axis=1)
+    products = jnp.concatenate([sums[2:3], sums[3:4]], axis=1)
+    scaling_row = lax.rsqrt(squares / channels + EPSILON)
+    second_row = scaling_row * scaling_row * scaling_row * products / channels
+    scaling = column(scaling_row)
+    second = column(second_row)
     c_turned = c_ref[...].astype(F32).T.astype(BF16)
     gains = []
     for pair in range(width // WIDE):
@@ -244,8 +284,7 @@
 
 
 def inner_kernel(
-    docs,
-    info_ref,
+    lengths_ref,
     x_ref,
     b_ref,
     c_ref,
@@ -267,8 +306,8 @@
 ):
     rows = x_ref.shape[0]
     pairs = x_ref.shape[1] // WIDE
-    _, resets = place_marks(info_ref, docs, rows, 0)
-    _, resets_row = place_marks(info_ref, docs, rows, 1)
+    _, resets = place_marks(lengths_ref, rows, 0)
+    _, resets_row = place_marks(lengths_ref, rows, 1)
     deltas, summed = deltas_ref[...], summed_ref[...]
     heads = deltas.shape[1]
     middle = summed[rows // 2 - 1 : rows // 2, :]
@@ -351,50 +390,78 @@
     at, of = ordered(rows)
     after = jnp.where(at >= of, 1.0, 0.0).astype(BF16)
     log_pull = mul_3x(along_ref[...] - back, after) + ends[:, 0:1]
-    raw = dt_ref[...] + bias_ref[...]
+    raw = dt_ref[...] + column(bias_ref[...])
     direct = back / softplus(raw)
-    dt_out_ref[...] = (direct - jnp.exp(alog_ref[...]) * log_pull) * sigmoid(raw)
-
-
-def gather_kernel(reverse, got_ref, marks_ref, out_ref, rest_ref):
+    dt_out_ref[...] = (direct - jnp.exp(column(alog_ref[...])) * log_pull) * sigmoid(raw)
+
+
+def gather_kernel(reverse, got_ref, marks_ref, out_ref, *gain_ref):
     order = list(range(GROUP))
     if reverse:
         order.reverse()
     joined = got_ref[order[0], 0:STATE, :]
-    rest = got_ref[0, STATE : STATE + 8, :]
     marks = marks_ref[0, STATE : STATE + 8, :]
     for one in order[1:]:
         joined = marks_ref[one, STATE : STATE + 1, :] * joined + got_ref[one, 0:STATE, :]
     for one in range(1, GROUP):
-        rest = rest + got_ref[one, STATE : STATE + 8, :]
         marks = marks * marks_ref[one, STATE : STATE + 8, :]
+    end = out_ref.shape[0] - 8
     out_ref[0:STATE, :] = joined
-    out_ref[STATE : STATE + 8, :] = marks
-    rest_ref[...] = rest
-
-
-def join_kernel(own_ref, got_ref, out_ref):
-    through = own_ref[STATE : STATE + 1, :]
-    out_ref[0:STATE, :] = own_ref[0:STATE, :] + through * got_ref[0:STATE, :]
-    out_ref[STATE : STATE + 8, :] = (
-        own_ref[STATE : STATE + 8, :] * got_ref[STATE : STATE + 8, :]
-    )
-
-
-def hand_kernel(reverse, near_ref, far_ref, got_ref, marks_ref, out_ref):
+    out_ref[end : end + 8, :] = marks
+    if reverse:
+        gain = got_ref[0, STATE : STATE + 8, :]
+        for one in range(1, GROUP):
+            gain = gain + got_ref[one, STATE : STATE + 8, :]
+        out_ref[STATE : STATE + 8, :] = gain
+        gain_ref[0][...] = gain
+
+
+def join_kernel(reverse, own_ref, got_ref, *refs):
+    end = own_ref.shape[0] - 8
+    through = own_ref[end : end + 1, :]
+    joined = own_ref[0:STATE, :] + through * got_ref[0:STATE, :]
+    if reverse:
+        gain_ref, gain_got_ref, out_ref, far_ref, gain_out_ref = refs
+        both = own_ref[STATE : STATE + 8, :] + got_ref[STATE : STATE + 8, :]
+        out_ref[STATE : STATE + 8, :] = both
+        far_ref[STATE : STATE + 8, :] = both
+        gain_out_ref[...] = gain_ref[...] + gain_got_ref[...]
+    else:
+        out_ref, far_ref = refs
+    out_ref[0:STATE, :] = joined
+    far_ref[0:STATE, :] = joined
+    out_ref[end : end + 8, :] = own_ref[end : end + 8, :] * got_ref[end : end + 8, :]
+
+
+def hand_kernel(reverse, near_ref, far_ref, got_ref, marks_ref, *refs):
     order = list(range(GROUP))
+    out_ref = refs[-2] if reverse else refs[-1]
+    end = near_ref.shape[0] - 8
+    holding = near_ref[0:STATE, :] + near_ref[end : end + 1, :] * far_ref[0:STATE, :]
     if reverse:
         order.reverse()
-    holding = near_ref[0:STATE, :] + near_ref[STATE : STATE + 1, :] * far_ref[0:STATE, :]
+        group = lax.axis_index("zh")
+        holding = jnp.where(group == lax.axis_size("zh") - 1, 0.0, holding)
     for one in order:
         out_ref[one] = holding
         if one != order[-1]:
             through = marks_ref[one, STATE : STATE + 1, :]
             holding = through * holding + got_ref[one, 0:STATE, :]
-
-
-def call(kernel, outs, *operands, smem=False):
-    in_specs = [pl.BlockSpec(memory_space=pltpu.VMEM) for _ in operands]
+    if reverse:
+        table = refs[0][...] + refs[1][...]
+        table = table + near_ref[STATE : STATE + 8, :] + far_ref[STATE : STATE + 8, :]
+        row = lax.broadcasted_iota(jnp.int32, table.shape, 0)
+        table = jnp.where(row == group, table, 0.0)
+        gain_ref = refs[-1]
+        share = gain_ref.shape[1]
+        lane = lax.broadcasted_iota(jnp.int32, (LANES, share), 0)
+        place = lax.broadcasted_iota(jnp.int32, (LANES, share), 1)
+        chosen = jnp.where(lane == place + share * member_index(), 1.0, 0.0).astype(BF16)
+        gain_ref[...] = jnp.sum(mul_3x(table, chosen), axis=0, keepdims=True)
+
+
+def call(kernel, outs, *operands, smem=False, hbm=False, scratch=()):
+    in_specs = [pl.BlockSpec(memory_space=pltpu.HBM if hbm else pltpu.VMEM) for _ in operands]
     if smem:
         in_specs[0] = pl.BlockSpec(memory_space=pltpu.SMEM)
     many = isinstance(outs, (list, tuple))
@@ -404,7 +471,8 @@
         out_shape=outs,
         in_specs=in_specs,
         out_specs=[spec] * len(outs) if many else spec,
-        compiler_params=pltpu.CompilerParams(vmem_limit_bytes=32 * 1024 * 1024),
+        scratch_shapes=scratch,
+        compiler_params=pltpu.CompilerParams(vmem_limit_bytes=16 * 1024 * 1024),
     )(*operands)
 
 
@@ -412,53 +480,65 @@
     return jax.ShapeDtypeStruct(shape, kind)
 
 
-def exchange(value):
-    return lax.all_to_all(value, ("zl", "x"), 0, 0, tiled=True)
-
-
-def moved(value, by):
+def exchange(value, axes):
+    return lax.all_to_all(value, axes, 0, 0, tiled=True)
+
+
+def moved(value, by, around):
     count = lax.axis_size("zh")
-    pairs = [(i, i + by) for i in range(count) if 0 <= i + by < count]
-    return lax.ppermute(value, "zh", pairs) if pairs else jnp.zeros_like(value)
-
-
-def swapped(value, bit):
-    count = lax.axis_size("zh")
-    if bit >= count:
-        return jnp.zeros_like(value)
-    return lax.ppermute(value, "zh", [(i, i ^ bit) for i in range(count)])
-
-
-def carry(own, marks, beside):
-    reverse = marks is not None
-    way = -1 if reverse else 1
-    got = exchange(own)
-    if not reverse:
-        marks = got
-    joined, rest = call(
-        functools.partial(gather_kernel, reverse),
-        [like(own.shape[1:]), like((8, LANES))],
+    pairs = [(i, i + by) for i in range(count)]
+    if around:
+        pairs = [(i, j % count) for i, j in pairs]
+    return lax.ppermute(value, "zh", [(i, j) for i, j in pairs if 0 <= j < count])
+
+
+def carry(own, beside):
+    got = exchange(own, ("zl", "x"))
+    message, tile = like(own.shape[1:]), like((STATE, LANES))
+    joined = call(functools.partial(gather_kernel, False), message, got, got)
+    from_next = moved(joined, 1, False)
+    from_next, beside = lax.optimization_barrier((from_next, beside()))
+    twice, state = call(
+        functools.partial(join_kernel, False), [message, tile], joined, from_next
+    )
+    handed = call(
+        functools.partial(hand_kernel, False),
+        like((GROUP, STATE, LANES)),
+        moved(twice, 1, False),
+        moved(state, 3, False),
         got,
-        marks,
-    )
-    from_next = moved(joined, way)
-    beside = beside()
-    if reverse:
-        rest = rest + swapped(rest, 4)
-    from_next, rest, beside = lax.optimization_barrier((from_next, rest, beside))
-    twice = call(join_kernel, like(own.shape[1:]), joined, from_next)
-    near, far = moved(twice, way), moved(twice, 3 * way)
-    if reverse:
-        rest = rest + swapped(rest, 2)
-    handed = call(
-        functools.partial(hand_kernel, reverse),
-        like((GROUP, STATE, LANES)),
+        got,
+    )
+    return (exchange(handed, ("zl", "x")), got, beside)
+
+
+def carry_back(own, marks, share, beside):
+    got = exchange(own, ("zl", "x"))
+    message, table = like((STATE + 16, LANES)), like((8, LANES))
+    joined, gain = call(functools.partial(gather_kernel, True), [message, table], got, marks)
+    from_next = moved(joined, -1, True)
+    gain_next = moved(gain, 1, True)
+    from_next, gain_next, beside = lax.optimization_barrier((from_next, gain_next, beside()))
+    twice, state, gain = call(
+        functools.partial(join_kernel, True),
+        [message, like((STATE + 8, LANES)), table],
+        joined,
+        from_next,
+        gain,
+        gain_next,
+    )
+    near, far = moved(twice, -1, True), moved(state, -3, True)
+    handed, gain = call(
+        functools.partial(hand_kernel, True),
+        [like((GROUP, STATE, LANES)), like((1, share))],
         near,
         far,
         got,
         marks,
-    )
-    return (exchange(handed), marks, rest, beside)
+        gain,
+        moved(gain, 2, True),
+    )
+    return (exchange(handed, ("zl", "x")), gain[0], beside)
 
 
 def per_device(
@@ -476,17 +556,9 @@
 ):
     rows, width = inputs_x.shape
     heads = dt_raw.shape[1]
-    docs = lengths.shape[0]
-    member = lax.axis_index(("zl", "x"))
-    group = lax.axis_index("zh")
-    total = rows * lax.axis_size("zh") * GROUP
     channels = float(width * lax.axis_size("tensor"))
-    first = (group * GROUP + member) * rows
-    info = jnp.concatenate(
-        [lengths, jnp.stack([first, jnp.int32(total - STRETCH)]).astype(jnp.int32)]
-    )
     steps = dt_raw.T
-    a_log, dt_bias = a_log[:, None], dt_bias[:, None]
+    a_log, dt_bias = a_log[None, :], dt_bias[None, :]
     skip_d, gain = skip_d[None, :], norm_gain[None, :]
     message = like((GROUP, STATE + 8, LANES))
     wide = like((rows, width))
@@ -494,22 +566,31 @@
     turned = like((heads, rows))
 
     own, summed, deltas = call(
-        functools.partial(states_kernel, docs),
+        states_kernel,
         [message, small, small],
-        info,
+        lengths,
         inputs_x,
         input_b,
         steps,
         a_log,
         dt_bias,
         smem=True,
+        hbm=True,
+        scratch=[
+            pltpu.VMEM(inputs_x.shape, BF16),
+            pltpu.VMEM(input_b.shape, BF16),
+            pltpu.VMEM(steps.shape, F32),
+            pltpu.VMEM(a_log.shape, F32),
+            pltpu.VMEM(dt_bias.shape, F32),
+            pltpu.SemaphoreType.DMA((5,)),
+        ],
     )
 
     def before():
         return call(
-            functools.partial(within_kernel, docs),
+            within_kernel,
             [wide, wide, wide, wide],
-            info,
+            lengths,
             inputs_x,
             gate_z,
             cotangent,
@@ -521,10 +602,10 @@
             smem=True,
         )
 
-    entering, marks, _, (within, fresh, gate, gated) = carry(own, None, before)
+    entering, marks, (within, fresh, gate, gated) = carry(own, before)
     core, bent, sums = call(
         output_kernel,
-        [wide, wide, like((2, rows))],
+        [wide, wide, like((lax.axis_size("tensor"), 2 * rows // LANES, LANES))],
         within,
         fresh,
         gate,
@@ -533,7 +614,7 @@
         gain,
         entering,
     )
-    sums = lax.all_gather(sums, "tensor")
+    sums = exchange(sums, "tensor")
     pulled, own_back = call(
         functools.partial(pull_kernel, channels),
         [wide, message],
@@ -548,7 +629,7 @@
 
     def after():
         return call(
-            functools.partial(inner_kernel, docs),
+            inner_kernel,
             [
                 wide,
                 wide,
@@ -558,7 +639,7 @@
                 turned,
                 turned,
             ],
-            info,
+            lengths,
             inputs_x,
             input_b,
             input_c,
@@ -573,7 +654,8 @@
             smem=True,
         )
 
-    later, _, gain_sum, beside = carry(own_back, marks, after)
+    share = width // (GROUP * lax.axis_size("zh"))
+    later, grad_gain, beside = carry_back(own_back, marks, share, after)
     base, weights, leaving, b_part, grad_c, along, back = beside
     grad_x, grad_b, grad_dt = call(
         final_kernel,
@@ -591,9 +673,6 @@
         back,
         later,
     )
-    gain_sum = gain_sum + swapped(gain_sum, 1)
-    share = width // (GROUP * lax.axis_size("zh"))
-    grad_gain = lax.dynamic_slice(gain_sum, (group, member * share), (1, share))[0]
     return (grad_x, grad_b, grad_c, grad_dt.T, grad_gain)
 
 

time: 155 us -> 139 us (0.90)
  the two profiles are of different devices: /device:TPU:2 before, /device:TPU:64 now
where the time goes in v3:
time: 139 us; the launch traced here: 138 us
  blocking collectives  62.2 us (45%)
  starting transfers between devices  47.4 us (34%)
  Pallas kernels  14.4 us (10%)
  waiting for transfers between devices  9.38 us (7%)
  local copies, waits for them, and re-layouts  3.9 us (3%)
    all_to_all x5, blocking collectives, exchange(): return lax.all_to_all(value, axes, 0, 0, tiled=True)  62.2 us
    ppermute x8, starting transfers between devices, moved(): lax.ppermute(value, 'zh', [(i, j) for i, j in pairs if 0 <= j < count])  47.4 us
    pallas_call x12, Pallas kernels, call(): pl.pallas_call(kernel, out_shape=outs, in_specs=in_specs, out_specs=[spec...  14.4 us
    ppermute x8, waiting for transfers between devices, moved(): lax.ppermute(value, 'zh', [(i, j) for i, j in pairs if 0 <= j < count])  9.38 us
    unnamed x28, local copies, waits for them, and re-layouts  3.9 us
  transfers between devices with their start and end apart: 8, of which 2 were waited for; matrix products, arithmetic and copies ran while one was open for 0% of the time, Pallas kernels for 5%

profile of v3, /device:TPU:64, one launch (start us, length us, event | category | flops | bytes accessed | tf_op | source)
XLA Modules:
  0.0 138.1 jit_solution(6935593191207871305)
XLA Ops:
  0.6 0.0 copy-start.10
  0.6 0.0 copy-start.12
  0.7 0.0 copy-start.13
  0.7 0.6 copy-done.10
  1.3 0.0 copy-done.12
  1.3 0.0 copy-done.13
  1.3 0.0 copy-start
  1.3 1.0 copy-done
  2.4 0.0 copy-start.3
  2.4 0.8 copy-done.3
  3.2 0.0 copy-start.7
  3.2 0.7 copy-done.7
  3.9 2.5 %shard_map.146 = (f32[8,136,128]{2,1,0:T(8,128)S(1)}, f32[256,16]{1,0:T(8,128)S(1)}, f32[256,16]{1,0:T(8,128)S(1)}) custom-call(s32[16]{0:T(128)S(1)} %copy-done.10, bf16[256,1024]{1,0:T(8,128)(2,1)S(1)} %copy-done, bf16[256,128]{1,0:T(8,128)(2,1)S(1)} %copy-done.3, f32[16,256]{1,0:T(8,128)S(1)} %bitcast.7, f32[1,16]{1,0:T(1,128)S(1)} %bitcast.13, ...), custom_call_target="tpu_custom_call" | custom-call | tf_op jit(solution)/shard_map/pallas_call | solution.py:469
  6.4 16.1 %all_to_all.25.got_ref.marks_ref = f32[8,136,128]{2,1,0:T(8,128)S(1)} all-to-all(f32[8,136,128]{2,1,0:T(8,128)S(1)} %get-tuple-element.50.own_ref), channel_id=1, replica_groups=mesh['zh'=8,'zl'=2,'x'=4,'tensor'=8] {'zl','x'}, dimensions={0} | all-to-all | bytes 1114112 | tf_op jit(solution)/shard_map/all_to_all | solution.py:484
  22.5 0.0 copy-start.2
  22.5 0.0 copy-start.4
  22.5 0.0 copy-start.5
  22.5 0.0 copy-start.6
  22.6 6.5 %collective-permute-start = (f32[136,128]{1,0:T(8,128)S(1)}, f32[136,128]{1,0:T(8,128)S(1)}, u32[]{:S(2)}, u32[]{:S(2)}) collective-permute-start(f32[136,128]{1,0:T(8,128)S(1)} %shard_map.147.own_ref), channel_id=1, source_target_pairs={{0,64},{64,128},{128,192},{192,256},{256,320},{320,384},{384,448},... | collective-permute-start | bytes 208904 | tf_op jit(solution)/shard_map/ppermute | solution.py:492
  29.1 0.0 copy-start.11
  29.1 0.0 copy-done.2
  29.1 0.0 copy-done.4
  29.1 0.0 copy-done.5
  29.2 0.0 copy-done.6
  29.2 0.6 copy-done.11
  29.8 2.9 %shard_map.148 = (f32[256,1024]{1,0:T(8,128)S(1)}, f32[256,1024]{1,0:T(8,128)S(1)}, f32[256,1024]{1,0:T(8,128)S(1)}, f32[256,1024]{1,0:T(8,128)S(1)}) custom-call(s32[16]{0:T(128)S(1)} %copy-done.10, bf16[256,1024]{1,0:T(8,128)(2,1)S(1)} %copy-done, bf16[256,1024]{1,0:T(8,128)(2,1)S(1)} %copy-done.5, bf16[256,1024]{1,0:T(8,128)(2,1)S(1)} %copy-done.6, ...), custom_call_target="tpu_custom_call" | custom-call | tf_op jit(solution)/shard_map/pallas_call | solution.py:469
  32.7 0.0 collective-permute-done.got_ref
  32.7 5.2 %collective-permute-start.1 = (f32[136,128]{1,0:T(8,128)S(1)}, f32[136,128]{1,0:T(8,128)S(1)}, u32[]{:S(2)}, u32[]{:S(2)}) collective-permute-start(f32[136,128]{1,0:T(8,128)S(1)} %get-tuple-element.62), channel_id=1, source_target_pairs={{0,64},{64,128},{128,192},{192,256},{256,320},{320,384},{384,448},... | collective-permute-start | bytes 208904 | tf_op jit(solution)/shard_map/ppermute | solution.py:492
  37.9 7.5 %collective-permute-start.2 = (f32[128,128]{1,0:T(8,128)S(1)}, f32[128,128]{1,0:T(8,128)S(1)}, u32[]{:S(2)}, u32[]{:S(2)}) collective-permute-start(f32[128,128]{1,0:T(8,128)S(1)} %get-tuple-element.63), channel_id=1, source_target_pairs={{0,192},{64,256},{128,320},{192,384},{256,448},{1,193},{65,257},{1... | collective-permute-start | bytes 196616 | tf_op jit(solution)/shard_map/ppermute | solution.py:492
  45.3 1.9 %collective-permute-done.2.far_ref = f32[128,128]{1,0:T(8,128)S(1)} collective-permute-done((f32[128,128]{1,0:T(8,128)S(1)}, f32[128,128]{1,0:T(8,128)S(1)}, u32[]{:S(2)}, u32[]{:S(2)}) %collective-permute-start.2) | collective-permute-done | bytes 65568 | tf_op jit(solution)/shard_map/ppermute | solution.py:492
  47.2 0.0 collective-permute-done.1.near_ref
  47.3 0.0 copy-start.9
  47.3 12.0 %all_to_all.26.entering_ref = f32[8,128,128]{2,1,0:T(8,128)S(1)} all-to-all(f32[8,128,128]{2,1,0:T(8,128)S(1)} %shard_map.150), channel_id=1, replica_groups=mesh['zh'=8,'zl'=2,'x'=4,'tensor'=8] {'zl','x'}, dimensions={0} | all-to-all | bytes 1048576 | tf_op jit(solution)/shard_map/all_to_all | solution.py:484
  59.3 0.0 copy-done.9
  59.3 0.9 shard_map.151
  60.2 9.6 %all_to_all.27.sums_ref = f32[8,4,128]{2,1,0:T(4,128)S(1)} all-to-all(f32[8,4,128]{2,1,0:T(4,128)S(1)} %get-tuple-element.66), channel_id=1, replica_groups=mesh['zh'=8,'zl'=2,'x'=4,'tensor'=8] {'tensor'}, dimensions={0} | all-to-all | bytes 32768 | tf_op jit(solution)/shard_map/all_to_all | solution.py:484
  69.8 0.7 shard_map.152
  70.6 13.3 %all_to_all.28.got_ref = f32[8,136,128]{2,1,0:T(8,128)S(1)} all-to-all(f32[8,136,128]{2,1,0:T(8,128)S(1)} %get-tuple-element.67), channel_id=1, replica_groups=mesh['zh'=8,'zl'=2,'x'=4,'tensor'=8] {'zl','x'}, dimensions={0} | all-to-all | bytes 1114112 | tf_op jit(solution)/shard_map/all_to_all | solution.py:484
  83.9 0.0 copy-start.1
  84.0 3.7 %collective-permute-start.3 = (f32[144,128]{1,0:T(8,128)S(1)}, f32[144,128]{1,0:T(8,128)S(1)}, u32[]{:S(2)}, u32[]{:S(2)}) collective-permute-start(f32[144,128]{1,0:T(8,128)S(1)} %get-tuple-element.68.own_ref), channel_id=1, source_target_pairs={{0,448},{64,0},{128,64},{192,128},{256,192},{320,256},{384,320},{4... | collective-permute-start | bytes 221192 | tf_op jit(solution)/shard_map/ppermute | solution.py:492
  87.7 6.4 %collective-permute-start.4 = (f32[8,128]{1,0:T(8,128)S(1)}, f32[8,128]{1,0:T(8,128)S(1)}, u32[]{:S(2)}, u32[]{:S(2)}) collective-permute-start(f32[8,128]{1,0:T(8,128)S(1)} %get-tuple-element.69.refs_0_), channel_id=1, source_target_pairs={{0,64},{64,128},{128,192},{192,256},{256,320},{320,384},{384,448},... | collective-permute-start | bytes 12296 | tf_op jit(solution)/shard_map/ppermute | solution.py:492
  94.2 0.0 copy-done.1
  94.2 4.3 %shard_map.154 = (f32[256,1024]{1,0:T(8,128)S(1)}, f32[256,1024]{1,0:T(8,128)S(1)}, f32[128,1024]{1,0:T(8,128)S(1)}, f32[256,128]{1,0:T(8,128)S(1)}, bf16[256,12...) custom-call(s32[16]{0:T(128)S(1)} %copy-done.10, bf16[256,1024]{1,0:T(8,128)(2,1)S(1)} %copy-done.1, ...), custom_call_target="tpu_custom_call" | custom-call | tf_op jit(solution)/shard_map/pallas_call | solution.py:469
  98.5 0.0 collective-permute-done.4.refs_1_
  98.5 0.0 collective-permute-done.3.got_ref
  98.5 4.1 %collective-permute-start.5 = (f32[144,128]{1,0:T(8,128)S(1)}, f32[144,128]{1,0:T(8,128)S(1)}, u32[]{:S(2)}, u32[]{:S(2)}) collective-permute-start(f32[144,128]{1,0:T(8,128)S(1)} %get-tuple-element.86), channel_id=1, source_target_pairs={{0,448},{64,0},{128,64},{192,128},{256,192},{320,256},{384,320},{4... | collective-permute-start | bytes 221192 | tf_op jit(solution)/shard_map/ppermute | solution.py:492
  102.6 12.0 %collective-permute-start.6 = (f32[136,128]{1,0:T(8,128)S(1)}, f32[136,128]{1,0:T(8,128)S(1)}, u32[]{:S(2)}, u32[]{:S(2)}) collective-permute-start(f32[136,128]{1,0:T(8,128)S(1)} %get-tuple-element.87), channel_id=1, source_target_pairs={{0,320},{64,384},{128,448},{192,0},{256,64},{320,128},{384,192},{4... | collective-permute-start | bytes 208904 | tf_op jit(solution)/shard_map/ppermute | solution.py:492
  114.6 1.9 %collective-permute-start.7 = (f32[8,128]{1,0:T(8,128)S(1)}, f32[8,128]{1,0:T(8,128)S(1)}, u32[]{:S(2)}, u32[]{:S(2)}) collective-permute-start(f32[8,128]{1,0:T(8,128)S(1)} %get-tuple-element.88.refs_0_), channel_id=1, source_target_pairs={{0,128},{64,192},{128,256},{192,320},{256,384},{320,448},{384,0},{... | collective-permute-start | bytes 12296 | tf_op jit(solution)/shard_map/ppermute | solution.py:492
  116.6 7.5 %collective-permute-done.7.refs_1_ = f32[8,128]{1,0:T(8,128)S(1)} collective-permute-done((f32[8,128]{1,0:T(8,128)S(1)}, f32[8,128]{1,0:T(8,128)S(1)}, u32[]{:S(2)}, u32[]{:S(2)}) %collective-permute-start.7) | collective-permute-done | bytes 4128 | tf_op jit(solution)/shard_map/ppermute | solution.py:492
  124.0 0.0 collective-permute-done.6.far_ref
  124.0 0.0 collective-permute-done.5.near_ref
  124.0 0.7 shard_map.156
  124.8 0.0 copy-start.8
  124.8 11.2 %all_to_all.29.later_ref = f32[8,128,128]{2,1,0:T(8,128)S(1)} all-to-all(f32[8,128,128]{2,1,0:T(8,128)S(1)} %get-tuple-element.89), channel_id=1, replica_groups=mesh['zh'=8,'zl'=2,'x'=4,'tensor'=8] {'zl','x'}, dimensions={0} | all-to-all | bytes 1048576 | tf_op jit(solution)/shard_map/all_to_all | solution.py:484
  135.9 0.0 copy-done.8
  135.9 2.2 %shard_map.157 = (bf16[256,1024]{1,0:T(8,128)(2,1)}, bf16[256,128]{1,0:T(8,128)(2,1)}, f32[16,256]{1,0:T(8,128)}) custom-call(bf16[256,1024]{1,0:T(8,128)(2,1)S(1)} %copy-done.1, bf16[256,128]{1,0:T(8,128)(2,1)S(1)} %copy-done.4, f32[16,256]{1,0:T(8,128)S(1)} %bitcast.8, f32[1,16]{1,0:T(1,128)S(1)} %bitcast.14, f32[1,16]{1,0:T(1,128)S(1)} %bitcast.16, ...), custom_call_target="tpu_custom_call" | custom-call | tf_op jit(solution)/shard_map/pallas_call | solution.py:469
  (5 shorter events, 0.2 us)
Async XLA Ops:
  0.6 0.7 copy-start.10
  0.6 0.7 copy-start.12
  0.7 0.7 copy-start.13
  1.3 1.0 copy-start
  2.4 0.8 copy-start.3
  3.2 0.7 copy-start.7
  22.5 6.6 %copy-start.2 = (bf16[256,128]{1,0:T(8,128)(2,1)S(1)}, bf16[256,128]{1,0:T(8,128)(2,1)}, u32[]{:S(2)}) copy-start(bf16[256,128]{1,0:T(8,128)(2,1)} %c_ref.7) | copy-start | bytes 196612
  22.5 6.6 %copy-start.4 = (bf16[256,128]{1,0:T(8,128)(2,1)S(1)}, bf16[256,128]{1,0:T(8,128)(2,1)}, u32[]{:S(2)}) copy-start(bf16[256,128]{1,0:T(8,128)(2,1)} %b_ref.5) | copy-start | bytes 196612
  22.5 6.6 %copy-start.5 = (bf16[256,1024]{1,0:T(8,128)(2,1)S(1)}, bf16[256,1024]{1,0:T(8,128)(2,1)}, u32[]{:S(2)}) copy-start(bf16[256,1024]{1,0:T(8,128)(2,1)} %z_ref.1) | copy-start | bytes 1572868
  22.5 6.6 %copy-start.6 = (bf16[256,1024]{1,0:T(8,128)(2,1)S(1)}, bf16[256,1024]{1,0:T(8,128)(2,1)}, u32[]{:S(2)}) copy-start(bf16[256,1024]{1,0:T(8,128)(2,1)} %cot_ref.1) | copy-start | bytes 1572868
  22.6 10.1 %collective-permute-start = (f32[136,128]{1,0:T(8,128)S(1)}, f32[136,128]{1,0:T(8,128)S(1)}, u32[]{:S(2)}, u32[]{:S(2)}) collective-permute-start(f32[136,128]{1,0:T(8,128)S(1)} %shard_map.147.own_ref), channel_id=1, source_target_pairs={{0,64},{64,128},{128,192},{192,256},{256,320},{320,384},{384,448},... | collective-permute-start | bytes 208904 | tf_op jit(solution)/shard_map/ppermute | solution.py:492
  29.1 0.7 copy-start.11
  32.7 14.5 %collective-permute-start.1 = (f32[136,128]{1,0:T(8,128)S(1)}, f32[136,128]{1,0:T(8,128)S(1)}, u32[]{:S(2)}, u32[]{:S(2)}) collective-permute-start(f32[136,128]{1,0:T(8,128)S(1)} %get-tuple-element.62), channel_id=1, source_target_pairs={{0,64},{64,128},{128,192},{192,256},{256,320},{320,384},{384,448},... | collective-permute-start | bytes 208904 | tf_op jit(solution)/shard_map/ppermute | solution.py:492
  37.9 9.4 %collective-permute-start.2 = (f32[128,128]{1,0:T(8,128)S(1)}, f32[128,128]{1,0:T(8,128)S(1)}, u32[]{:S(2)}, u32[]{:S(2)}) collective-permute-start(f32[128,128]{1,0:T(8,128)S(1)} %get-tuple-element.63), channel_id=1, source_target_pairs={{0,192},{64,256},{128,320},{192,384},{256,448},{1,193},{65,257},{1... | collective-permute-start | bytes 196616 | tf_op jit(solution)/shard_map/ppermute | solution.py:492
  47.3 12.0 %copy-start.9 = (f32[1024]{0:T(1024)S(1)}, f32[1024]{0:T(1024)}, u32[]{:S(2)}) copy-start(f32[1024]{0:T(1024)} %param.19) | copy-start | bytes 12292
  83.9 10.2 %copy-start.1 = (bf16[256,1024]{1,0:T(8,128)(2,1)S(1)}, bf16[256,1024]{1,0:T(8,128)(2,1)}, u32[]{:S(2)}) copy-start(bf16[256,1024]{1,0:T(8,128)(2,1)} %x_ref.5) | copy-start | bytes 1572868
  84.0 14.5 %collective-permute-start.3 = (f32[144,128]{1,0:T(8,128)S(1)}, f32[144,128]{1,0:T(8,128)S(1)}, u32[]{:S(2)}, u32[]{:S(2)}) collective-permute-start(f32[144,128]{1,0:T(8,128)S(1)} %get-tuple-element.68.own_ref), channel_id=1, source_target_pairs={{0,448},{64,0},{128,64},{192,128},{256,192},{320,256},{384,320},{4... | collective-permute-start | bytes 221192 | tf_op jit(solution)/shard_map/ppermute | solution.py:492
  87.7 10.8 %collective-permute-start.4 = (f32[8,128]{1,0:T(8,128)S(1)}, f32[8,128]{1,0:T(8,128)S(1)}, u32[]{:S(2)}, u32[]{:S(2)}) collective-permute-start(f32[8,128]{1,0:T(8,128)S(1)} %get-tuple-element.69.refs_0_), channel_id=1, source_target_pairs={{0,64},{64,128},{128,192},{192,256},{256,320},{320,384},{384,448},... | collective-permute-start | bytes 12296 | tf_op jit(solution)/shard_map/ppermute | solution.py:492
  98.5 25.5 %collective-permute-start.5 = (f32[144,128]{1,0:T(8,128)S(1)}, f32[144,128]{1,0:T(8,128)S(1)}, u32[]{:S(2)}, u32[]{:S(2)}) collective-permute-start(f32[144,128]{1,0:T(8,128)S(1)} %get-tuple-element.86), channel_id=1, source_target_pairs={{0,448},{64,0},{128,64},{192,128},{256,192},{320,256},{384,320},{4... | collective-permute-start | bytes 221192 | tf_op jit(solution)/shard_map/ppermute | solution.py:492
  102.6 21.4 %collective-permute-start.6 = (f32[136,128]{1,0:T(8,128)S(1)}, f32[136,128]{1,0:T(8,128)S(1)}, u32[]{:S(2)}, u32[]{:S(2)}) collective-permute-start(f32[136,128]{1,0:T(8,128)S(1)} %get-tuple-element.87), channel_id=1, source_target_pairs={{0,320},{64,384},{128,448},{192,0},{256,64},{320,128},{384,192},{4... | collective-permute-start | bytes 208904 | tf_op jit(solution)/shard_map/ppermute | solution.py:492
  114.6 9.4 %collective-permute-start.7 = (f32[8,128]{1,0:T(8,128)S(1)}, f32[8,128]{1,0:T(8,128)S(1)}, u32[]{:S(2)}, u32[]{:S(2)}) collective-permute-start(f32[8,128]{1,0:T(8,128)S(1)} %get-tuple-element.88.refs_0_), channel_id=1, source_target_pairs={{0,128},{64,192},{128,256},{192,320},{256,384},{320,448},{384,0},{... | collective-permute-start | bytes 12296 | tf_op jit(solution)/shard_map/ppermute | solution.py:492
  124.8 11.2 %copy-start.8 = (f32[256,16]{0,1:T(8,128)S(1)}, f32[256,16]{0,1:T(8,128)}, u32[]{:S(2)}) copy-start(f32[256,16]{0,1:T(8,128)} %param.15) | copy-start | bytes 49156

commit v4 on v3

--- a/solution.py
+++ b/solution.py
@@ -15,6 +15,7 @@
 WIDE = 2 * LANES
 GROUP = 8
 EPSILON = 1e-05
+ROOM = 62
 F32 = jnp.float32
 BF16 = jnp.bfloat16
 NN = (((1,), (0,)), ((), ()))
@@ -363,12 +364,23 @@
     along_ref,
     back_ref,
     later_ref,
+    gains_ref,
     x_out_ref,
     b_out_ref,
     dt_out_ref,
+    gain_out_ref,
 ):
     rows = x_ref.shape[0]
     heads = dt_ref.shape[0]
+    table = gains_ref[0]
+    for one in range(1, gains_ref.shape[0]):
+        table = table + gains_ref[one]
+    table = jnp.broadcast_to(table, (8, LANES))
+    share = gain_out_ref.shape[1]
+    lane = lax.broadcasted_iota(jnp.int32, (LANES, share), 0)
+    place = lax.broadcasted_iota(jnp.int32, (LANES, share), 1)
+    chosen = jnp.where(lane == place + share * member_index(), 1.0, 0.0).astype(BF16)
+    gain_out_ref[...] = mul_3x(table, chosen)[0:1]
     b = b_ref[...]
     b_twice = jnp.concatenate([b, b], axis=1)
     b_sum = b_in_ref[...]
@@ -412,56 +424,37 @@
         gain = got_ref[0, STATE : STATE + 8, :]
         for one in range(1, GROUP):
             gain = gain + got_ref[one, STATE : STATE + 8, :]
-        out_ref[STATE : STATE + 8, :] = gain
         gain_ref[0][...] = gain
 
 
-def join_kernel(reverse, own_ref, got_ref, *refs):
-    end = own_ref.shape[0] - 8
-    through = own_ref[end : end + 1, :]
+def join_kernel(own_ref, got_ref, out_ref, far_ref):
+    through = own_ref[STATE : STATE + 1, :]
     joined = own_ref[0:STATE, :] + through * got_ref[0:STATE, :]
-    if reverse:
-        gain_ref, gain_got_ref, out_ref, far_ref, gain_out_ref = refs
-        both = own_ref[STATE : STATE + 8, :] + got_ref[STATE : STATE + 8, :]
-        out_ref[STATE : STATE + 8, :] = both
-        far_ref[STATE : STATE + 8, :] = both
-        gain_out_ref[...] = gain_ref[...] + gain_got_ref[...]
-    else:
-        out_ref, far_ref = refs
     out_ref[0:STATE, :] = joined
     far_ref[0:STATE, :] = joined
-    out_ref[end : end + 8, :] = own_ref[end : end + 8, :] * got_ref[end : end + 8, :]
-
-
-def hand_kernel(reverse, near_ref, far_ref, got_ref, marks_ref, *refs):
+    out_ref[STATE : STATE + 8, :] = own_ref[STATE : STATE + 8, :] * got_ref[STATE : STATE + 8, :]
+
+
+def hand_members(holding, reverse, got_ref, marks_ref, out_ref):
     order = list(range(GROUP))
-    out_ref = refs[-2] if reverse else refs[-1]
-    end = near_ref.shape[0] - 8
-    holding = near_ref[0:STATE, :] + near_ref[end : end + 1, :] * far_ref[0:STATE, :]
     if reverse:
         order.reverse()
-        group = lax.axis_index("zh")
-        holding = jnp.where(group == lax.axis_size("zh") - 1, 0.0, holding)
     for one in order:
         out_ref[one] = holding
         if one != order[-1]:
             through = marks_ref[one, STATE : STATE + 1, :]
             holding = through * holding + got_ref[one, 0:STATE, :]
-    if reverse:
-        table = refs[0][...] + refs[1][...]
-        table = table + near_ref[STATE : STATE + 8, :] + far_ref[STATE : STATE + 8, :]
-        row = lax.broadcasted_iota(jnp.int32, table.shape, 0)
-        table = jnp.where(row == group, table, 0.0)
-        gain_ref = refs[-1]
-        share = gain_ref.shape[1]
-        lane = lax.broadcasted_iota(jnp.int32, (LANES, share), 0)
-        place = lax.broadcasted_iota(jnp.int32, (LANES, share), 1)
-        chosen = jnp.where(lane == place + share * member_index(), 1.0, 0.0).astype(BF16)
-        gain_ref[...] = jnp.sum(mul_3x(table, chosen), axis=0, keepdims=True)
-
-
-def call(kernel, outs, *operands, smem=False, hbm=False, scratch=()):
-    in_specs = [pl.BlockSpec(memory_space=pltpu.HBM if hbm else pltpu.VMEM) for _ in operands]
+
+
+def hand_kernel(reverse, near_ref, far_ref, got_ref, marks_ref, out_ref):
+    through = near_ref[STATE : STATE + 1, :]
+    holding = near_ref[0:STATE, :] + through * far_ref[0:STATE, :]
+    hand_members(holding, reverse, got_ref, marks_ref, out_ref)
+
+
+def call(kernel, outs, *operands, smem=False, hbm=False, scratch=(), room=16):
+    space = pltpu.HBM if hbm else pltpu.VMEM
+    in_specs = [jax.tree.map(lambda _: pl.BlockSpec(memory_space=space), one) for one in operands]
     if smem:
         in_specs[0] = pl.BlockSpec(memory_space=pltpu.SMEM)
     many = isinstance(outs, (list, tuple))
@@ -472,7 +465,7 @@
         in_specs=in_specs,
         out_specs=[spec] * len(outs) if many else spec,
         scratch_shapes=scratch,
-        compiler_params=pltpu.CompilerParams(vmem_limit_bytes=16 * 1024 * 1024),
+        compiler_params=pltpu.CompilerParams(vmem_limit_bytes=room * 1024 * 1024),
     )(*operands)
 
 
@@ -498,9 +491,7 @@
     joined = call(functools.partial(gather_kernel, False), message, got, got)
     from_next = moved(joined, 1, False)
     from_next, beside = lax.optimization_barrier((from_next, beside()))
-    twice, state = call(
-        functools.partial(join_kernel, False), [message, tile], joined, from_next
-    )
+    twice, state = call(join_kernel, [message, tile], joined, from_next)
     handed = call(
         functools.partial(hand_kernel, False),
         like((GROUP, STATE, LANES)),
@@ -512,33 +503,24 @@
     return (exchange(handed, ("zl", "x")), got, beside)
 
 
-def carry_back(own, marks, share, beside):
+def carry_back(own, marks, beside):
     got = exchange(own, ("zl", "x"))
-    message, table = like((STATE + 16, LANES)), like((8, LANES))
+    message, table, tile = like((STATE + 8, LANES)), like((8, LANES)), like((STATE, LANES))
     joined, gain = call(functools.partial(gather_kernel, True), [message, table], got, marks)
-    from_next = moved(joined, -1, True)
-    gain_next = moved(gain, 1, True)
-    from_next, gain_next, beside = lax.optimization_barrier((from_next, gain_next, beside()))
-    twice, state, gain = call(
-        functools.partial(join_kernel, True),
-        [message, like((STATE + 8, LANES)), table],
-        joined,
-        from_next,
-        gain,
-        gain_next,
-    )
-    near, far = moved(twice, -1, True), moved(state, -3, True)
-    handed, gain = call(
+    gains = exchange(gain[:, None, :], "zh")
+    from_next, beside = lax.optimization_barrier((moved(joined, -1, False), beside()))
+    twice, state = call(join_kernel, [message, tile], joined, from_next)
+    near, far = moved(twice, -1, False), moved(state, -3, False)
+    near, far, gains = lax.optimization_barrier((near, far, gains))
+    handed = call(
         functools.partial(hand_kernel, True),
-        [like((GROUP, STATE, LANES)), like((1, share))],
+        like((GROUP, STATE, LANES)),
         near,
         far,
         got,
         marks,
-        gain,
-        moved(gain, 2, True),
-    )
-    return (exchange(handed, ("zl", "x")), gain[0], beside)
+    )
+    return (exchange(handed, ("zl", "x")), gains, beside)
 
 
 def per_device(
@@ -576,6 +558,7 @@
         dt_bias,
         smem=True,
         hbm=True,
+        room=ROOM,
         scratch=[
             pltpu.VMEM(inputs_x.shape, BF16),
             pltpu.VMEM(input_b.shape, BF16),
@@ -654,12 +637,12 @@
             smem=True,
         )
 
+    later, gains, beside = carry_back(own_back, marks, after)
+    base, weights, leaving, b_part, grad_c, along, back = beside
     share = width // (GROUP * lax.axis_size("zh"))
-    later, grad_gain, beside = carry_back(own_back, marks, share, after)
-    base, weights, leaving, b_part, grad_c, along, back = beside
-    grad_x, grad_b, grad_dt = call(
+    grad_x, grad_b, grad_dt, grad_gain = call(
         final_kernel,
-        [like((rows, width), BF16), like((rows, STATE), BF16), turned],
+        [like((rows, width), BF16), like((rows, STATE), BF16), turned, like((1, share))],
         inputs_x,
         input_b,
         steps,
@@ -672,8 +655,9 @@
         along,
         back,
         later,
-    )
-    return (grad_x, grad_b, grad_c, grad_dt.T, grad_gain)
+        gains,
+    )
+    return (grad_x, grad_b, grad_c, grad_dt.T, grad_gain[0])
 
 
 def solution(mesh):

time: 139 us -> 137 us (0.986)
  the two profiles are of different devices: /device:TPU:64 before, /device:TPU:8 now
where the time goes in v4:
time: 137 us; the launch traced here: 136 us
  blocking collectives  89.4 us (65%)
  starting transfers between devices  26.2 us (19%)
  Pallas kernels  15.1 us (11%)
  waiting for transfers between devices  4.09 us (3%)
    all_to_all x6, blocking collectives, exchange(): return lax.all_to_all(value, axes, 0, 0, tiled=True)  89.4 us
    ppermute x6, starting transfers between devices, moved(): lax.ppermute(value, 'zh', [(i, j) for i, j in pairs if 0 <= j < count])  26.2 us
    pallas_call x12, Pallas kernels, call(): pl.pallas_call(kernel, out_shape=outs, in_specs=in_specs, out_specs=[spec...  15.1 us
    ppermute x6, waiting for transfers between devices, moved(): lax.ppermute(value, 'zh', [(i, j) for i, j in pairs if 0 <= j < count])  4.09 us
  transfers between devices with their start and end apart: 6, of which 2 were waited for; matrix products, arithmetic and copies ran while one was open for 0% of the time, Pallas kernels for 5%

profile of v4, /device:TPU:8, one launch (start us, length us, event | category | flops | bytes accessed | tf_op | source)
XLA Modules:
  0.0 136.3 jit_solution(11111000436714641850)
XLA Ops:
  0.6 3.8 %shard_map.146 = (f32[8,136,128]{2,1,0:T(8,128)}, f32[256,16]{1,0:T(8,128)}, f32[256,16]{1,0:T(8,128)}) custom-call(s32[16]{0:T(128)} %lengths_ref.5, bf16[256,1024]{1,0:T(8,128)(2,1)} %x_ref.5, bf16[256,128]{1,0:T(8,128)(2,1)} %b_ref.5, f32[16,256]{1,0:T(8,128)} %bitcast.8, f32[1,16]{1,0:T(1,128)} %bitcast.15, f32[1,16]{1,0:T(1,128)} %bitcast.17), custom_call_target="tpu_custom_call" | custom-call | tf_op jit(solution)/shard_map/pallas_call | solution.py:462
  4.4 0.0 copy-start.5
  4.4 0.0 copy-start.6
  4.4 0.0 copy-start.7
  4.4 16.5 %all_to_all.30.got_ref.marks_ref = f32[8,136,128]{2,1,0:T(8,128)S(1)} all-to-all(f32[8,136,128]{2,1,0:T(8,128)} %get-tuple-element.50.own_ref), channel_id=1, replica_groups=mesh['zh'=8,'zl'=2,'x'=4,'tensor'=8] {'zl','x'}, dimensions={0} | all-to-all | bytes 1114112 | tf_op jit(solution)/shard_map/all_to_all | solution.py:477
  20.9 0.0 copy-start
  20.9 0.0 copy-start.2
  20.9 0.0 copy-start.3
  20.9 0.0 copy-start.4
  21.0 5.3 %collective-permute-start = (f32[136,128]{1,0:T(8,128)S(1)}, f32[136,128]{1,0:T(8,128)S(1)}, u32[]{:S(2)}, u32[]{:S(2)}) collective-permute-start(f32[136,128]{1,0:T(8,128)S(1)} %shard_map.147.own_ref), channel_id=1, source_target_pairs={{0,64},{64,128},{128,192},{192,256},{256,320},{320,384},{384,448},... | collective-permute-start | bytes 208904 | tf_op jit(solution)/shard_map/ppermute | solution.py:485
  26.3 0.0 copy-start.10
  26.3 0.0 copy-start.11
  26.3 0.0 copy-done.5
  26.3 0.0 copy-done.6
  26.3 0.0 copy-done.7
  26.4 0.0 copy-done
  26.4 0.0 copy-done.2
  26.4 0.0 copy-done.3
  26.4 0.0 copy-done.4
  26.4 0.6 copy-done.10
  27.0 0.0 copy-done.11
  27.0 2.9 %shard_map.148 = (f32[256,1024]{1,0:T(8,128)S(1)}, f32[256,1024]{1,0:T(8,128)S(1)}, f32[256,1024]{1,0:T(8,128)S(1)}, f32[256,1024]{1,0:T(8,128)S(1)}) custom-call(s32[16]{0:T(128)S(1)} %copy-done.10, bf16[256,1024]{1,0:T(8,128)(2,1)S(1)} %copy-done, bf16[256,1024]{1,0:T(8,128)(2,1)S(1)} %copy-done.4, bf16[256,1024]{1,0:T(8,128)(2,1)S(1)} %copy-done.5, ...), custom_call_target="tpu_custom_call" | custom-call | tf_op jit(solution)/shard_map/pallas_call | solution.py:462
  29.9 0.0 collective-permute-done.got_ref
  29.9 6.4 %collective-permute-start.1 = (f32[136,128]{1,0:T(8,128)S(1)}, f32[136,128]{1,0:T(8,128)S(1)}, u32[]{:S(2)}, u32[]{:S(2)}) collective-permute-start(f32[136,128]{1,0:T(8,128)S(1)} %get-tuple-element.62), channel_id=1, source_target_pairs={{0,64},{64,128},{128,192},{192,256},{256,320},{320,384},{384,448},... | collective-permute-start | bytes 208904 | tf_op jit(solution)/shard_map/ppermute | solution.py:485
  36.3 10.4 %collective-permute-start.2 = (f32[128,128]{1,0:T(8,128)S(1)}, f32[128,128]{1,0:T(8,128)S(1)}, u32[]{:S(2)}, u32[]{:S(2)}) collective-permute-start(f32[128,128]{1,0:T(8,128)S(1)} %get-tuple-element.63), channel_id=1, source_target_pairs={{0,192},{64,256},{128,320},{192,384},{256,448},{1,193},{65,257},{1... | collective-permute-start | bytes 196616 | tf_op jit(solution)/shard_map/ppermute | solution.py:485
  46.8 1.9 %collective-permute-done.2.far_ref = f32[128,128]{1,0:T(8,128)S(1)} collective-permute-done((f32[128,128]{1,0:T(8,128)S(1)}, f32[128,128]{1,0:T(8,128)S(1)}, u32[]{:S(2)}, u32[]{:S(2)}) %collective-permute-start.2) | collective-permute-done | bytes 65568 | tf_op jit(solution)/shard_map/ppermute | solution.py:485
  48.6 0.0 collective-permute-done.1.near_ref
  48.7 0.0 copy-start.9
  48.7 11.0 %all_to_all.31.entering_ref = f32[8,128,128]{2,1,0:T(8,128)S(1)} all-to-all(f32[8,128,128]{2,1,0:T(8,128)S(1)} %shard_map.150), channel_id=1, replica_groups=mesh['zh'=8,'zl'=2,'x'=4,'tensor'=8] {'zl','x'}, dimensions={0} | all-to-all | bytes 1048576 | tf_op jit(solution)/shard_map/all_to_all | solution.py:477
  59.7 0.0 copy-done.9
  59.8 0.9 shard_map.151
  60.7 8.6 %all_to_all.32.sums_ref = f32[8,4,128]{2,1,0:T(4,128)S(1)} all-to-all(f32[8,4,128]{2,1,0:T(4,128)S(1)} %get-tuple-element.66), channel_id=1, replica_groups=mesh['zh'=8,'zl'=2,'x'=4,'tensor'=8] {'tensor'}, dimensions={0} | all-to-all | bytes 32768 | tf_op jit(solution)/shard_map/all_to_all | solution.py:477
  69.3 0.8 shard_map.152
  70.0 13.3 %all_to_all.33.got_ref = f32[8,136,128]{2,1,0:T(8,128)S(1)} all-to-all(f32[8,136,128]{2,1,0:T(8,128)S(1)} %get-tuple-element.67), channel_id=1, replica_groups=mesh['zh'=8,'zl'=2,'x'=4,'tensor'=8] {'zl','x'}, dimensions={0} | all-to-all | bytes 1114112 | tf_op jit(solution)/shard_map/all_to_all | solution.py:477
  83.4 0.0 copy-start.1
  83.4 1.4 %collective-permute-start.3 = (f32[136,128]{1,0:T(8,128)S(1)}, f32[136,128]{1,0:T(8,128)S(1)}, u32[]{:S(2)}, u32[]{:S(2)}) collective-permute-start(f32[136,128]{1,0:T(8,128)S(1)} %get-tuple-element.68.own_ref), channel_id=1, source_target_pairs={{64,0},{128,64},{192,128},{256,192},{320,256},{384,320},{448,384},... | collective-permute-start | bytes 208904 | tf_op jit(solution)/shard_map/ppermute | solution.py:485
  84.8 0.0 copy-done.1
  84.8 4.3 %shard_map.154 = (f32[256,1024]{1,0:T(8,128)S(1)}, f32[256,1024]{1,0:T(8,128)S(1)}, f32[128,1024]{1,0:T(8,128)S(1)}, f32[256,128]{1,0:T(8,128)S(1)}, bf16[256,12...) custom-call(s32[16]{0:T(128)S(1)} %copy-done.10, bf16[256,1024]{1,0:T(8,128)(2,1)S(1)} %copy-done, ...), custom_call_target="tpu_custom_call" | custom-call | tf_op jit(solution)/shard_map/pallas_call | solution.py:462
  89.2 2.2 %collective-permute-done.3.got_ref = f32[136,128]{1,0:T(8,128)S(1)} collective-permute-done((f32[136,128]{1,0:T(8,128)S(1)}, f32[136,128]{1,0:T(8,128)S(1)}, u32[]{:S(2)}, u32[]{:S(2)}) %collective-permute-start.3) | collective-permute-done | bytes 69664 | tf_op jit(solution)/shard_map/ppermute | solution.py:485
  91.4 1.3 collective-permute-start.4
  92.7 1.3 collective-permute-start.5
  94.0 28.7 %all_to_all.34.gains_ref = f32[8,1,128]{2,1,0:T(1,128)S(1)} all-to-all(f32[8,1,128]{2,1,0:T(1,128)S(1)} %bitcast.12), channel_id=1, replica_groups=mesh['zh'=8,'zl'=2,'x'=4,'tensor'=8] {'zh'}, dimensions={0} | all-to-all | bytes 8192 | tf_op jit(solution)/shard_map/all_to_all | solution.py:477
  122.7 0.0 collective-permute-done.5.far_ref
  122.7 0.0 collective-permute-done.4.near_ref
  122.7 0.1 shard_map.156
  122.8 0.0 copy-start.8
  122.8 0.0 copy-start.12
  122.8 0.0 copy-start.13
  122.8 11.2 %all_to_all.35.later_ref = f32[8,128,128]{2,1,0:T(8,128)S(1)} all-to-all(f32[8,128,128]{2,1,0:T(8,128)S(1)} %shard_map.156), channel_id=1, replica_groups=mesh['zh'=8,'zl'=2,'x'=4,'tensor'=8] {'zl','x'}, dimensions={0} | all-to-all | bytes 1048576 | tf_op jit(solution)/shard_map/all_to_all | solution.py:477
  134.0 0.0 copy-done.8
  134.0 0.0 copy-done.12
  134.0 0.0 copy-done.13
  134.0 2.3 %shard_map.157 = (bf16[256,1024]{1,0:T(8,128)(2,1)}, bf16[256,128]{1,0:T(8,128)(2,1)}, f32[16,256]{1,0:T(8,128)}, f32[1,16]{1,0:T(1,128)}) custom-call(bf16[256,1024]{1,0:T(8,128)(2,1)S(1)} %copy-done, bf16[256,128]{1,0:T(8,128)(2,1)S(1)} %copy-done.3, f32[16,256]{1,0:T(8,128)S(1)} %bitcast.9, f32[1,16]{1,0:T(1,128)S(1)} %bitcast.16, f32[1,16]{1,0:T(1,128)S(1)} %bitcast.18, ...), custom_call_target="tpu_custom_call" | custom-call | tf_op jit(solution)/shard_map/pallas_call | solution.py:462
  (5 shorter events, 0.2 us)
Async XLA Ops:
  4.4 21.9 %copy-start.5 = (bf16[256,1024]{1,0:T(8,128)(2,1)S(1)}, bf16[256,1024]{1,0:T(8,128)(2,1)}, u32[]{:S(2)}) copy-start(bf16[256,1024]{1,0:T(8,128)(2,1)} %cot_ref.1) | copy-start | bytes 1572868
  4.4 21.9 %copy-start.6 = (f32[256,16]{1,0:T(8,128)S(1)}, f32[256,16]{1,0:T(8,128)}, u32[]{:S(2)}) copy-start(f32[256,16]{1,0:T(8,128)} %get-tuple-element.51.summed_ref) | copy-start | bytes 49156
  4.4 21.9 %copy-start.7 = (f32[256,16]{1,0:T(8,128)S(1)}, f32[256,16]{1,0:T(8,128)}, u32[]{:S(2)}) copy-start(f32[256,16]{1,0:T(8,128)} %get-tuple-element.52.deltas_ref) | copy-start | bytes 49156
  20.9 5.4 %copy-start = (bf16[256,1024]{1,0:T(8,128)(2,1)S(1)}, bf16[256,1024]{1,0:T(8,128)(2,1)}, u32[]{:S(2)}) copy-start(bf16[256,1024]{1,0:T(8,128)(2,1)} %x_ref.5) | copy-start | bytes 1572868
  20.9 5.4 %copy-start.2 = (bf16[256,128]{1,0:T(8,128)(2,1)S(1)}, bf16[256,128]{1,0:T(8,128)(2,1)}, u32[]{:S(2)}) copy-start(bf16[256,128]{1,0:T(8,128)(2,1)} %c_ref.7) | copy-start | bytes 196612
  20.9 5.5 %copy-start.3 = (bf16[256,128]{1,0:T(8,128)(2,1)S(1)}, bf16[256,128]{1,0:T(8,128)(2,1)}, u32[]{:S(2)}) copy-start(bf16[256,128]{1,0:T(8,128)(2,1)} %b_ref.5) | copy-start | bytes 196612
  20.9 5.5 %copy-start.4 = (bf16[256,1024]{1,0:T(8,128)(2,1)S(1)}, bf16[256,1024]{1,0:T(8,128)(2,1)}, u32[]{:S(2)}) copy-start(bf16[256,1024]{1,0:T(8,128)(2,1)} %z_ref.1) | copy-start | bytes 1572868
  21.0 8.9 %collective-permute-start = (f32[136,128]{1,0:T(8,128)S(1)}, f32[136,128]{1,0:T(8,128)S(1)}, u32[]{:S(2)}, u32[]{:S(2)}) collective-permute-start(f32[136,128]{1,0:T(8,128)S(1)} %shard_map.147.own_ref), channel_id=1, source_target_pairs={{0,64},{64,128},{128,192},{192,256},{256,320},{320,384},{384,448},... | collective-permute-start | bytes 208904 | tf_op jit(solution)/shard_map/ppermute | solution.py:485
  26.3 0.7 copy-start.10
  26.3 0.7 copy-start.11
  29.9 18.7 %collective-permute-start.1 = (f32[136,128]{1,0:T(8,128)S(1)}, f32[136,128]{1,0:T(8,128)S(1)}, u32[]{:S(2)}, u32[]{:S(2)}) collective-permute-start(f32[136,128]{1,0:T(8,128)S(1)} %get-tuple-element.62), channel_id=1, source_target_pairs={{0,64},{64,128},{128,192},{192,256},{256,320},{320,384},{384,448},... | collective-permute-start | bytes 208904 | tf_op jit(solution)/shard_map/ppermute | solution.py:485
  36.3 12.3 %collective-permute-start.2 = (f32[128,128]{1,0:T(8,128)S(1)}, f32[128,128]{1,0:T(8,128)S(1)}, u32[]{:S(2)}, u32[]{:S(2)}) collective-permute-start(f32[128,128]{1,0:T(8,128)S(1)} %get-tuple-element.63), channel_id=1, source_target_pairs={{0,192},{64,256},{128,320},{192,384},{256,448},{1,193},{65,257},{1... | collective-permute-start | bytes 196616 | tf_op jit(solution)/shard_map/ppermute | solution.py:485
  48.7 11.1 %copy-start.9 = (f32[1024]{0:T(1024)S(1)}, f32[1024]{0:T(1024)}, u32[]{:S(2)}) copy-start(f32[1024]{0:T(1024)} %param.19) | copy-start | bytes 12292
  83.4 1.5 %copy-start.1 = (f32[8,136,128]{2,1,0:T(8,128)S(1)}, f32[8,136,128]{2,1,0:T(8,128)}, u32[]{:S(2)}) copy-start(f32[8,136,128]{2,1,0:T(8,128)} %get-tuple-element.50.own_ref) | copy-start | bytes 1671172
  83.4 8.0 %collective-permute-start.3 = (f32[136,128]{1,0:T(8,128)S(1)}, f32[136,128]{1,0:T(8,128)S(1)}, u32[]{:S(2)}, u32[]{:S(2)}) collective-permute-start(f32[136,128]{1,0:T(8,128)S(1)} %get-tuple-element.68.own_ref), channel_id=1, source_target_pairs={{64,0},{128,64},{192,128},{256,192},{320,256},{384,320},{448,384},... | collective-permute-start | bytes 208904 | tf_op jit(solution)/shard_map/ppermute | solution.py:485
  91.4 31.3 %collective-permute-start.4 = (f32[136,128]{1,0:T(8,128)S(1)}, f32[136,128]{1,0:T(8,128)S(1)}, u32[]{:S(2)}, u32[]{:S(2)}) collective-permute-start(f32[136,128]{1,0:T(8,128)S(1)} %get-tuple-element.84), channel_id=1, source_target_pairs={{64,0},{128,64},{192,128},{256,192},{320,256},{384,320},{448,384},... | collective-permute-start | bytes 208904 | tf_op jit(solution)/shard_map/ppermute | solution.py:485
  92.7 30.0 %collective-permute-start.5 = (f32[128,128]{1,0:T(8,128)S(1)}, f32[128,128]{1,0:T(8,128)S(1)}, u32[]{:S(2)}, u32[]{:S(2)}) collective-permute-start(f32[128,128]{1,0:T(8,128)S(1)} %get-tuple-element.85), channel_id=1, source_target_pairs={{192,0},{256,64},{320,128},{384,192},{448,256},{193,1},{257,65},{3... | collective-permute-start | bytes 196616 | tf_op jit(solution)/shard_map/ppermute | solution.py:485
  122.8 11.2 %copy-start.8 = (f32[256,16]{0,1:T(8,128)S(1)}, f32[256,16]{0,1:T(8,128)}, u32[]{:S(2)}) copy-start(f32[256,16]{0,1:T(8,128)} %param.15) | copy-start | bytes 49156
  122.8 11.2 %copy-start.12 = (f32[16]{0:T(128)S(1)}, f32[16]{0:T(128)}, u32[]{:S(2)}) copy-start(f32[16]{0:T(128)} %param.16) | copy-start | bytes 196
  122.8 11.2 %copy-start.13 = (f32[16]{0:T(128)S(1)}, f32[16]{0:T(128)}, u32[]{:S(2)}) copy-start(f32[16]{0:T(128)} %param.17) | copy-start | bytes 196

commit v5 on v4

--- a/solution.py
+++ b/solution.py
@@ -15,7 +15,6 @@
 WIDE = 2 * LANES
 GROUP = 8
 EPSILON = 1e-05
-ROOM = 62
 F32 = jnp.float32
 BF16 = jnp.bfloat16
 NN = (((1,), (0,)), ((), ()))
@@ -116,7 +115,7 @@
 
 
 def states_kernel(
-    lengths_ref,
+    lengths_hbm,
     x_hbm,
     b_hbm,
     dt_hbm,
@@ -125,6 +124,7 @@
     out_ref,
     summed_ref,
     deltas_ref,
+    lengths_ref,
     x_ref,
     b_ref,
     dt_ref,
@@ -132,33 +132,31 @@
     bias_ref,
     sems,
 ):
-    sources = (alog_hbm, bias_hbm, dt_hbm, b_hbm, x_hbm)
-    targets = (alog_ref, bias_ref, dt_ref, b_ref, x_ref)
+    rows = x_ref.shape[0]
+    pairs = x_ref.shape[1] // WIDE
+    moves = [(alog_hbm, alog_ref), (bias_hbm, bias_ref), (dt_hbm, dt_ref)]
+    moves += [(lengths_hbm, lengths_ref), (b_hbm, b_ref), (x_hbm, x_ref)]
     copies = [
         pltpu.make_async_copy(source, target, sems.at[one])
-        for one, (source, target) in enumerate(zip(sources, targets))
+        for one, (source, target) in enumerate(moves)
     ]
     for copy in copies:
         copy.start()
-    rows = x_ref.shape[0]
-    pairs = x_ref.shape[1] // WIDE
-    _, resets = place_marks(lengths_ref, rows, 0)
     at, of = ordered(rows)
     before = jnp.where(at <= of, 1.0, 0.0).astype(BF16)
     for copy in copies[:3]:
         copy.wait()
-    deltas_row = softplus(dt_ref[...] + column(bias_ref[...]))
-    summed = mul_3x(-jnp.exp(column(alog_ref[...])) * deltas_row, before).T
-    deltas = deltas_row.T
-    summed_ref[...] = summed
-    deltas_ref[...] = deltas
-    ending = summed[rows - 1 : rows, :]
-    last = resets[rows - 1 : rows, :]
-    weights = jnp.where(resets == last, jnp.exp(ending - summed), 0.0) * deltas
-    through = jnp.broadcast_to(jnp.where(last == 0, jnp.exp(ending), 0.0), (8, deltas.shape[1]))
+    deltas = softplus(dt_ref[...] + column(bias_ref[...]))
+    summed = mul_3x(-jnp.exp(column(alog_ref[...])) * deltas, before)
+    ending = summed[:, rows - 1 : rows]
     copies[3].wait()
+    _, resets = place_marks(lengths_ref, rows, 1)
+    last = resets[:, rows - 1 : rows]
+    weights = (jnp.where(resets == last, jnp.exp(ending - summed), 0.0) * deltas).T
+    through = jnp.broadcast_to(jnp.where(last == 0, jnp.exp(ending), 0.0), (deltas.shape[0], 8)).T
+    copies[4].wait()
     b_turned = b_ref[...].astype(F32).T.astype(BF16)
-    copies[4].wait()
+    copies[5].wait()
     for pair in range(pairs):
         weighted = x_ref[:, cols(pair)].astype(F32) * spread(weights, pair)
         state = mul_xs(b_turned, split(weighted))
@@ -167,6 +165,8 @@
             lanes = slice(half * LANES, (half + 1) * LANES)
             out_ref[2 * pair + half, 0:STATE, :] = state[:, lanes]
             out_ref[2 * pair + half, STATE : STATE + 8, :] = marks[:, lanes]
+    summed_ref[...] = summed.T
+    deltas_ref[...] = deltas.T
 
 
 def within_kernel(
@@ -299,6 +299,8 @@
     own_ref,
     base_ref,
     weights_ref,
+    high_ref,
+    low_ref,
     leaving_ref,
     b_out_ref,
     c_out_ref,
@@ -334,7 +336,9 @@
         direct = mul_ss(turned, raised) * lowered
         skipped = spread(skip, pair)
         base_ref[:, cols(pair)] = direct + skipped * pulled
-        weights_ref[:, cols(pair)] = spread(weights, pair)
+        spread_weights = spread(weights, pair)
+        weights_ref[:, cols(pair)] = spread_weights
+        high_ref[:, cols(pair)], low_ref[:, cols(pair)] = split(x * spread_weights)
         paired += mul_ss(raised, split(x * lowered), NT)
         entering = two_tiles(entering_ref, pair, slice(None))
         c_sum += mul_ss(split(pulled * fresh_ref[:, cols(pair)]), split(entering), NT)
@@ -359,6 +363,8 @@
     bias_ref,
     base_ref,
     weights_ref,
+    high_ref,
+    low_ref,
     leaving_ref,
     b_in_ref,
     along_ref,
@@ -393,7 +399,8 @@
         gained = mul(b_twice, jnp.concatenate(later, axis=0)) * weights
         x_out_ref[:, cols(pair)] = (base_ref[:, cols(pair)] + gained).astype(BF16)
         x = x_ref[:, cols(pair)].astype(F32)
-        b_sum += mul_ss(split(x * weights), later, NT)
+        both = mul(high_ref[:, cols(pair)], jnp.concatenate(later, axis=0), NT)
+        b_sum += both[:, :STATE] + (both[:, STATE:] + mul(low_ref[:, cols(pair)], later[0], NT))
         marks = head_marks(heads, pair)
         back += mul_xs(marks, split(x * gained), NT)
         end = jnp.sum(later_full * leaving_ref[:, cols(pair)], axis=0, keepdims=True)
@@ -452,11 +459,13 @@
     hand_members(holding, reverse, got_ref, marks_ref, out_ref)
 
 
-def call(kernel, outs, *operands, smem=False, hbm=False, scratch=(), room=16):
+def call(kernel, outs, *operands, smem=False, hbm=False, scratch=()):
     space = pltpu.HBM if hbm else pltpu.VMEM
     in_specs = [jax.tree.map(lambda _: pl.BlockSpec(memory_space=space), one) for one in operands]
     if smem:
         in_specs[0] = pl.BlockSpec(memory_space=pltpu.SMEM)
+    if hbm:
+        operands = [pltpu.with_memory_space_constraint(one, pltpu.HBM) for one in operands]
     many = isinstance(outs, (list, tuple))
     spec = pl.BlockSpec(memory_space=pltpu.VMEM)
     return pl.pallas_call(
@@ -465,7 +474,7 @@
         in_specs=in_specs,
         out_specs=[spec] * len(outs) if many else spec,
         scratch_shapes=scratch,
-        compiler_params=pltpu.CompilerParams(vmem_limit_bytes=room * 1024 * 1024),
+        compiler_params=pltpu.CompilerParams(vmem_limit_bytes=16 * 1024 * 1024),
     )(*operands)
 
 
@@ -556,16 +565,15 @@
         steps,
         a_log,
         dt_bias,
-        smem=True,
         hbm=True,
-        room=ROOM,
         scratch=[
+            pltpu.SMEM(lengths.shape, jnp.int32),
             pltpu.VMEM(inputs_x.shape, BF16),
             pltpu.VMEM(input_b.shape, BF16),
             pltpu.VMEM(steps.shape, F32),
             pltpu.VMEM(a_log.shape, F32),
             pltpu.VMEM(dt_bias.shape, F32),
-            pltpu.SemaphoreType.DMA((5,)),
+            pltpu.SemaphoreType.DMA((6,)),
         ],
     )
 
@@ -616,6 +624,8 @@
             [
                 wide,
                 wide,
+                like((rows, width), BF16),
+                like((rows, width), BF16),
                 like((STATE, width)),
                 like((rows, STATE)),
                 like((rows, STATE), BF16),
@@ -638,7 +648,7 @@
         )
 
     later, gains, beside = carry_back(own_back, marks, after)
-    base, weights, leaving, b_part, grad_c, along, back = beside
+    base, weights, high, low, leaving, b_part, grad_c, along, back = beside
     share = width // (GROUP * lax.axis_size("zh"))
     grad_x, grad_b, grad_dt, grad_gain = call(
         final_kernel,
@@ -650,6 +660,8 @@
         dt_bias,
         base,
         weights,
+        high,
+        low,
         leaving,
         b_part,
         along,

time: 137 us -> 135 us (0.985)
  Pallas kernels: 15.1 us -> 13.5 us
    pallas_call x12, Pallas kernels: 15.1 us -> 13.5 us  [call(): pl.pallas_call(kernel, out_shape=outs, in_specs=in_specs, out_specs=[spec...]
where the time goes in v5:
time: 135 us; the launch traced here: 134 us
  blocking collectives  89.1 us (66%)
  starting transfers between devices  26 us (19%)
  Pallas kernels  13.5 us (10%)
  waiting for transfers between devices  3.99 us (3%)
    all_to_all x6, blocking collectives, exchange(): return lax.all_to_all(value, axes, 0, 0, tiled=True)  89.1 us
    ppermute x6, starting transfers between devices, moved(): lax.ppermute(value, 'zh', [(i, j) for i, j in pairs if 0 <= j < count])  26 us
    pallas_call x12, Pallas kernels, call(): pl.pallas_call(kernel, out_shape=outs, in_specs=in_specs, out_specs=[spec...  13.5 us
    ppermute x6, waiting for transfers between devices, moved(): lax.ppermute(value, 'zh', [(i, j) for i, j in pairs if 0 <= j < count])  3.99 us
  transfers between devices with their start and end apart: 6, of which 2 were waited for; matrix products, arithmetic and copies ran while one was open for 0% of the time, Pallas kernels for 5%

profile of v5, /device:TPU:8, one launch (start us, length us, event | category | flops | bytes accessed | tf_op | source)
XLA Modules:
  0.0 134.1 jit_solution(14320014600081669859)
XLA Ops:
  0.6 2.4 %shard_map.146 = (f32[8,136,128]{2,1,0:T(8,128)S(1)}, f32[256,16]{1,0:T(8,128)S(1)}, f32[256,16]{1,0:T(8,128)S(1)}) custom-call(s32[16]{0:T(128)} %lengths_ref.3, bf16[256,1024]{1,0:T(8,128)(2,1)} %x_ref.5, bf16[256,128]{1,0:T(8,128)(2,1)} %b_ref.5, f32[16,256]{1,0:T(8,128)} %bitcast.8, f32[1,16]{1,0:T(1,128)} %bitcast.15, f32[1,16]{1,0:T(1,128)} %bitcast.17), custom_call_target="tpu_custom_call" | custom-call | tf_op jit(solution)/shard_map/pallas_call | solution.py:471
  3.0 0.0 copy-start.4
  3.0 16.3 %all_to_all.30.got_ref.marks_ref = f32[8,136,128]{2,1,0:T(8,128)S(1)} all-to-all(f32[8,136,128]{2,1,0:T(8,128)S(1)} %get-tuple-element.54.own_ref), channel_id=1, replica_groups=mesh['zh'=8,'zl'=2,'x'=4,'tensor'=8] {'zl','x'}, dimensions={0} | all-to-all | bytes 1114112 | tf_op jit(solution)/shard_map/all_to_all | solution.py:486
  19.3 0.0 copy-start
  19.3 0.0 copy-start.1
  19.3 0.0 copy-start.2
  19.3 0.0 copy-start.3
  19.3 5.3 %collective-permute-start = (f32[136,128]{1,0:T(8,128)S(1)}, f32[136,128]{1,0:T(8,128)S(1)}, u32[]{:S(2)}, u32[]{:S(2)}) collective-permute-start(f32[136,128]{1,0:T(8,128)S(1)} %shard_map.147.own_ref), channel_id=1, source_target_pairs={{0,64},{64,128},{128,192},{192,256},{256,320},{320,384},{384,448},... | collective-permute-start | bytes 208904 | tf_op jit(solution)/shard_map/ppermute | solution.py:494
  24.7 0.0 copy-start.7
  24.7 0.0 copy-start.8
  24.7 0.0 copy-done.4
  24.7 0.0 copy-done
  24.7 0.0 copy-done.1
  24.7 0.0 copy-done.2
  24.7 0.0 copy-done.3
  24.7 0.6 copy-done.7
  25.3 0.0 copy-done.8
  25.3 2.9 %shard_map.148 = (f32[256,1024]{1,0:T(8,128)S(1)}, f32[256,1024]{1,0:T(8,128)S(1)}, f32[256,1024]{1,0:T(8,128)S(1)}, f32[256,1024]{1,0:T(8,128)S(1)}) custom-call(s32[16]{0:T(128)S(1)} %copy-done.7, bf16[256,1024]{1,0:T(8,128)(2,1)S(1)} %copy-done, bf16[256,1024]{1,0:T(8,128)(2,1)S(1)} %copy-done.3, bf16[256,1024]{1,0:T(8,128)(2,1)S(1)} %copy-done.4, ...), custom_call_target="tpu_custom_call" | custom-call | tf_op jit(solution)/shard_map/pallas_call | solution.py:471
  28.2 0.0 collective-permute-done.got_ref
  28.3 6.4 %collective-permute-start.1 = (f32[136,128]{1,0:T(8,128)S(1)}, f32[136,128]{1,0:T(8,128)S(1)}, u32[]{:S(2)}, u32[]{:S(2)}) collective-permute-start(f32[136,128]{1,0:T(8,128)S(1)} %get-tuple-element.66), channel_id=1, source_target_pairs={{0,64},{64,128},{128,192},{192,256},{256,320},{320,384},{384,448},... | collective-permute-start | bytes 208904 | tf_op jit(solution)/shard_map/ppermute | solution.py:494
  34.7 10.4 %collective-permute-start.2 = (f32[128,128]{1,0:T(8,128)S(1)}, f32[128,128]{1,0:T(8,128)S(1)}, u32[]{:S(2)}, u32[]{:S(2)}) collective-permute-start(f32[128,128]{1,0:T(8,128)S(1)} %get-tuple-element.67), channel_id=1, source_target_pairs={{0,192},{64,256},{128,320},{192,384},{256,448},{1,193},{65,257},{1... | collective-permute-start | bytes 196616 | tf_op jit(solution)/shard_map/ppermute | solution.py:494
  45.1 1.9 %collective-permute-done.2.far_ref = f32[128,128]{1,0:T(8,128)S(1)} collective-permute-done((f32[128,128]{1,0:T(8,128)S(1)}, f32[128,128]{1,0:T(8,128)S(1)}, u32[]{:S(2)}, u32[]{:S(2)}) %collective-permute-start.2) | collective-permute-done | bytes 65568 | tf_op jit(solution)/shard_map/ppermute | solution.py:494
  47.0 0.0 collective-permute-done.1.near_ref
  47.1 0.0 copy-start.6
  47.1 11.0 %all_to_all.31.entering_ref = f32[8,128,128]{2,1,0:T(8,128)S(1)} all-to-all(f32[8,128,128]{2,1,0:T(8,128)S(1)} %shard_map.150), channel_id=1, replica_groups=mesh['zh'=8,'zl'=2,'x'=4,'tensor'=8] {'zl','x'}, dimensions={0} | all-to-all | bytes 1048576 | tf_op jit(solution)/shard_map/all_to_all | solution.py:486
  58.1 0.0 copy-done.6
  58.1 0.9 shard_map.151
  59.0 8.6 %all_to_all.32.sums_ref = f32[8,4,128]{2,1,0:T(4,128)S(1)} all-to-all(f32[8,4,128]{2,1,0:T(4,128)S(1)} %get-tuple-element.70), channel_id=1, replica_groups=mesh['zh'=8,'zl'=2,'x'=4,'tensor'=8] {'tensor'}, dimensions={0} | all-to-all | bytes 32768 | tf_op jit(solution)/shard_map/all_to_all | solution.py:486
  67.7 0.7 shard_map.152
  68.4 13.3 %all_to_all.33.got_ref = f32[8,136,128]{2,1,0:T(8,128)S(1)} all-to-all(f32[8,136,128]{2,1,0:T(8,128)S(1)} %get-tuple-element.71), channel_id=1, replica_groups=mesh['zh'=8,'zl'=2,'x'=4,'tensor'=8] {'zl','x'}, dimensions={0} | all-to-all | bytes 1114112 | tf_op jit(solution)/shard_map/all_to_all | solution.py:486
  81.8 1.3 collective-permute-start.3
  83.1 4.4 %shard_map.154 = (f32[256,1024]{1,0:T(8,128)S(1)}, f32[256,1024]{1,0:T(8,128)S(1)}, bf16[256,1024]{1,0:T(8,128)(2,1)S(1)}, bf16[256,1024]{1,0:T(8,128)(2,1)S(1)}...) custom-call(s32[16]{0:T(128)S(1)} %copy-done.7, ...), custom_call_target="tpu_custom_call" | custom-call | tf_op jit(solution)/shard_map/pallas_call | solution.py:471
  87.5 2.1 %collective-permute-done.3.got_ref = f32[136,128]{1,0:T(8,128)S(1)} collective-permute-done((f32[136,128]{1,0:T(8,128)S(1)}, f32[136,128]{1,0:T(8,128)S(1)}, u32[]{:S(2)}, u32[]{:S(2)}) %collective-permute-start.3) | collective-permute-done | bytes 69664 | tf_op jit(solution)/shard_map/ppermute | solution.py:494
  89.6 1.3 collective-permute-start.4
  90.9 1.3 collective-permute-start.5
  92.2 28.7 %all_to_all.34.gains_ref = f32[8,1,128]{2,1,0:T(1,128)S(1)} all-to-all(f32[8,1,128]{2,1,0:T(1,128)S(1)} %bitcast.12), channel_id=1, replica_groups=mesh['zh'=8,'zl'=2,'x'=4,'tensor'=8] {'zh'}, dimensions={0} | all-to-all | bytes 8192 | tf_op jit(solution)/shard_map/all_to_all | solution.py:486
  120.9 0.0 collective-permute-done.5.far_ref
  120.9 0.0 collective-permute-done.4.near_ref
  120.9 0.1 shard_map.156
  120.9 0.0 copy-start.5
  121.0 0.0 copy-start.9
  121.0 0.0 copy-start.10
  121.0 11.2 %all_to_all.35.later_ref = f32[8,128,128]{2,1,0:T(8,128)S(1)} all-to-all(f32[8,128,128]{2,1,0:T(8,128)S(1)} %shard_map.156), channel_id=1, replica_groups=mesh['zh'=8,'zl'=2,'x'=4,'tensor'=8] {'zl','x'}, dimensions={0} | all-to-all | bytes 1048576 | tf_op jit(solution)/shard_map/all_to_all | solution.py:486
  132.2 0.0 copy-done.5
  132.2 0.0 copy-done.9
  132.2 0.0 copy-done.10
  132.2 1.9 %shard_map.157 = (bf16[256,1024]{1,0:T(8,128)(2,1)}, bf16[256,128]{1,0:T(8,128)(2,1)}, f32[16,256]{1,0:T(8,128)}, f32[1,16]{1,0:T(1,128)}) custom-call(bf16[256,1024]{1,0:T(8,128)(2,1)S(1)} %copy-done, bf16[256,128]{1,0:T(8,128)(2,1)S(1)} %copy-done.2, f32[16,256]{1,0:T(8,128)S(1)} %bitcast.9, f32[1,16]{1,0:T(1,128)S(1)} %bitcast.16, f32[1,16]{1,0:T(1,128)S(1)} %bitcast.18, ...), custom_call_target="tpu_custom_call" | custom-call | tf_op jit(solution)/shard_map/pallas_call | solution.py:471
  (5 shorter events, 0.2 us)
Async XLA Ops:
  3.0 21.7 %copy-start.4 = (bf16[256,1024]{1,0:T(8,128)(2,1)S(1)}, bf16[256,1024]{1,0:T(8,128)(2,1)}, u32[]{:S(2)}) copy-start(bf16[256,1024]{1,0:T(8,128)(2,1)} %cot_ref.1) | copy-start | bytes 1572868
  19.3 5.4 %copy-start = (bf16[256,1024]{1,0:T(8,128)(2,1)S(1)}, bf16[256,1024]{1,0:T(8,128)(2,1)}, u32[]{:S(2)}) copy-start(bf16[256,1024]{1,0:T(8,128)(2,1)} %x_ref.5) | copy-start | bytes 1572868
  19.3 5.4 %copy-start.1 = (bf16[256,128]{1,0:T(8,128)(2,1)S(1)}, bf16[256,128]{1,0:T(8,128)(2,1)}, u32[]{:S(2)}) copy-start(bf16[256,128]{1,0:T(8,128)(2,1)} %c_ref.7) | copy-start | bytes 196612
  19.3 5.4 %copy-start.2 = (bf16[256,128]{1,0:T(8,128)(2,1)S(1)}, bf16[256,128]{1,0:T(8,128)(2,1)}, u32[]{:S(2)}) copy-start(bf16[256,128]{1,0:T(8,128)(2,1)} %b_ref.5) | copy-start | bytes 196612
  19.3 5.4 %copy-start.3 = (bf16[256,1024]{1,0:T(8,128)(2,1)S(1)}, bf16[256,1024]{1,0:T(8,128)(2,1)}, u32[]{:S(2)}) copy-start(bf16[256,1024]{1,0:T(8,128)(2,1)} %z_ref.1) | copy-start | bytes 1572868
  19.3 8.9 %collective-permute-start = (f32[136,128]{1,0:T(8,128)S(1)}, f32[136,128]{1,0:T(8,128)S(1)}, u32[]{:S(2)}, u32[]{:S(2)}) collective-permute-start(f32[136,128]{1,0:T(8,128)S(1)} %shard_map.147.own_ref), channel_id=1, source_target_pairs={{0,64},{64,128},{128,192},{192,256},{256,320},{320,384},{384,448},... | collective-permute-start | bytes 208904 | tf_op jit(solution)/shard_map/ppermute | solution.py:494
  24.7 0.7 copy-start.7
  24.7 0.7 copy-start.8
  28.3 18.7 %collective-permute-start.1 = (f32[136,128]{1,0:T(8,128)S(1)}, f32[136,128]{1,0:T(8,128)S(1)}, u32[]{:S(2)}, u32[]{:S(2)}) collective-permute-start(f32[136,128]{1,0:T(8,128)S(1)} %get-tuple-element.66), channel_id=1, source_target_pairs={{0,64},{64,128},{128,192},{192,256},{256,320},{320,384},{384,448},... | collective-permute-start | bytes 208904 | tf_op jit(solution)/shard_map/ppermute | solution.py:494
  34.7 12.3 %collective-permute-start.2 = (f32[128,128]{1,0:T(8,128)S(1)}, f32[128,128]{1,0:T(8,128)S(1)}, u32[]{:S(2)}, u32[]{:S(2)}) collective-permute-start(f32[128,128]{1,0:T(8,128)S(1)} %get-tuple-element.67), channel_id=1, source_target_pairs={{0,192},{64,256},{128,320},{192,384},{256,448},{1,193},{65,257},{1... | collective-permute-start | bytes 196616 | tf_op jit(solution)/shard_map/ppermute | solution.py:494
  47.1 11.1 %copy-start.6 = (f32[1024]{0:T(1024)S(1)}, f32[1024]{0:T(1024)}, u32[]{:S(2)}) copy-start(f32[1024]{0:T(1024)} %param.19) | copy-start | bytes 12292
  81.8 7.8 %collective-permute-start.3 = (f32[136,128]{1,0:T(8,128)S(1)}, f32[136,128]{1,0:T(8,128)S(1)}, u32[]{:S(2)}, u32[]{:S(2)}) collective-permute-start(f32[136,128]{1,0:T(8,128)S(1)} %get-tuple-element.72.own_ref), channel_id=1, source_target_pairs={{64,0},{128,64},{192,128},{256,192},{320,256},{384,320},{448,384},... | collective-permute-start | bytes 208904 | tf_op jit(solution)/shard_map/ppermute | solution.py:494
  89.6 31.3 %collective-permute-start.4 = (f32[136,128]{1,0:T(8,128)S(1)}, f32[136,128]{1,0:T(8,128)S(1)}, u32[]{:S(2)}, u32[]{:S(2)}) collective-permute-start(f32[136,128]{1,0:T(8,128)S(1)} %get-tuple-element.92), channel_id=1, source_target_pairs={{64,0},{128,64},{192,128},{256,192},{320,256},{384,320},{448,384},... | collective-permute-start | bytes 208904 | tf_op jit(solution)/shard_map/ppermute | solution.py:494
  90.9 30.0 %collective-permute-start.5 = (f32[128,128]{1,0:T(8,128)S(1)}, f32[128,128]{1,0:T(8,128)S(1)}, u32[]{:S(2)}, u32[]{:S(2)}) collective-permute-start(f32[128,128]{1,0:T(8,128)S(1)} %get-tuple-element.93), channel_id=1, source_target_pairs={{192,0},{256,64},{320,128},{384,192},{448,256},{193,1},{257,65},{3... | collective-permute-start | bytes 196616 | tf_op jit(solution)/shard_map/ppermute | solution.py:494
  120.9 11.2 %copy-start.5 = (f32[256,16]{0,1:T(8,128)S(1)}, f32[256,16]{0,1:T(8,128)}, u32[]{:S(2)}) copy-start(f32[256,16]{0,1:T(8,128)} %param.15) | copy-start | bytes 49156
  121.0 11.2 %copy-start.9 = (f32[16]{0:T(128)S(1)}, f32[16]{0:T(128)}, u32[]{:S(2)}) copy-start(f32[16]{0:T(128)} %param.16) | copy-start | bytes 196
  121.0 11.2 %copy-start.10 = (f32[16]{0:T(128)S(1)}, f32[16]{0:T(128)}, u32[]{:S(2)}) copy-start(f32[16]{0:T(128)} %param.17) | copy-start | bytes 196

commit v6 on v5

--- a/solution.py
+++ b/solution.py
@@ -547,7 +547,7 @@
 ):
     rows, width = inputs_x.shape
     heads = dt_raw.shape[1]
-    channels = float(width * lax.axis_size("tensor"))
+    channels = float(width * lax.axis_size(("y", "core")))
     steps = dt_raw.T
     a_log, dt_bias = a_log[None, :], dt_bias[None, :]
     skip_d, gain = skip_d[None, :], norm_gain[None, :]
@@ -596,7 +596,7 @@
     entering, marks, (within, fresh, gate, gated) = carry(own, before)
     core, bent, sums = call(
         output_kernel,
-        [wide, wide, like((lax.axis_size("tensor"), 2 * rows // LANES, LANES))],
+        [wide, wide, like((1, 2 * rows // LANES, LANES))],
         within,
         fresh,
         gate,
@@ -605,7 +605,8 @@
         gain,
         entering,
     )
-    sums = exchange(sums, "tensor")
+    sums = lax.all_gather(sums[0], "core").sum(0)
+    sums = exchange(jnp.broadcast_to(sums, (lax.axis_size("y"),) + sums.shape), "y")
     pulled, own_back = call(
         functools.partial(pull_kernel, channels),
         [wide, message],
@@ -675,15 +676,17 @@
 def solution(mesh):
     count, across = mesh.devices.shape
     split_mesh = Mesh(
-        mesh.devices.reshape(count // GROUP, 2, GROUP // 2, across), ("zh", "zl", "x", "tensor")
+        mesh.devices.reshape(count // GROUP, 2, GROUP // 2, across // 2, 2),
+        ("zh", "zl", "x", "y", "core"),
     )
     tokens = ("zh", "zl", "x")
-    both = P(tokens, "tensor")
-    alone = P("tensor")
+    heads = ("y", "core")
+    both = P(tokens, heads)
+    alone = P(heads)
     return jax.shard_map(
         per_device,
         mesh=split_mesh,
         in_specs=(both, both, both, both, both, alone, alone, alone, alone, P(), both),
-        out_specs=(both, both, both, both, P(("tensor", "zh", "zl", "x"))),
+        out_specs=(both, both, both, both, P(heads + tokens)),
         check_vma=False,
     )

time: 135 us -> 142 us (1.052)
  local copies, waits for them, and re-layouts: 0.65 us -> 6.32 us
    unnamed x22 -> x40, local copies, waits for them, and re-layouts: 0.65 us -> 6.32 us
    all_gather x0 -> x1, blocking collectives: none -> 1.77 us  [per_device(): sums = lax.all_gather(sums[0], 'core').sum(0)]
where the time goes in v6:
time: 142 us; the launch traced here: 141 us
  blocking collectives  90 us (63%)
  starting transfers between devices  26.2 us (18%)
  Pallas kernels  13.3 us (9%)
  local copies, waits for them, and re-layouts  6.32 us (4%)
  waiting for transfers between devices  4.09 us (3%)
    all_to_all x6, blocking collectives, exchange(): return lax.all_to_all(value, axes, 0, 0, tiled=True)  88.2 us
    ppermute x6, starting transfers between devices, moved(): lax.ppermute(value, 'zh', [(i, j) for i, j in pairs if 0 <= j < count])  26.2 us
    pallas_call x12, Pallas kernels, call(): pl.pallas_call(kernel, out_shape=outs, in_specs=in_specs, out_specs=[spec...  13.3 us
    unnamed x40, local copies, waits for them, and re-layouts  6.32 us
    ppermute x6, waiting for transfers between devices, moved(): lax.ppermute(value, 'zh', [(i, j) for i, j in pairs if 0 <= j < count])  4.09 us
  transfers between devices with their start and end apart: 6, of which 2 were waited for; matrix products, arithmetic and copies ran while one was open for 0% of the time, Pallas kernels for 5%

profile of v6, /device:TPU:8, one launch (start us, length us, event | category | flops | bytes accessed | tf_op | source)
XLA Modules:
  0.0 140.8 jit_solution(5621069393749091190)
XLA Ops:
  0.6 2.4 %shard_map.146 = (f32[8,136,128]{2,1,0:T(8,128)S(1)}, f32[256,16]{1,0:T(8,128)S(1)}, f32[256,16]{1,0:T(8,128)S(1)}) custom-call(s32[16]{0:T(128)} %lengths_ref.3, bf16[256,1024]{1,0:T(8,128)(2,1)} %x_ref.5, bf16[256,128]{1,0:T(8,128)(2,1)} %b_ref.5, f32[16,256]{1,0:T(8,128)} %bitcast.8, f32[1,16]{1,0:T(1,128)} %bitcast.15, f32[1,16]{1,0:T(1,128)} %bitcast.17), custom_call_target="tpu_custom_call" | custom-call | tf_op jit(solution)/shard_map/pallas_call | solution.py:471
  3.0 0.0 copy-start.12
  3.0 0.0 copy-start.11
  3.0 16.3 %all_to_all.30.got_ref.marks_ref = f32[8,136,128]{2,1,0:T(8,128)S(1)} all-to-all(f32[8,136,128]{2,1,0:T(8,128)S(1)} %get-tuple-element.54.own_ref), channel_id=1, replica_groups=mesh['zh'=8,'zl'=2,'x'=4,'y'=4,'core'=2] {'zl','x'}, dimensions={0} | all-to-all | bytes 1114112 | tf_op jit(solution)/shard_map/all_to_all | solution.py:486
  19.3 0.0 copy-start
  19.3 0.0 copy-start.6
  19.3 0.0 copy-start.7
  19.3 0.0 copy-start.10
  19.4 5.3 %collective-permute-start = (f32[136,128]{1,0:T(8,128)S(1)}, f32[136,128]{1,0:T(8,128)S(1)}, u32[]{:S(2)}, u32[]{:S(2)}) collective-permute-start(f32[136,128]{1,0:T(8,128)S(1)} %shard_map.147.own_ref), channel_id=1, source_target_pairs={{0,64},{64,128},{128,192},{192,256},{256,320},{320,384},{384,448},... | collective-permute-start | bytes 208904 | tf_op jit(solution)/shard_map/ppermute | solution.py:494
  24.7 0.0 copy-start.16
  24.7 0.0 copy-start.17
  24.7 0.0 copy-done.12
  24.7 0.0 copy-done.11
  24.7 0.0 copy-done
  24.7 0.0 copy-done.6
  24.7 0.0 copy-done.7
  24.7 0.0 copy-done.10
  24.8 0.6 copy-done.16
  25.3 0.0 copy-done.17
  25.4 2.9 %shard_map.148 = (f32[256,1024]{1,0:T(8,128)S(1)}, f32[256,1024]{1,0:T(8,128)S(1)}, f32[256,1024]{1,0:T(8,128)S(1)}, f32[256,1024]{1,0:T(8,128)S(1)}) custom-call(s32[16]{0:T(128)S(1)} %copy-done.16, bf16[256,1024]{1,0:T(8,128)(2,1)S(1)} %copy-done, bf16[256,1024]{1,0:T(8,128)(2,1)S(1)} %copy-done.10, bf16[256,1024]{1,0:T(8,128)(2,1)S(1)} %copy-done.11, ...), custom_call_target="tpu_custom_call" | custom-call | tf_op jit(solution)/shard_map/pallas_call | solution.py:471
  28.2 0.0 copy-start.1
  28.2 0.0 collective-permute-done.got_ref
  28.3 6.4 %collective-permute-start.1 = (f32[136,128]{1,0:T(8,128)S(1)}, f32[136,128]{1,0:T(8,128)S(1)}, u32[]{:S(2)}, u32[]{:S(2)}) collective-permute-start(f32[136,128]{1,0:T(8,128)S(1)} %get-tuple-element.66), channel_id=1, source_target_pairs={{0,64},{64,128},{128,192},{192,256},{256,320},{320,384},{384,448},... | collective-permute-start | bytes 208904 | tf_op jit(solution)/shard_map/ppermute | solution.py:494
  34.7 10.5 %collective-permute-start.2 = (f32[128,128]{1,0:T(8,128)S(1)}, f32[128,128]{1,0:T(8,128)S(1)}, u32[]{:S(2)}, u32[]{:S(2)}) collective-permute-start(f32[128,128]{1,0:T(8,128)S(1)} %get-tuple-element.67), channel_id=1, source_target_pairs={{0,192},{64,256},{128,320},{192,384},{256,448},{1,193},{65,257},{1... | collective-permute-start | bytes 196616 | tf_op jit(solution)/shard_map/ppermute | solution.py:494
  45.1 1.9 %collective-permute-done.2.far_ref = f32[128,128]{1,0:T(8,128)S(1)} collective-permute-done((f32[128,128]{1,0:T(8,128)S(1)}, f32[128,128]{1,0:T(8,128)S(1)}, u32[]{:S(2)}, u32[]{:S(2)}) %collective-permute-start.2) | collective-permute-done | bytes 65568 | tf_op jit(solution)/shard_map/ppermute | solution.py:494
  47.0 0.0 collective-permute-done.1.near_ref
  47.1 0.0 copy-start.15
  47.1 11.0 %all_to_all.31.entering_ref = f32[8,128,128]{2,1,0:T(8,128)S(1)} all-to-all(f32[8,128,128]{2,1,0:T(8,128)S(1)} %shard_map.150), channel_id=1, replica_groups=mesh['zh'=8,'zl'=2,'x'=4,'y'=4,'core'=2] {'zl','x'}, dimensions={0} | all-to-all | bytes 1048576 | tf_op jit(solution)/shard_map/all_to_all | solution.py:486
  58.1 0.0 copy-done.1
  58.1 0.0 copy-done.15
  58.1 0.9 shard_map.151
  59.0 0.0 copy-start.3
  59.0 1.0 copy-done.3
  60.0 0.0 copy-start.8
  60.0 1.0 copy-done.8
  61.0 1.8 %all_gather.3 = f32[2,4,128]{2,1,0:T(4,128)S(1)} all-gather(f32[1,4,128]{2,1,0:T(4,128)S(1)} %get-tuple-element.70), channel_id=1, replica_groups=mesh['zh'=8,'zl'=2,'x'=4,'y'=4,'core'=2] {'core'}, dimensions={0}, use_global_device_ids=true | all-gather | bytes 6144 | tf_op jit(solution)/shard_map/all_gather | solution.py:608
  62.8 8.6 %all_to_all.32.sums_ref = f32[4,4,128]{2,1,0:T(4,128)S(1)} all-to-all(f32[4,4,128]{2,1,0:T(4,128)S(1)} %broadcast_in_dim.22), channel_id=1, replica_groups=mesh['zh'=8,'zl'=2,'x'=4,'y'=4,'core'=2] {'y'}, dimensions={0} | all-to-all | bytes 16384 | tf_op jit(solution)/shard_map/all_to_all | solution.py:486
  71.4 0.0 copy-start.2
  71.4 1.2 copy-done.2
  72.6 0.0 copy-start.4
  72.6 1.2 copy-done.4
  73.8 1.2 copy-done.9
  75.0 0.7 shard_map.152
  75.8 0.0 copy-start.5
  75.8 12.4 %all_to_all.33.got_ref = f32[8,136,128]{2,1,0:T(8,128)S(1)} all-to-all(f32[8,136,128]{2,1,0:T(8,128)S(1)} %get-tuple-element.71), channel_id=1, replica_groups=mesh['zh'=8,'zl'=2,'x'=4,'y'=4,'core'=2] {'zl','x'}, dimensions={0} | all-to-all | bytes 1114112 | tf_op jit(solution)/shard_map/all_to_all | solution.py:486
  88.2 1.4 %collective-permute-start.3 = (f32[136,128]{1,0:T(8,128)S(1)}, f32[136,128]{1,0:T(8,128)S(1)}, u32[]{:S(2)}, u32[]{:S(2)}) collective-permute-start(f32[136,128]{1,0:T(8,128)S(1)} %get-tuple-element.72.own_ref), channel_id=1, source_target_pairs={{64,0},{128,64},{192,128},{256,192},{320,256},{384,320},{448,384},... | collective-permute-start | bytes 208904 | tf_op jit(solution)/shard_map/ppermute | solution.py:494
  89.6 0.0 copy-done.5
  89.6 0.0 copy-done.13
  89.6 4.3 %shard_map.154 = (f32[256,1024]{1,0:T(8,128)S(1)}, f32[256,1024]{1,0:T(8,128)S(1)}, bf16[256,1024]{1,0:T(8,128)(2,1)S(1)}, bf16[256,1024]{1,0:T(8,128)(2,1)S(1)}...) custom-call(s32[16]{0:T(128)S(1)} %copy-done.16, ...), custom_call_target="tpu_custom_call" | custom-call | tf_op jit(solution)/shard_map/pallas_call | solution.py:471
  94.0 2.2 %collective-permute-done.3.got_ref = f32[136,128]{1,0:T(8,128)S(1)} collective-permute-done((f32[136,128]{1,0:T(8,128)S(1)}, f32[136,128]{1,0:T(8,128)S(1)}, u32[]{:S(2)}, u32[]{:S(2)}) %collective-permute-start.3) | collective-permute-done | bytes 69664 | tf_op jit(solution)/shard_map/ppermute | solution.py:494
  96.2 1.3 collective-permute-start.4
  97.5 1.3 collective-permute-start.5
  98.8 28.8 %all_to_all.34.gains_ref = f32[8,1,128]{2,1,0:T(1,128)S(1)} all-to-all(f32[8,1,128]{2,1,0:T(1,128)S(1)} %bitcast.12), channel_id=1, replica_groups=mesh['zh'=8,'zl'=2,'x'=4,'y'=4,'core'=2] {'zh'}, dimensions={0} | all-to-all | bytes 8192 | tf_op jit(solution)/shard_map/all_to_all | solution.py:486
  127.6 0.0 collective-permute-done.5.far_ref
  127.6 0.0 collective-permute-done.4.near_ref
  127.6 0.1 shard_map.156
  127.7 0.0 copy-start.14
  127.7 0.0 copy-start.18
  127.7 0.0 copy-start.19
  127.7 11.2 %all_to_all.35.later_ref = f32[8,128,128]{2,1,0:T(8,128)S(1)} all-to-all(f32[8,128,128]{2,1,0:T(8,128)S(1)} %shard_map.156), channel_id=1, replica_groups=mesh['zh'=8,'zl'=2,'x'=4,'y'=4,'core'=2] {'zl','x'}, dimensions={0} | all-to-all | bytes 1048576 | tf_op jit(solution)/shard_map/all_to_all | solution.py:486
  138.9 0.0 copy-done.14
  138.9 0.0 copy-done.18
  138.9 0.0 copy-done.19
  138.9 1.9 %shard_map.157 = (bf16[256,1024]{1,0:T(8,128)(2,1)}, bf16[256,128]{1,0:T(8,128)(2,1)}, f32[16,256]{1,0:T(8,128)}, f32[1,16]{1,0:T(1,128)}) custom-call(bf16[256,1024]{1,0:T(8,128)(2,1)S(1)} %copy-done, bf16[256,128]{1,0:T(8,128)(2,1)S(1)} %copy-done.7, f32[16,256]{1,0:T(8,128)S(1)} %bitcast.9, f32[1,16]{1,0:T(1,128)S(1)} %bitcast.16, f32[1,16]{1,0:T(1,128)S(1)} %bitcast.18, ...), custom_call_target="tpu_custom_call" | custom-call | tf_op jit(solution)/shard_map/pallas_call | solution.py:471
  (9 shorter events, 0.2 us)
Async XLA Ops:
  3.0 21.7 %copy-start.12 = (f32[256,16]{1,0:T(8,128)}, f32[256,16]{1,0:T(8,128)S(1)}, u32[]{:S(2)}) copy-start(f32[256,16]{1,0:T(8,128)S(1)} %get-tuple-element.56.deltas_ref) | copy-start | bytes 49156
  3.0 21.7 %copy-start.11 = (bf16[256,1024]{1,0:T(8,128)(2,1)S(1)}, bf16[256,1024]{1,0:T(8,128)(2,1)}, u32[]{:S(2)}) copy-start(bf16[256,1024]{1,0:T(8,128)(2,1)} %cot_ref.1) | copy-start | bytes 1572868
  19.3 5.4 %copy-start = (bf16[256,1024]{1,0:T(8,128)(2,1)S(1)}, bf16[256,1024]{1,0:T(8,128)(2,1)}, u32[]{:S(2)}) copy-start(bf16[256,1024]{1,0:T(8,128)(2,1)} %x_ref.5) | copy-start | bytes 1572868
  19.3 5.4 %copy-start.6 = (bf16[256,128]{1,0:T(8,128)(2,1)S(1)}, bf16[256,128]{1,0:T(8,128)(2,1)}, u32[]{:S(2)}) copy-start(bf16[256,128]{1,0:T(8,128)(2,1)} %c_ref.7) | copy-start | bytes 196612
  19.3 5.4 %copy-start.7 = (bf16[256,128]{1,0:T(8,128)(2,1)S(1)}, bf16[256,128]{1,0:T(8,128)(2,1)}, u32[]{:S(2)}) copy-start(bf16[256,128]{1,0:T(8,128)(2,1)} %b_ref.5) | copy-start | bytes 196612
  19.3 5.4 %copy-start.10 = (bf16[256,1024]{1,0:T(8,128)(2,1)S(1)}, bf16[256,1024]{1,0:T(8,128)(2,1)}, u32[]{:S(2)}) copy-start(bf16[256,1024]{1,0:T(8,128)(2,1)} %z_ref.1) | copy-start | bytes 1572868
  19.4 8.9 %collective-permute-start = (f32[136,128]{1,0:T(8,128)S(1)}, f32[136,128]{1,0:T(8,128)S(1)}, u32[]{:S(2)}, u32[]{:S(2)}) collective-permute-start(f32[136,128]{1,0:T(8,128)S(1)} %shard_map.147.own_ref), channel_id=1, source_target_pairs={{0,64},{64,128},{128,192},{192,256},{256,320},{320,384},{384,448},... | collective-permute-start | bytes 208904 | tf_op jit(solution)/shard_map/ppermute | solution.py:494
  24.7 0.7 copy-start.16
  24.7 0.7 copy-start.17
  28.2 29.9 %copy-start.1 = (f32[256,1024]{1,0:T(8,128)}, f32[256,1024]{1,0:T(8,128)S(1)}, u32[]{:S(2)}) copy-start(f32[256,1024]{1,0:T(8,128)S(1)} %get-tuple-element.64.gated_ref) | copy-start | bytes 3145732
  28.3 18.8 %collective-permute-start.1 = (f32[136,128]{1,0:T(8,128)S(1)}, f32[136,128]{1,0:T(8,128)S(1)}, u32[]{:S(2)}, u32[]{:S(2)}) collective-permute-start(f32[136,128]{1,0:T(8,128)S(1)} %get-tuple-element.66), channel_id=1, source_target_pairs={{0,64},{64,128},{128,192},{192,256},{256,320},{320,384},{384,448},... | collective-permute-start | bytes 208904 | tf_op jit(solution)/shard_map/ppermute | solution.py:494
  34.7 12.4 %collective-permute-start.2 = (f32[128,128]{1,0:T(8,128)S(1)}, f32[128,128]{1,0:T(8,128)S(1)}, u32[]{:S(2)}, u32[]{:S(2)}) collective-permute-start(f32[128,128]{1,0:T(8,128)S(1)} %get-tuple-element.67), channel_id=1, source_target_pairs={{0,192},{64,256},{128,320},{192,384},{256,448},{1,193},{65,257},{1... | collective-permute-start | bytes 196616 | tf_op jit(solution)/shard_map/ppermute | solution.py:494
  47.1 11.1 %copy-start.15 = (f32[1024]{0:T(1024)S(1)}, f32[1024]{0:T(1024)}, u32[]{:S(2)}) copy-start(f32[1024]{0:T(1024)} %param.19) | copy-start | bytes 12292
  59.0 1.0 copy-start.3
  60.0 1.0 copy-start.8
  71.4 1.2 copy-start.2
  72.6 1.2 copy-start.4
  73.8 1.2 copy-start.9
  75.8 13.9 %copy-start.5 = (f32[256,1024]{1,0:T(8,128)S(1)}, f32[256,1024]{1,0:T(8,128)}, u32[]{:S(2)}) copy-start(f32[256,1024]{1,0:T(8,128)} %copy-done.3) | copy-start | bytes 3145732
  88.1 1.5 %copy-start.13 = (f32[256,16]{1,0:T(8,128)S(1)}, f32[256,16]{1,0:T(8,128)}, u32[]{:S(2)}) copy-start(f32[256,16]{1,0:T(8,128)} %copy-done.12) | copy-start | bytes 49156
  88.2 8.0 %collective-permute-start.3 = (f32[136,128]{1,0:T(8,128)S(1)}, f32[136,128]{1,0:T(8,128)S(1)}, u32[]{:S(2)}, u32[]{:S(2)}) collective-permute-start(f32[136,128]{1,0:T(8,128)S(1)} %get-tuple-element.72.own_ref), channel_id=1, source_target_pairs={{64,0},{128,64},{192,128},{256,192},{320,256},{384,320},{448,384},... | collective-permute-start | bytes 208904 | tf_op jit(solution)/shard_map/ppermute | solution.py:494
  96.2 31.4 %collective-permute-start.4 = (f32[136,128]{1,0:T(8,128)S(1)}, f32[136,128]{1,0:T(8,128)S(1)}, u32[]{:S(2)}, u32[]{:S(2)}) collective-permute-start(f32[136,128]{1,0:T(8,128)S(1)} %get-tuple-element.92), channel_id=1, source_target_pairs={{64,0},{128,64},{192,128},{256,192},{320,256},{384,320},{448,384},... | collective-permute-start | bytes 208904 | tf_op jit(solution)/shard_map/ppermute | solution.py:494
  97.5 30.1 %collective-permute-start.5 = (f32[128,128]{1,0:T(8,128)S(1)}, f32[128,128]{1,0:T(8,128)S(1)}, u32[]{:S(2)}, u32[]{:S(2)}) collective-permute-start(f32[128,128]{1,0:T(8,128)S(1)} %get-tuple-element.93), channel_id=1, source_target_pairs={{192,0},{256,64},{320,128},{384,192},{448,256},{193,1},{257,65},{3... | collective-permute-start | bytes 196616 | tf_op jit(solution)/shard_map/ppermute | solution.py:494
  127.7 11.2 %copy-start.14 = (f32[256,16]{0,1:T(8,128)S(1)}, f32[256,16]{0,1:T(8,128)}, u32[]{:S(2)}) copy-start(f32[256,16]{0,1:T(8,128)} %param.15) | copy-start | bytes 49156
  127.7 11.2 %copy-start.18 = (f32[16]{0:T(128)S(1)}, f32[16]{0:T(128)}, u32[]{:S(2)}) copy-start(f32[16]{0:T(128)} %param.16) | copy-start | bytes 196
  127.7 11.2 %copy-start.19 = (f32[16]{0:T(128)S(1)}, f32[16]{0:T(128)}, u32[]{:S(2)}) copy-start(f32[16]{0:T(128)} %param.17) | copy-start | bytes 196
